TPU v7x, 256 devices: a whole 4x4x8 slice. The times are simulated.
256 devices in a mesh: ctx: 64 (over y, z, x_lo), head: 4 (over x_hi, core).
Axes of the slice: x: 4 (x_hi: 2, x_lo: 2; x = x_hi * 2 + x_lo), y: 4, z: 8, core: 2. Of those that a mesh axis runs over, the one named last changes fastest.
Arguments:
- queries: bfloat16 [32, 8192, 128], P('head', 'ctx'), as said below
- keys: bfloat16 [4, 8192, 128], P('head', 'ctx'), as said below
- values: bfloat16 [4, 8192, 128], P('head', 'ctx'), may hold values from -6 to 6
- evict_logits: float32 [4, 8192], P('head', 'ctx'), may hold values from -12 to 12
- block_order: int32 [64, 2], replicated, may hold values from 0 to 127, as said below
- grad_y: bfloat16 [8192, 5120], P(('ctx', 'head')), may hold values from -24 to 24
- w_out: bfloat16 [4096, 5120], P('head'), may hold values from -0.09375 to 0.09375
Outputs:
- query_grad: bfloat16 [32, 8192, 128], P('head', 'ctx')
- key_grad: float32 [4, 8192, 128], P('head', 'ctx')
- value_grad: float32 [4, 8192, 128], P('head', 'ctx')
- logit_grad: float32 [4, 8192], P('head', 'ctx')
Inputs may be any that keep to these rules, and one draw needn't show every extreme that they name: `block_order`: row s holds the two position blocks of ctx shard s: a block c below 64 in column 0 and the block 127 - c in column 1; every block appears once. `queries`: real values of order one or more. `keys`: real values of order one or more.
All inputs are finite; a program needn't handle non-finite values.
Results may differ from a plain program's by a relative error of at most 0.04.
Values may be sent and summed in bfloat16 or wider, within the bound.
No kernel may reach another device: no remote copies, remote signals or barrier semaphores. Data moves between devices by JAX's collectives and lax.ppermute only.
A program may use at most 64 MiB of HBM per device.

v0:
```python
import math

import jax
import jax.numpy as jnp
from jax import lax
from jax.sharding import PartitionSpec as P

WINDOW = 256


lowest = -1e30


def per_device(queries, keys, values, evict_logits, block_order, grad_y, w_out):
    local_heads, shard_len, head_dim = queries.shape
    half_len = shard_len // 2
    query_rows = local_heads * half_len
    scaling = 1.0 / math.sqrt(head_dim)
    my_shard = lax.axis_index("ctx")
    shard_count = lax.axis_size("ctx")
    cotangent = jnp.einsum(
        "td,fd->tf",
        lax.all_gather(grad_y, "head", axis=0, tiled=True),
        w_out,
        preferred_element_type=jnp.float32,
    )
    cotangent = cotangent.astype(jnp.bfloat16).reshape(2, half_len, local_heads, head_dim)
    cotangent = cotangent.transpose(0, 2, 1, 3).reshape(2, query_rows, head_dim)
    query_mat = queries.reshape(local_heads, 2, half_len, head_dim).transpose(1, 0, 2, 3)
    query_mat = query_mat.reshape(2, query_rows, head_dim)
    offsets = jnp.arange(query_rows, dtype=jnp.int32) % half_len
    query_pos = block_order[my_shard][:, None] * half_len + offsets[None, :]

    def score_tile(key_rows, logit_rows, key_pos, query_block):
        scores = (
            jnp.einsum(
                "kd,qd->kq", key_rows, query_mat[query_block], preferred_element_type=jnp.float32
            )
            * scaling
        )
        distance = query_pos[query_block][None, :] - key_pos[:, None]
        delayed = distance >= WINDOW
        scores = scores - jnp.where(delayed, jax.nn.softplus(logit_rows)[:, None], 0.0)
        return (scores, distance >= 0, delayed)

    def split_keys(portion, first_row, count, first_owner):
        width = count * shard_len
        key_part = lax.dynamic_slice_in_dim(portion[0][0], first_row, width, 0).reshape(
            count, 2, half_len, head_dim
        )
        value_part = lax.dynamic_slice_in_dim(portion[1][0], first_row, width, 0).reshape(
            count, 2, half_len, head_dim
        )
        logit_part = lax.dynamic_slice_in_dim(portion[2][0], first_row, width, 0).reshape(
            count, 2, half_len
        )
        owners = first_owner + jnp.arange(count, dtype=jnp.int32)
        owner_blocks = block_order[owners]
        key_pos = (
            owner_blocks[:, :, None] * half_len
            + jnp.arange(half_len, dtype=jnp.int32)[None, None, :]
        )
        halves = []
        for half_index in range(2):
            halves.append(
                (
                    key_part[:, half_index].reshape(count * half_len, head_dim),
                    value_part[:, half_index].reshape(count * half_len, head_dim),
                    logit_part[:, half_index].reshape(count * half_len),
                    key_pos[:, half_index].reshape(count * half_len),
                )
            )
        return halves

    def sweep(step_fn, running, portion, row_start):
        owned = portion[0].shape[1] // shard_len
        first_owner = row_start // shard_len

        def turn(turn_index, inner):
            return step_fn(inner, portion, turn_index * 4 * shard_len, 4, turn_index * 4)

        running = lax.fori_loop(0, owned // 4, turn, running)
        return running

    pairing = ((0, (0, 1)), (1, (1,)))

    def stats_step(running, portion, first_row, count, first_owner):
        halves = split_keys(portion, first_row, count, first_owner)
        running = list(running)
        for half_index, query_blocks in pairing:
            key_rows, value_rows, logit_rows, key_pos = halves[half_index]
            for query_block in query_blocks:
                row_peak, row_total, weighted = running[query_block]
                scores, visible, delayed = score_tile(key_rows, logit_rows, key_pos, query_block)
                prob_grad = jnp.einsum(
                    "kd,qd->kq",
                    value_rows,
                    cotangent[query_block],
                    preferred_element_type=jnp.float32,
                )
                new_peak = jnp.maximum(
                    row_peak, jnp.max(jnp.where(visible, scores, lowest), axis=0)
                )
                factor = jnp.exp(row_peak - new_peak)
                weights = jnp.where(visible, jnp.exp(scores - new_peak[None, :]), 0.0)
                running[query_block] = (
                    new_peak,
                    row_total * factor + jnp.sum(weights, axis=0),
                    weighted * factor + jnp.sum(weights * prob_grad, axis=0),
                )
        return tuple(running)

    empty_rows = jnp.zeros((query_rows,), jnp.float32)
    peak_rows = jnp.full((query_rows,), lowest, jnp.float32)
    stats_init = ((peak_rows, empty_rows, empty_rows), (peak_rows, empty_rows, empty_rows))
    stats = sweep(
        stats_step,
        stats_init,
        (
            lax.all_gather(keys, "ctx", axis=1, tiled=True),
            lax.all_gather(values, "ctx", axis=1, tiled=True),
            lax.all_gather(evict_logits.astype(jnp.bfloat16), "ctx", axis=1, tiled=True).astype(
                jnp.float32
            ),
        ),
        jnp.int32(0),
    )
    log_norm = [stats[index_block][0] + jnp.log(stats[index_block][1]) for index_block in range(2)]
    mean_grad = [stats[index_block][2] / stats[index_block][1] for index_block in range(2)]

    def grad_terms(query_sums, portion, first_row, count, first_owner):
        query_sums = list(query_sums)
        halves = split_keys(portion, first_row, count, first_owner)
        key_parts = []
        value_parts = []
        logit_parts = []
        for half_index, query_blocks in pairing:
            key_rows, value_rows, logit_rows, key_pos = halves[half_index]
            key_sum = jnp.zeros((count * half_len, head_dim), jnp.float32)
            value_sum = jnp.zeros((count * half_len, head_dim), jnp.float32)
            logit_sum = jnp.zeros((count * half_len,), jnp.float32)
            for query_block in query_blocks:
                scores, visible, delayed = score_tile(key_rows, logit_rows, key_pos, query_block)
                probs = jnp.where(visible, jnp.exp(scores - log_norm[query_block][None, :]), 0.0)
                prob_grad = jnp.einsum(
                    "kd,qd->kq",
                    value_rows,
                    cotangent[query_block],
                    preferred_element_type=jnp.float32,
                )
                score_grad = probs * (prob_grad - mean_grad[query_block][None, :])
                grad_half = score_grad.astype(jnp.bfloat16)
                probs_half = probs.astype(jnp.bfloat16)
                query_sums[query_block] = query_sums[query_block] + jnp.einsum(
                    "kq,kd->qd", grad_half, key_rows, preferred_element_type=jnp.float32
                )
                key_sum = key_sum + jnp.einsum(
                    "kq,qd->kd",
                    grad_half,
                    query_mat[query_block],
                    preferred_element_type=jnp.float32,
                )
                value_sum = value_sum + jnp.einsum(
                    "kq,qd->kd",
                    probs_half,
                    cotangent[query_block],
                    preferred_element_type=jnp.float32,
                )
                logit_sum = logit_sum + jnp.sum(jnp.where(delayed, score_grad, 0.0), axis=1)
            key_parts.append(key_sum.reshape(count, 1, half_len, head_dim))
            value_parts.append(value_sum.reshape(count, 1, half_len, head_dim))
            logit_parts.append(logit_sum.reshape(count, 1, half_len))
        key_block = jnp.concatenate(key_parts, axis=1).reshape(count * shard_len, head_dim)
        value_block = jnp.concatenate(value_parts, axis=1).reshape(count * shard_len, head_dim)
        logit_block = jnp.concatenate(logit_parts, axis=1).reshape(count * shard_len)
        return (tuple(query_sums), key_block, value_block, logit_block)

    def grad_step(running, portion, first_row, count, first_owner):
        query_sums, key_terms, value_terms, logit_terms = running
        query_sums, key_block, value_block, logit_block = grad_terms(
            query_sums, portion, first_row, count, first_owner
        )
        target_row = first_owner * shard_len
        key_terms = lax.dynamic_update_slice_in_dim(key_terms, key_block, target_row, 0)
        value_terms = lax.dynamic_update_slice_in_dim(value_terms, value_block, target_row, 0)
        logit_terms = lax.dynamic_update_slice_in_dim(logit_terms, logit_block, target_row, 0)
        return (query_sums, key_terms, value_terms, logit_terms)

    zero_queries = jnp.zeros((query_rows, head_dim), jnp.float32)
    grad_init = (
        (zero_queries, zero_queries),
        jnp.zeros((shard_count * shard_len, head_dim), jnp.float32),
        jnp.zeros((shard_count * shard_len, head_dim), jnp.float32),
        jnp.zeros((shard_count * shard_len,), jnp.float32),
    )
    results = sweep(
        grad_step,
        grad_init,
        (
            lax.all_gather(keys, "ctx", axis=1, tiled=True),
            lax.all_gather(values, "ctx", axis=1, tiled=True),
            lax.all_gather(evict_logits.astype(jnp.bfloat16), "ctx", axis=1, tiled=True).astype(
                jnp.float32
            ),
        ),
        jnp.int32(0),
    )
    query_sums, key_terms, value_terms, logit_terms = results
    summed = (
        lax.psum_scatter(key_terms, "ctx", scatter_dimension=0, tiled=True),
        lax.psum_scatter(value_terms, "ctx", scatter_dimension=0, tiled=True),
        lax.psum_scatter(logit_terms, "ctx", scatter_dimension=0, tiled=True),
    )
    key_total, value_total, logit_total = (summed[0], summed[1], summed[2])
    query_sum = (jnp.stack(query_sums) * scaling).astype(jnp.bfloat16)
    query_grad = query_sum.reshape(2, local_heads, half_len, head_dim).transpose(1, 0, 2, 3)
    query_grad = query_grad.reshape(local_heads, shard_len, head_dim)
    key_grad = (key_total * scaling)[None]
    value_grad = value_total[None]
    logit_grad = (-jax.nn.sigmoid(evict_logits[0]) * logit_total)[None]
    return (query_grad, key_grad, value_grad, logit_grad)


def solution(mesh):
    return jax.shard_map(
        per_device,
        mesh=mesh,
        in_specs=(
            P("head", "ctx", None),
            P("head", "ctx", None),
            P("head", "ctx", None),
            P("head", "ctx"),
            P(),
            P(("ctx", "head"), None),
            P("head", None),
        ),
        out_specs=(
            P("head", "ctx", None),
            P("head", "ctx", None),
            P("head", "ctx", None),
            P("head", "ctx"),
        ),
        check_vma=False,
    )
```

profile of v0, /device:TPU:2, one launch (start us, length us, event | category | flops | bytes accessed | tf_op | source)
XLA Modules:
  0.0 1504.7 jit_solution(7877232861619817451)
XLA Ops:
  10.3 1.0 copy.27
  11.9 153.1 %all_gather.16 = bf16[1,8192]{1,0:T(2,128)(2,1)S(1)} all-gather(bf16[1,128]{1,0:T(2,128)(2,1)S(1)} %convert_element_type.75), channel_id=1, replica_groups=mesh['ctx'=64,'head'=4] {'ctx'}, dimensions={1}, use_global_device_ids=true | all-gather | bytes 16640 | tf_op jit(solution)/shard_map/all_gather | solution.py:202
  166.0 8.0 fusion.96
  174.1 163.3 %all-gather.4.cloned.1.call-done = bf16[1,8192,128]{2,1,0:T(8,128)(2,1)} async-done(((bf16[1,128,128]{2,1,0:T(8,128)(2,1)}), bf16[1,8192,128]{2,1,0:T(8,128)(2,1)}) %all-gather.4.cloned.1.call-update) | async-done | bytes 2097168 | tf_op jit(solution)/shard_map/all_gather | solution.py:200
  337.4 298.7 %all-gather.6.cloned.1.call-done = bf16[1,8192,128]{2,1,0:T(8,128)(2,1)} async-done(((bf16[1,128,128]{2,1,0:T(8,128)(2,1)}), bf16[1,8192,128]{2,1,0:T(8,128)(2,1)}) %all-gather.6.cloned.1.call-update) | async-done | bytes 2097168 | tf_op jit(solution)/shard_map/all_gather | solution.py:201
  636.2 84.8 %while.50 = (s32[]{:T(128)}, f32[512]{0:T(512)S(1)}, f32[512]{0:T(512)S(1)}, f32[512]{0:T(512)S(1)}, f32[512]{0:T(512)S(1)}, /*index=5*/f32[512]{0:T(512)S(1)}, ...) while((s32[]{:T(128)}, f32[512]{0:T(512)S(1)}, ...), condition=%wide.region_10.11_spmd.clone, body=%wide.region_0.10_spmd.clone.sunk | while | flops 208942112 | bytes 7640539 | solution.py:82
  721.0 2.2 broadcast.267
  723.2 2.2 broadcast.267.clone
  725.4 136.7 %while.51 = (s32[]{:T(128)}, f32[512,128]{1,0:T(8,128)S(1)}, f32[512,128]{1,0:T(8,128)S(1)}, f32[8192,128]{1,0:T(8,128)}, f32[8192,128]{1,0:T(8,128)}, /*index=5...) while((s32[]{:T(128)}, f32[512,128]{1,0:T(8,128)S(1)}, ...), condition=%wide.region_15.16_spmd.clone, body=%wide.region_11.15_spmd.clone.sunk | while | flops 510267936 | bytes 18512376 | solution.py:82
  727.7 0.9 constant_dynamic-slice_fusion.11
  736.2 0.9 constant_dynamic-slice_fusion.11
  744.7 0.9 constant_dynamic-slice_fusion.11
  753.3 0.9 constant_dynamic-slice_fusion.11
  761.8 0.9 constant_dynamic-slice_fusion.11
  770.4 0.9 constant_dynamic-slice_fusion.11
  779.0 0.9 constant_dynamic-slice_fusion.11
  787.5 0.9 constant_dynamic-slice_fusion.11
  796.1 0.9 constant_dynamic-slice_fusion.11
  804.6 0.9 constant_dynamic-slice_fusion.11
  813.2 0.9 constant_dynamic-slice_fusion.11
  864.0 303.5 %all-reduce = f32[8192]{0:T(1024)S(1)} all-reduce(f32[8192]{0:T(1024)S(1)} %get-tuple-element.749), channel_id=4, replica_groups=mesh['ctx'=64,'head'=4] {'ctx'}, use_global_device_ids=true, to_apply=%region_18.19.clone | all-reduce | flops 8192 | bytes 65536
  1168.9 10.4 reduce-scatter.3.cloned.1.call-done
  1179.3 1.5 multiply_bitcast_fusion
  1180.8 317.4 %reduce-scatter.5.cloned.1.call-done = f32[128,128]{1,0:T(8,128)} async-done(((f32[8192,128]{1,0:T(8,128)}), f32[128,128]{1,0:T(8,128)}) %reduce-scatter.5.cloned.1.call-update) | async-done | bytes 65552 | tf_op jit(solution)/shard_map/reduce_scatter | solution.py:211
  (1290 shorter events, 213.8 us)
Async XLA Ops:
  7.2 158.8 %all-gather.8.cloned.1.call-start = ((), (), s32[]{:S(2)}) async-start(), calls=%async_computation.4 | async-start | bytes 1638400 | tf_op jit(solution)/shard_map/all_gather | solution.py:23
  7.9 329.6 %all-gather.4.cloned.1.call-start = ((), (), s32[]{:S(2)}) async-start(), calls=%async_computation.2 | async-start | bytes 2129920 | tf_op jit(solution)/shard_map/all_gather | solution.py:200
  8.6 627.5 %all-gather.6.cloned.1.call-start = ((), (), s32[]{:S(2)}) async-start(), calls=%async_computation.3 | async-start | bytes 2129920 | tf_op jit(solution)/shard_map/all_gather | solution.py:201
  9.4 1169.9 %reduce-scatter.3.cloned.1.call-start = ((), (), s32[]{:S(2)}) async-start(), calls=%async_computation.5 | async-start | bytes 4259840 | tf_op jit(solution)/shard_map/reduce_scatter | solution.py:210
  862.1 0.7 copy-start.1
  862.1 306.2 %copy-start = (f32[1,128]{1,0:T(1,128)S(1)}, f32[1,128]{1,0:T(1,128)}, u32[]{:S(2)}) copy-start(f32[1,128]{1,0:T(1,128)} %param.14) | copy-start | bytes 1540
  862.2 636.0 %reduce-scatter.5.cloned.1.call-start = ((), (), s32[]{:S(2)}) async-start(), calls=%async_computation.6 | async-start | bytes 4259840 | tf_op jit(solution)/shard_map/reduce_scatter | solution.py:211
Sparse Core Ops, SparseCore 0:
  9.8 26.8 all-gather.7
  38.5 298.9 all-gather.3
  339.2 296.8 all-gather.5
  862.3 316.9 reduce-scatter.2
  1182.4 315.7 reduce-scatter.4
where the time goes:
time: 1510 us; the launch traced here: 1500 us
  waiting for transfers between devices  792 us (52%)
  blocking collectives  457 us (30%)
  local copies, waits for them, and re-layouts  121 us (8%)
  matrix products  102 us (7%)
    reduce_scatter x1, waiting for transfers between devices, per_device(): lax.psum_scatter(value_terms, 'ctx', scatter_dimension=0, tiled=True)  317 us
    unnamed x1, blocking collectives  303 us
    all_gather x1, waiting for transfers between devices, per_device(): lax.all_gather(values, 'ctx', axis=1, tiled=True)  299 us
    all_gather x1, waiting for transfers between devices, per_device(): lax.all_gather(keys, 'ctx', axis=1, tiled=True)  163 us
    all_gather x1, blocking collectives, per_device(): lax.all_gather(evict_logits.astype(jnp.bfloat16), 'ctx', axis=1, tiled=True)  153 us
    dot_general x96, matrix products, score_tile(): jnp.einsum('kd,qd->kq', key_rows, query_mat[query_block], preferred_eleme...  31.7 us
  transfers between devices with their start and end apart: 5, of which 4 were waited for; matrix products, arithmetic and copies ran while one was open for 1% of the time, Pallas kernels for 0%

commit v1 on v0

v1 whole, which is shorter than its diff:
```python
import functools
import math

import jax
import jax.numpy as jnp
from jax import lax
from jax.experimental import pallas as pl
from jax.experimental.pallas import tpu as pltpu
from jax.sharding import Mesh, PartitionSpec as P

WINDOW = 256
HD = 128
HALF = 64
SHARD = 128
HEADS = 8
ROWS = HEADS * HALF
BLOCKS = 128
LOWEST = -1e30
SCALE = 1.0 / math.sqrt(HD)

NA = 4
NZ = 8
SLOTS = 2 * NZ
QB = 2 * NA
KV_ROWS = 2 * SHARD + 16

STEP = 4
CK = STEP * HALF
PER_BLOCK = SLOTS // STEP
TILES = [slice(j * SHARD, (j + 1) * SHARD) for j in range(ROWS // SHARD)]
WIDE = 256
WIDE_TILES = [slice(j * WIDE, (j + 1) * WIDE) for j in range(ROWS // WIDE)]
SKIP = 64
HIDDEN = 1000

QBLOCK_AT, SEEN_AT, SLOT_AT, POS_AT = 0, 1, 3, 5

NT = (((1,), (1,)), ((), ()))
NN = (((1,), (0,)), ((), ()))
f32, bf16, i32 = jnp.float32, jnp.bfloat16, jnp.int32


def dot(a, b, dims):
    return lax.dot_general(a, b, dims, preferred_element_type=f32)


def plan_of(blocks, y, z, xl):
    shape = (8, NA * NZ * 2)
    sub = lax.broadcasted_iota(i32, shape, 0)
    lane = lax.broadcasted_iota(i32, shape, 1)
    low = jnp.broadcast_to(blocks[0:1, :].astype(f32), shape)
    high = BLOCKS - 1.0 - low

    def picked(mask, value, axis=1):
        return jnp.sum(jnp.where(mask, value, 0.0), axis=axis, keepdims=True)

    q_low = picked(lane == ((y + (sub >> 1)) & (NA - 1)) * (2 * NZ) + z * 2 + xl, low)
    q_block = jnp.where((sub[:, :1] & 1) == 1, BLOCKS - 1.0 - q_low, q_low)
    columns = {QBLOCK_AT: q_block}
    for col in range(2):
        x = xl if col == 0 else 1 - xl
        here = ((lane >> 4) == y) & ((lane & 1) == x)
        columns[SEEN_AT + col] = picked(here & (low <= q_block), 1.0) + picked(here & (high <= q_block), 1.0)
        k_low = picked(here & (((lane >> 1) & (NZ - 1)) == sub), low)
        columns[SLOT_AT + col] = picked(here & (low < k_low), 1.0)
        rank = picked(k_low < low, 1.0, axis=0)
        columns[POS_AT + col] = picked(here & (rank == sub.astype(f32)), low)
    at = lax.broadcasted_iota(i32, (8, SHARD), 1)
    return sum(jnp.where(at == n, value, 0.0) for n, value in columns.items()).astype(i32)


def pack_kernel(where, k_ref, v_ref, logit_ref, blocks_ref, out_ref, plan_ref):
    plan_ref[...] = plan_of(blocks_ref[...], *where())
    logit = logit_ref[...]
    penalty = jnp.maximum(logit, 0.0) + jnp.log(1.0 + jnp.exp(-jnp.abs(logit)))
    upper = penalty.astype(bf16).astype(f32)
    tail = jnp.concatenate([upper, penalty - upper, jnp.zeros((14, SHARD), f32)], axis=0).astype(bf16)
    for j in range(NZ):
        out_ref[j, 0:SHARD, :] = k_ref[0]
        out_ref[j, SHARD : 2 * SHARD, :] = v_ref[0]
        out_ref[j, 2 * SHARD :, :] = tail


def cotangent_kernel(where, g0, g1, g2, g3, w_ref, out_ref, rows):
    @pl.when(pl.program_id(0) == 0)
    def _():
        xh, core = where()
        pieces = ((xh, core, g0), (1 - xh, core, g1), (xh, 1 - core, g2), (1 - xh, 1 - core, g3))
        for a, b, ref in pieces:
            rows[pl.ds(pl.multiple_of((a * 2 + b) * 32, 32), 32), :] = ref[...]

    cot = dot(rows[...], w_ref[...], NT).astype(bf16)
    for i in range(2):
        out_ref[i] = cot[:, i * HD : (i + 1) * HD]


def sort_keys(plan_ref, col, kv_ref, ks, vs, pen=None):
    for j in range(NZ):
        low = plan_ref[j, SLOT_AT + col]
        if pen is not None:
            rows = kv_ref[j, 2 * SHARD : 2 * SHARD + 16, :].astype(f32)
            penalty = jnp.broadcast_to(rows[0:1] + rows[1:2], (SHARD, SHARD)).T
        for half, slot in ((0, low), (1, SLOTS - 1 - low)):
            at = pl.ds(pl.multiple_of(slot * HALF, HALF), HALF)
            here = slice(half * HALF, (half + 1) * HALF)
            ks[at, :] = kv_ref[j, here, :]
            vs[at, :] = kv_ref[j, SHARD + half * HALF : SHARD + (half + 1) * HALF, :]
            if pen is not None:
                pen[at, :] = penalty[here, :]


def turn(src, dest):
    for i in range(SLOTS * HALF // SHARD):
        dest[i] = src[i * SHARD : (i + 1) * SHARD, :].astype(f32).T.astype(bf16)


def list_steps(plan_ref, col, pos, steps):
    for n in range(NZ):
        low = plan_ref[n, POS_AT + col]
        pos[n] = low
        pos[SLOTS - 1 - n] = BLOCKS - 1 - low
    count = jnp.int32(0)
    for rh in range(QB):
        groups = (plan_ref[rh, SEEN_AT + col] + STEP - 1) // STEP
        for c in range(PER_BLOCK):
            steps[count] = rh * PER_BLOCK + c
            count = count + (c < groups).astype(i32)
    last = steps[count - 1]
    for i in range(3):
        steps[count + i] = last + SKIP
    return count


def step_of(steps, t):
    v = steps[t]
    rh = (v // PER_BLOCK) % QB
    c = v % PER_BLOCK
    return v, rh, c, pl.ds(pl.multiple_of(c * CK, CK), CK)


def thresholds(plan_ref, pos, v, rh, c):
    q_block = plan_ref[rh, QBLOCK_AT]
    ahead = [(q_block - pos[c * STEP + i]) * HALF for i in range(STEP)]
    return [(jnp.where(v >= SKIP, HIDDEN, -d), WINDOW - d) for d in ahead]


def offsets():
    shape = (HALF, SHARD)
    return lax.broadcasted_iota(i32, shape, 1) % HALF - lax.broadcasted_iota(i32, shape, 0)


def block_rows(c, i):
    return pl.ds(pl.multiple_of(c * CK + i * HALF, HALF), HALF)


def turned_piece(ref, c):
    n = CK // SHARD
    return jnp.concatenate([ref[c * n + i] for i in range(n)], axis=1)


def load_rows(refs, dest):
    for r, ref in enumerate(refs):
        for half in range(2):
            dest[2 * r + half] = ref[:, half * HALF : (half + 1) * HALF, :].reshape(ROWS, HD)


def forward_kernel(col, plan_ref, *refs):
    if col == 0:
        rows_in, (kv_ref, o_ref, st_ref, peaks, exps, qs, qt), refs = refs[:4], refs[4:11], refs[11:]
    else:
        (qt, kv_ref, o_ref, st_ref, peaks, exps), refs = refs[:6], refs[6:]
    ks, vs, vt, pen, s_a, s_b, f_a, f_b, pos, steps = refs
    count = list_steps(plan_ref, col, pos, steps)
    if col == 0:
        load_rows(rows_in, qs)
        for rh in range(QB):
            qt[rh] = qs[rh].astype(f32).T.astype(bf16)
    sort_keys(plan_ref, col, kv_ref, ks, vs, pen)
    turn(vs, vt)
    o_ref[...] = jnp.zeros_like(o_ref)
    for rh in range(QB):
        st_ref[rh, 0:1, :] = jnp.full((1, ROWS), LOWEST, f32)
        st_ref[rh, 1:2, :] = jnp.zeros((1, ROWS), f32)
    exps[0] = jnp.zeros_like(exps[0])
    f_b[...] = jnp.ones_like(f_b)

    def score(t, s_ref):
        _, rh, _, at = step_of(steps, t)
        s_ref[...] = dot(ks[at, :], qt[rh], NN)

    def soften(t, s_ref, f_ref):
        v, rh, c, _ = step_of(steps, t)
        limits = thresholds(plan_ref, pos, v, rh, c)
        offset = offsets()
        for lanes in TILES:
            parts = []
            for i, (seen, late) in enumerate(limits):
                s = s_ref[i * HALF : (i + 1) * HALF, lanes] * SCALE
                s = s - jnp.where(offset >= late, pen[block_rows(c, i), :], 0.0)
                parts.append(jnp.where(offset >= seen, s, LOWEST))
            peak = st_ref[rh, 0:1, lanes]
            tops = functools.reduce(jnp.maximum, parts)
            new_peak = jnp.maximum(peak, jnp.max(tops, axis=0, keepdims=True))
            factor = jnp.exp(peak - new_peak)
            parts = [jnp.exp(s - new_peak) for s in parts]
            total = jnp.sum(sum(parts), axis=0, keepdims=True)
            for i, p in enumerate(parts):
                exps[t, i * HALF : (i + 1) * HALF, lanes] = p.astype(bf16)
            f_ref[0:1, lanes] = factor
            peaks[t, 0:1, lanes] = new_peak
            st_ref[rh, 0:1, lanes] = new_peak
            st_ref[rh, 1:2, lanes] = st_ref[rh, 1:2, lanes] * factor + total

    def attend(t, f_ref):
        _, rh, c, _ = step_of(steps, t)
        o_ref[rh] = o_ref[rh] * f_ref[0:1, :] + dot(turned_piece(vt, c), exps[t], NN)

    score(0, s_a)

    def pair(i, _):
        t = 2 * i
        attend(jnp.maximum(t - 1, 0), f_b)
        score(t + 1, s_b)
        soften(t, s_a, f_a)
        attend(t, f_a)
        score(t + 2, s_a)
        soften(t + 1, s_b, f_b)
        return 0

    pairs = (count + 1) // 2
    lax.fori_loop(0, pairs, pair, 0)
    attend(2 * pairs - 1, f_b)


def weigh_kernel(o0, st0, o1, st1, c0, c1, c2, c3, out_ref, cs, ct):
    for r, ref in enumerate((c0, c1, c2, c3)):
        for half in range(2):
            rh = 2 * r + half
            rows = ref[:, half * HALF : (half + 1) * HALF, :].reshape(ROWS, HD)
            cot = rows.astype(f32).T
            cs[rh] = rows
            ct[rh] = cot.astype(bf16)
            peak = jnp.maximum(st0[rh, 0:1, :], st1[rh, 0:1, :])
            f0, f1 = (jnp.exp(st[rh, 0:1, :] - peak) for st in (st0, st1))
            total = st0[rh, 1:2, :] * f0 + st1[rh, 1:2, :] * f1
            seen = total > 0.0
            weighted = jnp.sum(cot * (o0[rh] * f0 + o1[rh] * f1), axis=0, keepdims=True)
            safe = jnp.where(seen, total, 1.0)
            out_ref[rh : rh + 1, :] = jnp.where(seen, peak + jnp.log(safe), LOWEST)
            out_ref[QB + rh : QB + rh + 1, :] = weighted / safe


def merge_stats(pieces, stats):
    for r in range(NA):
        for half in range(2):
            rh = 2 * r + half
            parts = [(ref, 2 * ((r - t) % NA) + half) for t, ref in enumerate(pieces)]
            norms = [ref[n : n + 1, :] for ref, n in parts]
            means = [ref[QB + n : QB + n + 1, :] for ref, n in parts]
            peak = functools.reduce(jnp.maximum, norms)
            shares = [jnp.exp(norm - peak) for norm in norms]
            total = sum(shares)
            stats[rh, 0:1, :] = peak + jnp.log(total)
            stats[rh, 1:2, :] = sum(share * mean for share, mean in zip(shares, means)) / total


def backward_kernel(col, plan_ref, *refs):
    (qs, cs, ct, kv_ref, peaks, exps), pieces, refs = refs[:6], refs[6:10], refs[10:]
    if col == 1:
        (dq, dkv_ref), refs = refs[:2], refs[2:]
    else:
        (dq_before,), dq_out, (dkv_ref,), refs = refs[:1], refs[1:5], refs[5:6], refs[6:]
        (dq, turned, sems), refs = refs[:3], refs[3:]
    ks, vs, kt, dk, dv, dl, stats, p_a, p_b, d_a, d_b, pos, steps = refs
    count = list_steps(plan_ref, col, pos, steps)
    sort_keys(plan_ref, col, kv_ref, ks, vs)
    turn(ks, kt)
    for ref in (dk, dv, dl, p_b, d_b):
        ref[...] = jnp.zeros_like(ref)
    dq[...] = jnp.zeros_like(dq) if col == 1 else dq_before[...]
    merge_stats(pieces, stats)

    def differ(t, p_ref, d_ref):
        v, rh, c, _ = step_of(steps, t)
        offset = offsets()
        shares = [jnp.exp(peaks[t, 0:1, lanes] - stats[rh, 0:1, lanes]) for lanes in TILES]
        for i, (_, late) in enumerate(thresholds(plan_ref, pos, v, rh, c)):
            at = block_rows(c, i)
            rows = slice(i * HALF, (i + 1) * HALF)
            delayed = offset >= late
            late_sum = dl[at, :]
            for wide in WIDE_TILES:
                grad = dot(vs[at, :], ct[rh, :, wide], NN)
                for j in range(WIDE // SHARD):
                    here = slice(j * SHARD, (j + 1) * SHARD)
                    lanes = slice(wide.start + here.start, wide.start + here.stop)
                    p = exps[t, rows, lanes].astype(f32) * shares[lanes.start // SHARD]
                    d = p * (grad[:, here] - stats[rh, 1:2, lanes])
                    late_sum = late_sum + jnp.where(delayed, d, 0.0)
                    p_ref[rows, lanes] = p.astype(bf16)
                    d_ref[rows, lanes] = d.astype(bf16)
            dl[at, :] = late_sum

    def gather(t, p_ref, d_ref):
        _, rh, c, at = step_of(steps, t)
        dk[at, :] += dot(d_ref[...], qs[rh], NN)
        dv[at, :] += dot(p_ref[...], cs[rh], NN)
        dq[rh] += dot(turned_piece(kt, c), d_ref[...], NN)

    def pair(i, _):
        t = 2 * i
        gather(jnp.maximum(t - 1, 0), p_b, d_b)
        differ(t, p_a, d_a)
        gather(t, p_a, d_a)
        differ(t + 1, p_b, d_b)
        return 0

    pairs = (count + 1) // 2
    lax.fori_loop(0, pairs, pair, 0)
    gather(2 * pairs - 1, p_b, d_b)
    copies = []
    if col == 0:
        for r, ref in enumerate(dq_out):
            for half in range(2):
                rows = (dq[2 * r + half].T * SCALE).astype(bf16)
                turned[r, :, half * HALF : (half + 1) * HALF, :] = rows.reshape(HEADS, HALF, HD)
            copies.append(pltpu.make_async_copy(turned.at[r], ref, sems.at[r]))
            copies[-1].start()
    for j in range(NZ):
        low = plan_ref[j, SLOT_AT + col]
        spots = [pl.ds(pl.multiple_of(slot * HALF, HALF), HALF) for slot in (low, SLOTS - 1 - low)]
        for half, at in enumerate(spots):
            dkv_ref[j, half * HALF : (half + 1) * HALF, :] = (dk[at, :] * SCALE).astype(dkv_ref.dtype)
            dkv_ref[j, SHARD + half * HALF : SHARD + (half + 1) * HALF, :] = dv[at, :].astype(dkv_ref.dtype)
        late = jnp.concatenate([dl[at, :] for at in spots], axis=0)
        total = jnp.sum(late.T, axis=0, keepdims=True)
        dkv_ref[j, 2 * SHARD : 2 * SHARD + 16, :] = jnp.concatenate(
            [total, jnp.zeros((15, SHARD), f32)], axis=0
        ).astype(dkv_ref.dtype)
    for copy in copies:
        copy.wait()


VMEM = pl.BlockSpec(memory_space=pltpu.VMEM)
SMEM = pl.BlockSpec(memory_space=pltpu.SMEM)
HBM = pl.BlockSpec(memory_space=pltpu.HBM)


def grant(mib):
    return pltpu.CompilerParams(vmem_limit_bytes=mib * 1024 * 1024)


MOST = 5 * NA
ROOMY = grant(54)
KEYS = SLOTS * HALF
shaped = jax.ShapeDtypeStruct


def cost(us):
    return pl.CostEstimate(flops=int(us * 1e9), bytes_accessed=2**20, transcendentals=0)


def run_pack(where, keys, values, logits, block_order):
    return pl.pallas_call(
        functools.partial(pack_kernel, where),
        out_shape=(shaped((NZ, KV_ROWS, HD), bf16), shaped((8, SHARD), i32)),
        in_specs=[VMEM] * 4,
        out_specs=(VMEM, VMEM),
        name="pack",
    )(keys, values, logits, block_order.T)


def run_cotangent(where, pieces, w_out):
    rows, width = w_out.shape
    return pl.pallas_call(
        functools.partial(cotangent_kernel, where),
        out_shape=shaped((HEADS, SHARD, HD), bf16),
        grid=(HEADS // 2,),
        in_specs=[pl.BlockSpec((32, width), lambda i: (0, 0))] * 4
        + [pl.BlockSpec((2 * HD, width), lambda i: (i, 0))],
        out_specs=pl.BlockSpec((2, SHARD, HD), lambda i: (i, 0, 0)),
        scratch_shapes=[pltpu.VMEM((SHARD, width), bf16)],
        compiler_params=ROOMY,
        cost_estimate=cost(5),
        name="cotangent",
    )(*pieces, w_out)


def run_forward(col, plan, q, kv):
    out_shape = (
        shaped((QB, HD, ROWS), f32),
        shaped((QB, 2, ROWS), f32),
        shaped((MOST, 1, ROWS), f32),
        shaped((MOST, CK, ROWS), bf16),
    )
    if col == 0:
        out_shape += (shaped((QB, ROWS, HD), bf16), shaped((QB, HD, ROWS), bf16))
    o, st, peaks, exps, *turned = pl.pallas_call(
        functools.partial(forward_kernel, col),
        out_shape=out_shape,
        in_specs=[SMEM] + [VMEM] * (len(q) + 1),
        out_specs=(VMEM,) * len(out_shape),
        scratch_shapes=[
            pltpu.VMEM((KEYS, HD), bf16),
            pltpu.VMEM((KEYS, HD), bf16),
            pltpu.VMEM((KEYS // SHARD, HD, SHARD), bf16),
            pltpu.VMEM((KEYS, SHARD), f32),
            pltpu.VMEM((CK, ROWS), f32),
            pltpu.VMEM((CK, ROWS), f32),
            pltpu.VMEM((8, ROWS), f32),
            pltpu.VMEM((8, ROWS), f32),
            pltpu.SMEM((SLOTS,), i32),
            pltpu.SMEM((QB * PER_BLOCK + 3,), i32),
        ],
        compiler_params=grant(14),
        cost_estimate=cost(10),
        name=f"forward{col}",
    )(plan, *q, kv)
    return (o, st), (peaks, exps), turned


def run_weigh(sums, cot):
    return pl.pallas_call(
        weigh_kernel,
        out_shape=(
            shaped((2 * QB, ROWS), f32),
            shaped((QB, ROWS, HD), bf16),
            shaped((QB, HD, ROWS), bf16),
        ),
        in_specs=[VMEM] * 8,
        out_specs=(VMEM,) * 3,
        compiler_params=grant(8),
        name="weigh",
    )(*sums, *cot)


def run_backward(col, plan, rows, kv, exps, stats, dq_sum=None):
    if col == 1:
        more, scratch = (), []
        out_shape = (shaped((QB, HD, ROWS), f32), shaped((NZ, KV_ROWS, HD), bf16))
        out_specs = (VMEM, VMEM)
    else:
        more = (dq_sum,)
        scratch = [
            pltpu.VMEM((QB, HD, ROWS), f32),
            pltpu.VMEM((NA, HEADS, SHARD, HD), bf16),
            pltpu.SemaphoreType.DMA((NA,)),
        ]
        out_shape = (shaped((HEADS, SHARD, HD), bf16),) * NA + (shaped((NZ, KV_ROWS, HD), f32),)
        out_specs = (HBM,) * NA + (VMEM,)
    return pl.pallas_call(
        functools.partial(backward_kernel, col),
        out_shape=out_shape,
        in_specs=[SMEM] + [VMEM] * (10 + len(more)),
        out_specs=out_specs,
        scratch_shapes=scratch
        + [
            pltpu.VMEM((KEYS, HD), bf16),
            pltpu.VMEM((KEYS, HD), bf16),
            pltpu.VMEM((KEYS // SHARD, HD, SHARD), bf16),
            pltpu.VMEM((KEYS, HD), f32),
            pltpu.VMEM((KEYS, HD), f32),
            pltpu.VMEM((KEYS, SHARD), f32),
            pltpu.VMEM((QB, 2, ROWS), f32),
        ]
        + [pltpu.VMEM((CK, ROWS), bf16)] * 4
        + [pltpu.SMEM((SLOTS,), i32), pltpu.SMEM((QB * PER_BLOCK + 3,), i32)],
        compiler_params=grant(18),
        cost_estimate=cost(15),
        name=f"backward{col}",
    )(plan, *rows, kv, *exps, *stats, *more)


def from_y(x, r):
    return lax.ppermute(x, "y", [((i + r) % NA, i) for i in range(NA)])


def gather_y(x):
    return [x] + [from_y(x, r) for r in range(1, NA)]


def swap(x, axis):
    return lax.ppermute(x, axis, [(0, 1), (1, 0)])


def place():
    return lax.axis_index("y"), lax.axis_index("z"), lax.axis_index("xl")


def head_place():
    return lax.axis_index("xh"), lax.axis_index("core")


def per_device(queries, keys, values, evict_logits, block_order, grad_y, w_out):
    packed, plan = run_pack(place, keys, values, evict_logits, block_order)
    kv = lax.all_to_all(packed, "z", 0, 0, tiled=True)
    over = swap(grad_y, "xh")
    pieces = (grad_y, over, swap(grad_y, "core"), swap(over, "core"))
    q_all = gather_y(queries)
    cot = run_cotangent(head_place, pieces, w_out)
    kv_other = swap(kv, "xl")
    cot_all = gather_y(cot)
    sums0, exps0, (qs, qt) = run_forward(0, plan, q_all, kv)
    sums1, exps1, _ = run_forward(1, plan, (qt,), kv_other)
    stats, cs, ct = run_weigh((*sums0, *sums1), cot_all)
    rows = (qs, cs, ct)
    stats = gather_y(stats)
    dq_sum, dkv_other = run_backward(1, plan, rows, kv_other, exps1, stats)
    dkv_here = swap(dkv_other, "xl")
    *dq, dkv = run_backward(0, plan, rows, kv, exps0, stats, dq_sum)
    dkv = (dkv + dkv_here.astype(f32)).astype(bf16)
    dkv = jnp.sum(lax.all_to_all(dkv, "z", 0, 0, tiled=True).astype(f32), axis=0)
    query_grad = dq[0].astype(f32)
    for r in range(1, NA):
        query_grad = query_grad + from_y(dq[r], NA - r).astype(f32)
    logit_grad = -jax.nn.sigmoid(evict_logits[0]) * dkv[2 * SHARD]
    return (
        query_grad.astype(bf16),
        dkv[None, :SHARD],
        dkv[None, SHARD : 2 * SHARD],
        logit_grad[None],
    )


def solution(mesh):
    split = Mesh(mesh.devices.reshape(4, 8, 2, 2, 2), ("y", "z", "xl", "xh", "core"))
    ctx, head = ("y", "z", "xl"), ("xh", "core")
    return jax.shard_map(
        per_device,
        mesh=split,
        in_specs=(
            P(head, ctx, None),
            P(head, ctx, None),
            P(head, ctx, None),
            P(head, ctx),
            P(),
            P(ctx + head, None),
            P(head, None),
        ),
        out_specs=(
            P(head, ctx, None),
            P(head, ctx, None),
            P(head, ctx, None),
            P(head, ctx),
        ),
        check_vma=False,
    )
```

time: 1510 us -> 108 us (0.07)
  waiting for transfers between devices: 792 us -> 16.1 us
  blocking collectives: 457 us -> 0 us
  local copies, waits for them, and re-layouts: 121 us -> 2.13 us
  matrix products: 102 us -> 0 us
  Pallas kernels: 0 us -> 45.2 us
  starting transfers between devices: 0.19 us -> 40.4 us
    all_gather x3 -> x0, waiting for transfers between devices: 462 us -> none  [the longest x1 299 us: per_device(): lax.all_gather(values, 'ctx', axis=1, tiled=True)]
    reduce_scatter x2 -> x0, waiting for transfers between devices: 328 us -> none  [the longest x1 317 us: per_device(): lax.psum_scatter(value_terms, 'ctx', scatter_dimension=0, tiled=True)]
    unnamed x1 -> x0, blocking collectives: 303 us -> none
    all_gather x1 -> x0, blocking collectives: 153 us -> none  [per_device(): lax.all_gather(evict_logits.astype(jnp.bfloat16), 'ctx', axis=1, tiled=True)]
    dot_general x337 -> x0, matrix products: 102 us -> none  [the longest x96 31.7 us: score_tile(): jnp.einsum('kd,qd->kq', key_rows, query_mat[query_block], preferred_eleme...]
    dynamic_slice x96 -> x0, local copies, waits for them, and re-layouts: 59.5 us -> none  [the longest x32 29.4 us: split_keys(): lax.dynamic_slice_in_dim(portion[1][0], first_row, width, 0)]
    pallas_call x0 -> x7, Pallas kernels: none -> 45.2 us  [the longest x2 20.1 us: run_backward(): pl.pallas_call(functools.partial(backward_kernel, col), out_shape=out_sha...]
    ppermute x0 -> x17, starting transfers between devices: none -> 24.3 us  [the longest x12 19.1 us: from_y(): return lax.ppermute(x, 'y', [((i + r) % NA, i) for i in range(NA)])]
  transfers between devices with their start and end apart: 5 -> 19, of which waited for: 4 -> 6; matrix products, arithmetic and copies ran while one was open for 1% -> 1% of each run, Pallas kernels for 0% -> 33%
where the time goes in v1:
time: 108 us; the launch traced here: 107 us
  Pallas kernels  45.2 us (42%)
  starting transfers between devices  40.4 us (37%)
  waiting for transfers between devices  16.1 us (15%)
  other arithmetic  2.37 us (2%)
  local copies, waits for them, and re-layouts  2.13 us (2%)
    pallas_call x2, Pallas kernels, run_backward(): pl.pallas_call(functools.partial(backward_kernel, col), out_shape=out_sha...  20.1 us
    ppermute x12, starting transfers between devices, from_y(): return lax.ppermute(x, 'y', [((i + r) % NA, i) for i in range(NA)])  19.1 us
    pallas_call x2, Pallas kernels, run_forward(): pl.pallas_call(functools.partial(forward_kernel, col), out_shape=out_shap...  14.9 us
    ppermute x12, waiting for transfers between devices, from_y(): return lax.ppermute(x, 'y', [((i + r) % NA, i) for i in range(NA)])  10.2 us
    all_to_all x1, starting transfers between devices, per_device(): kv = lax.all_to_all(packed, 'z', 0, 0, tiled=True)  8.47 us
    pallas_call x1, Pallas kernels, run_cotangent(): pl.pallas_call(functools.partial(cotangent_kernel, where), out_shape=shap...  7.74 us
    all_to_all x1, starting transfers between devices, per_device(): lax.all_to_all(dkv, 'z', 0, 0, tiled=True).astype(f32)  7.57 us
    ppermute x5, starting transfers between devices, swap(): return lax.ppermute(x, axis, [(0, 1), (1, 0)])  5.19 us
  transfers between devices with their start and end apart: 19, of which 6 were waited for; matrix products, arithmetic and copies ran while one was open for 1% of the time, Pallas kernels for 33%

profile of v1, /device:TPU:2, one launch (start us, length us, event | category | flops | bytes accessed | tf_op | source)
XLA Modules:
  0.0 107.0 jit_solution(14193488383719427411)
XLA Ops:
  0.6 2.2 %collective-permute-start.4 = (bf16[32,5120]{1,0:T(8,128)(2,1)}, bf16[32,5120]{1,0:T(8,128)(2,1)S(1)}, u32[]{:S(2)}, u32[]{:S(2)}) collective-permute-start(bf16[32,5120]{1,0:T(8,128)(2,1)} %g0.1), channel_id=1, source_target_pairs={{0,2},{2,0},{1,3},{3,1},{4,6},{6,4},{5,7},{7,5},{8,10},{10,8},{9,1... | collective-permute-start | bytes 983048 | tf_op jit(solution)/shard_map/ppermute | solution.py:483
  2.8 1.7 %pack.1 = (bf16[8,272,128]{2,1,0:T(8,128)(2,1)}, s32[8,128]{1,0:T(8,128)}) custom-call(bf16[1,128,128]{2,1,0:T(8,128)(2,1)} %k_ref.1, bf16[1,128,128]{2,1,0:T(8,128)(2,1)} %v_ref.1, f32[1,128]{1,0:T(1,128)} %logit_ref.1, s32[2,64]{1,0:T(2,128)} %bitcast.5), custom_call_target="tpu_custom_call" | custom-call | tf_op jit(solution)/shard_map/pack/pallas_call | solution.py:364
  4.6 8.5 %all-to-all-start = ((bf16[8,272,128]{2,1,0:T(8,128)(2,1)}), bf16[8,272,128]{2,1,0:T(8,128)(2,1)S(1)}, u32[]{:S(2)}, u32[]{:S(2)}) async-start(bf16[8,272,128]{2,1,0:T(8,128)(2,1)} %get-tuple-element.27), calls=%async_computation | async-start | bytes 1114112 | tf_op jit(solution)/shard_map/all_to_all | solution.py:496
  13.6 3.2 %collective-permute-start.1 = (bf16[8,128,128]{2,1,0:T(8,128)(2,1)}, bf16[8,128,128]{2,1,0:T(8,128)(2,1)S(1)}, u32[]{:S(2)}, u32[]{:S(2)}) collective-permute-start(bf16[8,128,128]{2,1,0:T(8,128)(2,1)} %refs_0_.1), channel_id=1, source_target_pairs={{128,0},{192,64},{0,128},{64,192},{129,1},{193,65},{1,129},{65,193... | collective-permute-start | bytes 786440 | tf_op jit(solution)/shard_map/ppermute | solution.py:475
  16.8 1.1 collective-permute-start
  17.9 1.0 collective-permute-start.2
  20.3 7.7 %cotangent.1.c0 = bf16[8,128,128]{2,1,0:T(8,128)(2,1)} custom-call(bf16[32,5120]{1,0:T(8,128)(2,1)} %g0.1, bf16[32,5120]{1,0:T(8,128)(2,1)} %copy-done.4, bf16[32,5120]{1,0:T(8,128)(2,1)} %copy-done.5, bf16[32,5120]{1,0:T(8,128)(2,1)} %copy-done.6, bf16[1024,5120]{1,0:T(8,128)(2,1)} %w_ref.1), custom_call_target="tpu_custom_call" | custom-call | flops 5000000000 | bytes 1048576 | tf_op jit(solution)/shard_map/cotangent/pallas_call | solution.py:375
  28.8 3.1 %collective-permute-start.8 = (bf16[8,128,128]{2,1,0:T(8,128)(2,1)}, bf16[8,128,128]{2,1,0:T(8,128)(2,1)S(1)}, u32[]{:S(2)}, u32[]{:S(2)}) collective-permute-start(bf16[8,128,128]{2,1,0:T(8,128)(2,1)} %cotangent.1.c0), channel_id=1, source_target_pairs={{128,0},{192,64},{0,128},{64,192},{129,1},{193,65},{1,129},{65,193... | collective-permute-start | bytes 786440 | tf_op jit(solution)/shard_map/ppermute | solution.py:475
  31.8 1.5 %collective-permute-start.3 = (bf16[8,272,128]{2,1,0:T(8,128)(2,1)S(1)}, bf16[8,272,128]{2,1,0:T(8,128)(2,1)S(1)}, u32[]{:S(2)}, u32[]{:S(2)}) collective-permute-start(bf16[8,272,128]{2,1,0:T(8,128)(2,1)S(1)} %all-to-all-done.refs_4_.refs_3_), channel_id=1, source_target_pairs={{0,4},{4,0},{1,5},{5,1},{2,6},{6,2},{3,7},{7,3},{8,12},{12,8},{9,1... | collective-permute-start | bytes 1671176 | tf_op jit(solution)/shard_map/ppermute | solution.py:483
  33.4 7.9 %forward0.1 = (f32[8,128,512]{2,1,0:T(8,128)S(1)}, f32[8,2,512]{2,1,0:T(2,128)S(1)}, f32[20,1,512]{2,1,0:T(1,128)S(1)}, bf16[20,256,512]{2,1,0:T(8,128)(2,1)S(1)...) custom-call(s32[8,128]{1,0:T(8,128)S(1)} %copy-done.2, bf16[8,128,128]{2,1,0:T(8,128)(2,1)S(1)} %copy-done.1, ...), custom_call_target="tpu_custom_call" | custom-call | flops 10000000000 | bytes 1048576 | tf_op jit(solution)/shard_map/forward0/pallas_call | solution.py:398
  41.3 3.8 %collective-permute-done.3.refs_1_.refs_3_ = bf16[8,272,128]{2,1,0:T(8,128)(2,1)S(1)} collective-permute-done((bf16[8,272,128]{2,1,0:T(8,128)(2,1)S(1)}, bf16[8,272,128]{2,1,0:T(8,128)(2,1)S(1)}, u32[]{:S(2)}, u32[]{:S(2)}) %collective-permute-start.3) | collective-permute-done | bytes 557088 | tf_op jit(solution)/shard_map/ppermute | solution.py:483
  45.2 7.0 %forward1.1 = (f32[8,128,512]{2,1,0:T(8,128)S(1)}, f32[8,2,512]{2,1,0:T(2,128)S(1)}, f32[20,1,512]{2,1,0:T(1,128)S(1)}, bf16[20,256,512]{2,1,0:T(8,128)(2,1)S(1)}) custom-call(s32[8,128]{1,0:T(8,128)S(1)} %copy-done.2, bf16[8,128,512]{2,1,0:T(8,128)(2,1)S(1)} %get-tuple-element.31.refs_0_, bf16[8,272,128]{2,1,0:T(8,128)(2,1)S(1)} %collective-permute-done.3.refs_1_.refs_3_), custom_call_target="tpu_custom_call" | custom-call | flops 10000000000 | bytes 1048576 | tf_op jit(solution)/shard_map/forward1/pallas_call | solution.py:398
  52.9 1.7 %collective-permute-start.12 = (f32[16,512]{1,0:T(8,128)S(1)}, f32[16,512]{1,0:T(8,128)S(1)}, u32[]{:S(2)}, u32[]{:S(2)}) collective-permute-start(f32[16,512]{1,0:T(8,128)S(1)} %get-tuple-element.38.refs_6_), channel_id=1, source_target_pairs={{192,0},{0,64},{64,128},{128,192},{193,1},{1,65},{65,129},{129,193... | collective-permute-start | bytes 98312 | tf_op jit(solution)/shard_map/ppermute | solution.py:475
  54.6 3.3 %collective-permute-start.11 = (f32[16,512]{1,0:T(8,128)S(1)}, f32[16,512]{1,0:T(8,128)S(1)}, u32[]{:S(2)}, u32[]{:S(2)}) collective-permute-start(f32[16,512]{1,0:T(8,128)S(1)} %get-tuple-element.38.refs_6_), channel_id=1, source_target_pairs={{128,0},{192,64},{0,128},{64,192},{129,1},{193,65},{1,129},{65,193... | collective-permute-start | bytes 98312 | tf_op jit(solution)/shard_map/ppermute | solution.py:475
  58.0 1.3 %collective-permute-start.10 = (f32[16,512]{1,0:T(8,128)S(1)}, f32[16,512]{1,0:T(8,128)S(1)}, u32[]{:S(2)}, u32[]{:S(2)}) collective-permute-start(f32[16,512]{1,0:T(8,128)S(1)} %get-tuple-element.38.refs_6_), channel_id=1, source_target_pairs={{64,0},{128,64},{192,128},{0,192},{65,1},{129,65},{193,129},{1,193... | collective-permute-start | bytes 98312 | tf_op jit(solution)/shard_map/ppermute | solution.py:475
  60.2 1.7 %collective-permute-done.10.refs_7_ = f32[16,512]{1,0:T(8,128)S(1)} collective-permute-done((f32[16,512]{1,0:T(8,128)S(1)}, f32[16,512]{1,0:T(8,128)S(1)}, u32[]{:S(2)}, u32[]{:S(2)}) %collective-permute-start.10) | collective-permute-done | bytes 32800 | tf_op jit(solution)/shard_map/ppermute | solution.py:475
  61.9 9.1 %backward1.1 = (f32[8,128,512]{2,1,0:T(8,128)S(1)}, bf16[8,272,128]{2,1,0:T(8,128)(2,1)S(1)}) custom-call(s32[8,128]{1,0:T(8,128)S(1)} %copy-done.2, bf16[8,512,128]{2,1,0:T(8,128)(2,1)S(1)} %get-tuple-element.28.refs_0_, bf16[8,512,128]{2,1,0:T(8,128)(2,1)S(1)} %get-tuple-element.34.refs_1_, bf16[8,128,512]{2,1,0:T(8,128)(2,1)S(1)} %get-tuple-element.35.refs_2_, ...), custom_call_target="tpu_custom_call" | custom-call | flops 15000000512 | bytes 1048576 | tf_op jit(solution)/shard_map/backward1/pallas_call | solution.py:451
  71.9 11.0 %backward0.1 = (bf16[8,128,128]{2,1,0:T(8,128)(2,1)S(1)}, bf16[8,128,128]{2,1,0:T(8,128)(2,1)S(1)}, bf16[8,128,128]{2,1,0:T(8,128)(2,1)S(1)}, bf16[8,128,128]{2,1,0:T(8,128)(2,1)S(1)}, f32[8,272,128]{2,1,0:T(8,128)S(1)}) custom-call(s32[8,128]{1,0:T(8,128)S(1)} %copy-done.2, bf16[8,512,128]{2,1,0:T(8,128)(2,1)S(1)} %get-tuple-element.28.refs_0_, ...), custom_call_target="tpu_custom_call" | custom-call | flops 15000000512 | bytes 1048576 | tf_op jit(solution)/shard_map/backward0/pallas_call | solution.py:451
  83.8 7.6 %all-to-all-start.1 = ((bf16[8,272,128]{2,1,0:T(8,128)(2,1)}), bf16[8,272,128]{2,1,0:T(8,128)(2,1)S(1)}, u32[]{:S(2)}, u32[]{:S(2)}) async-start(bf16[8,272,128]{2,1,0:T(8,128)(2,1)} %add_convert_fusion), calls=%async_computation.1 | async-start | bytes 1114112 | tf_op jit(solution)/shard_map/all_to_all | solution.py:512
  91.4 0.9 collective-permute-start.13
  92.3 1.5 %collective-permute-start.14 = (bf16[8,128,128]{2,1,0:T(8,128)(2,1)S(1)}, bf16[8,128,128]{2,1,0:T(8,128)(2,1)S(1)}, u32[]{:S(2)}, u32[]{:S(2)}) collective-permute-start(bf16[8,128,128]{2,1,0:T(8,128)(2,1)S(1)} %get-tuple-element.44), channel_id=1, source_target_pairs={{128,0},{192,64},{0,128},{64,192},{129,1},{193,65},{1,129},{65,193... | collective-permute-start | bytes 786440 | tf_op jit(solution)/shard_map/ppermute | solution.py:475
  93.8 1.3 %collective-permute-start.15 = (bf16[8,128,128]{2,1,0:T(8,128)(2,1)S(1)}, bf16[8,128,128]{2,1,0:T(8,128)(2,1)S(1)}, u32[]{:S(2)}, u32[]{:S(2)}) collective-permute-start(bf16[8,128,128]{2,1,0:T(8,128)(2,1)S(1)} %get-tuple-element.45), channel_id=1, source_target_pairs={{64,0},{128,64},{192,128},{0,192},{65,1},{129,65},{193,129},{1,193... | collective-permute-start | bytes 786440 | tf_op jit(solution)/shard_map/ppermute | solution.py:475
  95.2 6.9 %collective-permute-done.13 = bf16[8,128,128]{2,1,0:T(8,128)(2,1)S(1)} collective-permute-done((bf16[8,128,128]{2,1,0:T(8,128)(2,1)S(1)}, bf16[8,128,128]{2,1,0:T(8,128)(2,1)S(1)}, u32[]{:S(2)}, u32[]{:S(2)}) %collective-permute-start.13) | collective-permute-done | bytes 262176 | tf_op jit(solution)/shard_map/ppermute | solution.py:475
  103.6 2.1 %all-to-all-done.1 = bf16[8,272,128]{2,1,0:T(8,128)(2,1)S(1)} async-done(((bf16[8,272,128]{2,1,0:T(8,128)(2,1)}), bf16[8,272,128]{2,1,0:T(8,128)(2,1)S(1)}, u32[]{:S(2)}, u32[]{:S(2)}) %all-to-all-start.1) | async-done | bytes 557088 | tf_op jit(solution)/shard_map/all_to_all | solution.py:512
  (40 shorter events, 8.9 us)
Async XLA Ops:
  0.6 12.5 %collective-permute-start.4 = (bf16[32,5120]{1,0:T(8,128)(2,1)}, bf16[32,5120]{1,0:T(8,128)(2,1)S(1)}, u32[]{:S(2)}, u32[]{:S(2)}) collective-permute-start(bf16[32,5120]{1,0:T(8,128)(2,1)} %g0.1), channel_id=1, source_target_pairs={{0,2},{2,0},{1,3},{3,1},{4,6},{6,4},{5,7},{7,5},{8,10},{10,8},{9,1... | collective-permute-start | bytes 983048 | tf_op jit(solution)/shard_map/ppermute | solution.py:483
  4.6 27.3 %all-to-all-start = ((bf16[8,272,128]{2,1,0:T(8,128)(2,1)}), bf16[8,272,128]{2,1,0:T(8,128)(2,1)S(1)}, u32[]{:S(2)}, u32[]{:S(2)}) async-start(bf16[8,272,128]{2,1,0:T(8,128)(2,1)} %get-tuple-element.27), calls=%async_computation | async-start | bytes 1114112 | tf_op jit(solution)/shard_map/all_to_all | solution.py:496
  13.0 20.3 %copy-start.1 = (bf16[8,128,128]{2,1,0:T(8,128)(2,1)S(1)}, bf16[8,128,128]{2,1,0:T(8,128)(2,1)}, u32[]{:S(2)}) copy-start(bf16[8,128,128]{2,1,0:T(8,128)(2,1)} %refs_0_.1) | copy-start | bytes 786436
  13.0 20.3 %copy-start.2 = (s32[8,128]{1,0:T(8,128)S(1)}, s32[8,128]{1,0:T(8,128)}, u32[]{:S(2)}) copy-start(s32[8,128]{1,0:T(8,128)} %get-tuple-element.26.plan_ref) | copy-start | bytes 12292
  13.0 5.8 %collective-permute-start.5 = (bf16[32,5120]{1,0:T(8,128)(2,1)}, bf16[32,5120]{1,0:T(8,128)(2,1)S(1)}, u32[]{:S(2)}, u32[]{:S(2)}) collective-permute-start(bf16[32,5120]{1,0:T(8,128)(2,1)} %g0.1), channel_id=1, source_target_pairs={{0,1},{1,0},{2,3},{3,2},{4,5},{5,4},{6,7},{7,6},{8,9},{9,8},{10,11... | collective-permute-start | bytes 983048 | tf_op jit(solution)/shard_map/ppermute | solution.py:483
  13.2 5.7 %copy-start.4 = (bf16[32,5120]{1,0:T(8,128)(2,1)}, bf16[32,5120]{1,0:T(8,128)(2,1)S(1)}, u32[]{:S(2)}) copy-start(bf16[32,5120]{1,0:T(8,128)(2,1)S(1)} %collective-permute-done.4.g1) | copy-start | bytes 983044
  13.2 5.7 %collective-permute-start.6 = (bf16[32,5120]{1,0:T(8,128)(2,1)S(1)}, bf16[32,5120]{1,0:T(8,128)(2,1)S(1)}, u32[]{:S(2)}, u32[]{:S(2)}) collective-permute-start(bf16[32,5120]{1,0:T(8,128)(2,1)S(1)} %collective-permute-done.4.g1), channel_id=1, source_target_pairs={{0,1},{1,0},{2,3},{3,2},{4,5},{5,4},{6,7},{7,6},{8,9},{9,8},{10,11... | collective-permute-start | bytes 983048 | tf_op jit(solution)/shard_map/ppermute | solution.py:483
  13.6 18.2 %collective-permute-start.1 = (bf16[8,128,128]{2,1,0:T(8,128)(2,1)}, bf16[8,128,128]{2,1,0:T(8,128)(2,1)S(1)}, u32[]{:S(2)}, u32[]{:S(2)}) collective-permute-start(bf16[8,128,128]{2,1,0:T(8,128)(2,1)} %refs_0_.1), channel_id=1, source_target_pairs={{128,0},{192,64},{0,128},{64,192},{129,1},{193,65},{1,129},{65,193... | collective-permute-start | bytes 786440 | tf_op jit(solution)/shard_map/ppermute | solution.py:475
  16.8 15.0 %collective-permute-start = (bf16[8,128,128]{2,1,0:T(8,128)(2,1)}, bf16[8,128,128]{2,1,0:T(8,128)(2,1)S(1)}, u32[]{:S(2)}, u32[]{:S(2)}) collective-permute-start(bf16[8,128,128]{2,1,0:T(8,128)(2,1)} %refs_0_.1), channel_id=1, source_target_pairs={{64,0},{128,64},{192,128},{0,192},{65,1},{129,65},{193,129},{1,193... | collective-permute-start | bytes 786440 | tf_op jit(solution)/shard_map/ppermute | solution.py:475
  17.9 15.5 %collective-permute-start.2 = (bf16[8,128,128]{2,1,0:T(8,128)(2,1)}, bf16[8,128,128]{2,1,0:T(8,128)(2,1)S(1)}, u32[]{:S(2)}, u32[]{:S(2)}) collective-permute-start(bf16[8,128,128]{2,1,0:T(8,128)(2,1)} %refs_0_.1), channel_id=1, source_target_pairs={{192,0},{0,64},{64,128},{128,192},{193,1},{1,65},{65,129},{129,193... | collective-permute-start | bytes 786440 | tf_op jit(solution)/shard_map/ppermute | solution.py:475
  28.1 24.1 %collective-permute-start.9 = (bf16[8,128,128]{2,1,0:T(8,128)(2,1)}, bf16[8,128,128]{2,1,0:T(8,128)(2,1)S(1)}, u32[]{:S(2)}, u32[]{:S(2)}) collective-permute-start(bf16[8,128,128]{2,1,0:T(8,128)(2,1)} %cotangent.1.c0), channel_id=1, source_target_pairs={{192,0},{0,64},{64,128},{128,192},{193,1},{1,65},{65,129},{129,193... | collective-permute-start | bytes 786440 | tf_op jit(solution)/shard_map/ppermute | solution.py:475
  28.8 23.4 %collective-permute-start.8 = (bf16[8,128,128]{2,1,0:T(8,128)(2,1)}, bf16[8,128,128]{2,1,0:T(8,128)(2,1)S(1)}, u32[]{:S(2)}, u32[]{:S(2)}) collective-permute-start(bf16[8,128,128]{2,1,0:T(8,128)(2,1)} %cotangent.1.c0), channel_id=1, source_target_pairs={{128,0},{192,64},{0,128},{64,192},{129,1},{193,65},{1,129},{65,193... | collective-permute-start | bytes 786440 | tf_op jit(solution)/shard_map/ppermute | solution.py:475
  31.8 20.4 %collective-permute-start.7 = (bf16[8,128,128]{2,1,0:T(8,128)(2,1)}, bf16[8,128,128]{2,1,0:T(8,128)(2,1)S(1)}, u32[]{:S(2)}, u32[]{:S(2)}) collective-permute-start(bf16[8,128,128]{2,1,0:T(8,128)(2,1)} %cotangent.1.c0), channel_id=1, source_target_pairs={{64,0},{128,64},{192,128},{0,192},{65,1},{129,65},{193,129},{1,193... | collective-permute-start | bytes 786440 | tf_op jit(solution)/shard_map/ppermute | solution.py:475
  31.8 13.3 %collective-permute-start.3 = (bf16[8,272,128]{2,1,0:T(8,128)(2,1)S(1)}, bf16[8,272,128]{2,1,0:T(8,128)(2,1)S(1)}, u32[]{:S(2)}, u32[]{:S(2)}) collective-permute-start(bf16[8,272,128]{2,1,0:T(8,128)(2,1)S(1)} %all-to-all-done.refs_4_.refs_3_), channel_id=1, source_target_pairs={{0,4},{4,0},{1,5},{5,1},{2,6},{6,2},{3,7},{7,3},{8,12},{12,8},{9,1... | collective-permute-start | bytes 1671176 | tf_op jit(solution)/shard_map/ppermute | solution.py:483
  45.2 7.0 %copy-start = (bf16[8,128,128]{2,1,0:T(8,128)(2,1)S(1)}, bf16[8,128,128]{2,1,0:T(8,128)(2,1)}, u32[]{:S(2)}) copy-start(bf16[8,128,128]{2,1,0:T(8,128)(2,1)} %cotangent.1.c0) | copy-start | bytes 786436
  52.9 6.4 %collective-permute-start.12 = (f32[16,512]{1,0:T(8,128)S(1)}, f32[16,512]{1,0:T(8,128)S(1)}, u32[]{:S(2)}, u32[]{:S(2)}) collective-permute-start(f32[16,512]{1,0:T(8,128)S(1)} %get-tuple-element.38.refs_6_), channel_id=1, source_target_pairs={{192,0},{0,64},{64,128},{128,192},{193,1},{1,65},{65,129},{129,193... | collective-permute-start | bytes 98312 | tf_op jit(solution)/shard_map/ppermute | solution.py:475
  54.6 5.6 %collective-permute-start.11 = (f32[16,512]{1,0:T(8,128)S(1)}, f32[16,512]{1,0:T(8,128)S(1)}, u32[]{:S(2)}, u32[]{:S(2)}) collective-permute-start(f32[16,512]{1,0:T(8,128)S(1)} %get-tuple-element.38.refs_6_), channel_id=1, source_target_pairs={{128,0},{192,64},{0,128},{64,192},{129,1},{193,65},{1,129},{65,193... | collective-permute-start | bytes 98312 | tf_op jit(solution)/shard_map/ppermute | solution.py:475
  58.0 3.9 %collective-permute-start.10 = (f32[16,512]{1,0:T(8,128)S(1)}, f32[16,512]{1,0:T(8,128)S(1)}, u32[]{:S(2)}, u32[]{:S(2)}) collective-permute-start(f32[16,512]{1,0:T(8,128)S(1)} %get-tuple-element.38.refs_6_), channel_id=1, source_target_pairs={{64,0},{128,64},{192,128},{0,192},{65,1},{129,65},{193,129},{1,193... | collective-permute-start | bytes 98312 | tf_op jit(solution)/shard_map/ppermute | solution.py:475
  71.0 11.9 %collective-permute-start.16 = (bf16[8,272,128]{2,1,0:T(8,128)(2,1)S(1)}, bf16[8,272,128]{2,1,0:T(8,128)(2,1)S(1)}, u32[]{:S(2)}, u32[]{:S(2)}) collective-permute-start(bf16[8,272,128]{2,1,0:T(8,128)(2,1)S(1)} %get-tuple-element.47), channel_id=1, source_target_pairs={{0,4},{4,0},{1,5},{5,1},{2,6},{6,2},{3,7},{7,3},{8,12},{12,8},{9,1... | collective-permute-start | bytes 1671176 | tf_op jit(solution)/shard_map/ppermute | solution.py:483
  83.8 22.0 %copy-start.3 = (f32[1,128]{1,0:T(1,128)S(1)}, f32[1,128]{1,0:T(1,128)}, u32[]{:S(2)}) copy-start(f32[1,128]{1,0:T(1,128)} %logit_ref.1) | copy-start | bytes 1540
  83.8 21.9 %all-to-all-start.1 = ((bf16[8,272,128]{2,1,0:T(8,128)(2,1)}), bf16[8,272,128]{2,1,0:T(8,128)(2,1)S(1)}, u32[]{:S(2)}, u32[]{:S(2)}) async-start(bf16[8,272,128]{2,1,0:T(8,128)(2,1)} %add_convert_fusion), calls=%async_computation.1 | async-start | bytes 1114112 | tf_op jit(solution)/shard_map/all_to_all | solution.py:512
  91.4 10.7 %collective-permute-start.13 = (bf16[8,128,128]{2,1,0:T(8,128)(2,1)S(1)}, bf16[8,128,128]{2,1,0:T(8,128)(2,1)S(1)}, u32[]{:S(2)}, u32[]{:S(2)}) collective-permute-start(bf16[8,128,128]{2,1,0:T(8,128)(2,1)S(1)} %get-tuple-element.43), channel_id=1, source_target_pairs={{192,0},{0,64},{64,128},{128,192},{193,1},{1,65},{65,129},{129,193... | collective-permute-start | bytes 786440 | tf_op jit(solution)/shard_map/ppermute | solution.py:475
  92.3 9.8 %collective-permute-start.14 = (bf16[8,128,128]{2,1,0:T(8,128)(2,1)S(1)}, bf16[8,128,128]{2,1,0:T(8,128)(2,1)S(1)}, u32[]{:S(2)}, u32[]{:S(2)}) collective-permute-start(bf16[8,128,128]{2,1,0:T(8,128)(2,1)S(1)} %get-tuple-element.44), channel_id=1, source_target_pairs={{128,0},{192,64},{0,128},{64,192},{129,1},{193,65},{1,129},{65,193... | collective-permute-start | bytes 786440 | tf_op jit(solution)/shard_map/ppermute | solution.py:475
  93.8 8.9 %collective-permute-start.15 = (bf16[8,128,128]{2,1,0:T(8,128)(2,1)S(1)}, bf16[8,128,128]{2,1,0:T(8,128)(2,1)S(1)}, u32[]{:S(2)}, u32[]{:S(2)}) collective-permute-start(bf16[8,128,128]{2,1,0:T(8,128)(2,1)S(1)} %get-tuple-element.45), channel_id=1, source_target_pairs={{64,0},{128,64},{192,128},{0,192},{65,1},{129,65},{193,129},{1,193... | collective-permute-start | bytes 786440 | tf_op jit(solution)/shard_map/ppermute | solution.py:475
  (2 other events, 1.5 us)

commit v2 on v1

--- a/solution.py
+++ b/solution.py
@@ -33,7 +33,8 @@
 SKIP = 64
 HIDDEN = 1000
 
-QBLOCK_AT, SEEN_AT, SLOT_AT, POS_AT = 0, 1, 3, 5
+QBLOCK_AT, SEEN_AT, SLOT_AT, POS_AT, FAR_AT = 0, 1, 3, 5, 7
+FAR = (WINDOW + 2 * HALF - 2) // HALF
 
 NT = (((1,), (1,)), ((), ()))
 NN = (((1,), (0,)), ((), ()))
@@ -61,6 +62,8 @@
         x = xl if col == 0 else 1 - xl
         here = ((lane >> 4) == y) & ((lane & 1) == x)
         columns[SEEN_AT + col] = picked(here & (low <= q_block), 1.0) + picked(here & (high <= q_block), 1.0)
+        far = q_block - FAR
+        columns[FAR_AT + col] = picked(here & (low <= far), 1.0) + picked(here & (high <= far), 1.0)
         k_low = picked(here & (((lane >> 1) & (NZ - 1)) == sub), low)
         columns[SLOT_AT + col] = picked(here & (low < k_low), 1.0)
         rank = picked(k_low < low, 1.0, axis=0)
@@ -69,8 +72,11 @@
     return sum(jnp.where(at == n, value, 0.0) for n, value in columns.items()).astype(i32)
 
 
-def pack_kernel(where, k_ref, v_ref, logit_ref, blocks_ref, out_ref, plan_ref):
+def plan_kernel(where, blocks_ref, plan_ref):
     plan_ref[...] = plan_of(blocks_ref[...], *where())
+
+
+def pack_kernel(k_ref, v_ref, logit_ref, out_ref):
     logit = logit_ref[...]
     penalty = jnp.maximum(logit, 0.0) + jnp.log(1.0 + jnp.exp(-jnp.abs(logit)))
     upper = penalty.astype(bf16).astype(f32)
@@ -82,16 +88,14 @@
 
 
 def cotangent_kernel(where, g0, g1, g2, g3, w_ref, out_ref, rows):
-    @pl.when(pl.program_id(0) == 0)
-    def _():
-        xh, core = where()
-        pieces = ((xh, core, g0), (1 - xh, core, g1), (xh, 1 - core, g2), (1 - xh, 1 - core, g3))
-        for a, b, ref in pieces:
-            rows[pl.ds(pl.multiple_of((a * 2 + b) * 32, 32), 32), :] = ref[...]
-
-    cot = dot(rows[...], w_ref[...], NT).astype(bf16)
-    for i in range(2):
-        out_ref[i] = cot[:, i * HD : (i + 1) * HD]
+    xh, core = where()
+    pieces = ((xh, core, g0), (1 - xh, core, g1), (xh, 1 - core, g2), (1 - xh, 1 - core, g3))
+    for a, b, ref in pieces:
+        rows[pl.ds(pl.multiple_of((a * 2 + b) * 32, 32), 32), :] = ref[...]
+    for i in range(0, HEADS, 2):
+        cot = dot(rows[...], w_ref[i * HD : (i + 2) * HD, :], NT).astype(bf16)
+        out_ref[i] = cot[:, :HD]
+        out_ref[i + 1] = cot[:, HD:]
 
 
 def sort_keys(plan_ref, col, kv_ref, ks, vs, pen=None):
@@ -120,15 +124,21 @@
         pos[n] = low
         pos[SLOTS - 1 - n] = BLOCKS - 1 - low
     count = jnp.int32(0)
+    far = [plan_ref[rh, FAR_AT + col] // STEP for rh in range(QB)]
+    for rh in range(QB):
+        for c in range(PER_BLOCK):
+            steps[count] = rh * PER_BLOCK + c
+            count = count + (c < far[rh]).astype(i32)
+    plain = count
     for rh in range(QB):
         groups = (plan_ref[rh, SEEN_AT + col] + STEP - 1) // STEP
         for c in range(PER_BLOCK):
             steps[count] = rh * PER_BLOCK + c
-            count = count + (c < groups).astype(i32)
+            count = count + ((c >= far[rh]) & (c < groups)).astype(i32)
     last = steps[count - 1]
     for i in range(3):
         steps[count + i] = last + SKIP
-    return count
+    return plain, count
 
 
 def step_of(steps, t):
@@ -170,7 +180,7 @@
     else:
         (qt, kv_ref, o_ref, st_ref, peaks, exps), refs = refs[:6], refs[6:]
     ks, vs, vt, pen, s_a, s_b, f_a, f_b, pos, steps = refs
-    count = list_steps(plan_ref, col, pos, steps)
+    plain, count = list_steps(plan_ref, col, pos, steps)
     if col == 0:
         load_rows(rows_in, qs)
         for rh in range(QB):
@@ -188,7 +198,7 @@
         _, rh, _, at = step_of(steps, t)
         s_ref[...] = dot(ks[at, :], qt[rh], NN)
 
-    def soften(t, s_ref, f_ref):
+    def soften(t, s_ref, f_ref, masked):
         v, rh, c, _ = step_of(steps, t)
         limits = thresholds(plan_ref, pos, v, rh, c)
         offset = offsets()
@@ -196,8 +206,12 @@
             parts = []
             for i, (seen, late) in enumerate(limits):
                 s = s_ref[i * HALF : (i + 1) * HALF, lanes] * SCALE
-                s = s - jnp.where(offset >= late, pen[block_rows(c, i), :], 0.0)
-                parts.append(jnp.where(offset >= seen, s, LOWEST))
+                penalty = pen[block_rows(c, i), :]
+                if masked:
+                    s = s - jnp.where(offset >= late, penalty, 0.0)
+                    parts.append(jnp.where(offset >= seen, s, LOWEST))
+                else:
+                    parts.append(s - penalty)
             peak = st_ref[rh, 0:1, lanes]
             tops = functools.reduce(jnp.maximum, parts)
             new_peak = jnp.maximum(peak, jnp.max(tops, axis=0, keepdims=True))
@@ -217,18 +231,19 @@
 
     score(0, s_a)
 
-    def pair(i, _):
+    def pair(masked, i, _):
         t = 2 * i
         attend(jnp.maximum(t - 1, 0), f_b)
         score(t + 1, s_b)
-        soften(t, s_a, f_a)
+        soften(t, s_a, f_a, masked)
         attend(t, f_a)
         score(t + 2, s_a)
-        soften(t + 1, s_b, f_b)
+        soften(t + 1, s_b, f_b, masked)
         return 0
 
     pairs = (count + 1) // 2
-    lax.fori_loop(0, pairs, pair, 0)
+    lax.fori_loop(0, plain // 2, functools.partial(pair, False), 0)
+    lax.fori_loop(plain // 2, pairs, functools.partial(pair, True), 0)
     attend(2 * pairs - 1, f_b)
 
 
@@ -272,7 +287,7 @@
         (dq_before,), dq_out, (dkv_ref,), refs = refs[:1], refs[1:5], refs[5:6], refs[6:]
         (dq, turned, sems), refs = refs[:3], refs[3:]
     ks, vs, kt, dk, dv, dl, stats, p_a, p_b, d_a, d_b, pos, steps = refs
-    count = list_steps(plan_ref, col, pos, steps)
+    plain, count = list_steps(plan_ref, col, pos, steps)
     sort_keys(plan_ref, col, kv_ref, ks, vs)
     turn(ks, kt)
     for ref in (dk, dv, dl, p_b, d_b):
@@ -280,26 +295,30 @@
     dq[...] = jnp.zeros_like(dq) if col == 1 else dq_before[...]
     merge_stats(pieces, stats)
 
-    def differ(t, p_ref, d_ref):
+    def differ(t, p_ref, d_ref, masked):
         v, rh, c, _ = step_of(steps, t)
         offset = offsets()
+        limits = thresholds(plan_ref, pos, v, rh, c)
         shares = [jnp.exp(peaks[t, 0:1, lanes] - stats[rh, 0:1, lanes]) for lanes in TILES]
-        for i, (_, late) in enumerate(thresholds(plan_ref, pos, v, rh, c)):
-            at = block_rows(c, i)
-            rows = slice(i * HALF, (i + 1) * HALF)
-            delayed = offset >= late
-            late_sum = dl[at, :]
+        for first in range(0, STEP, 2):
+            blocks = (first, first + 1)
+            late_sums = [dl[block_rows(c, i), :] for i in blocks]
+            at = pl.ds(pl.multiple_of(c * CK + first * HALF, SHARD), 2 * HALF)
             for wide in WIDE_TILES:
                 grad = dot(vs[at, :], ct[rh, :, wide], NN)
-                for j in range(WIDE // SHARD):
-                    here = slice(j * SHARD, (j + 1) * SHARD)
-                    lanes = slice(wide.start + here.start, wide.start + here.stop)
-                    p = exps[t, rows, lanes].astype(f32) * shares[lanes.start // SHARD]
-                    d = p * (grad[:, here] - stats[rh, 1:2, lanes])
-                    late_sum = late_sum + jnp.where(delayed, d, 0.0)
-                    p_ref[rows, lanes] = p.astype(bf16)
-                    d_ref[rows, lanes] = d.astype(bf16)
-            dl[at, :] = late_sum
+                for n, i in enumerate(blocks):
+                    rows = slice(i * HALF, (i + 1) * HALF)
+                    for j in range(WIDE // SHARD):
+                        here = slice(j * SHARD, (j + 1) * SHARD)
+                        lanes = slice(wide.start + here.start, wide.start + here.stop)
+                        p = exps[t, rows, lanes].astype(f32) * shares[lanes.start // SHARD]
+                        d = p * (grad[n * HALF : (n + 1) * HALF, here] - stats[rh, 1:2, lanes])
+                        late = jnp.where(offset >= limits[i][1], d, 0.0) if masked else d
+                        late_sums[n] = late_sums[n] + late
+                        p_ref[rows, lanes] = p.astype(bf16)
+                        d_ref[rows, lanes] = d.astype(bf16)
+            for n, i in enumerate(blocks):
+                dl[block_rows(c, i), :] = late_sums[n]
 
     def gather(t, p_ref, d_ref):
         _, rh, c, at = step_of(steps, t)
@@ -307,16 +326,17 @@
         dv[at, :] += dot(p_ref[...], cs[rh], NN)
         dq[rh] += dot(turned_piece(kt, c), d_ref[...], NN)
 
-    def pair(i, _):
+    def pair(masked, i, _):
         t = 2 * i
         gather(jnp.maximum(t - 1, 0), p_b, d_b)
-        differ(t, p_a, d_a)
+        differ(t, p_a, d_a, masked)
         gather(t, p_a, d_a)
-        differ(t + 1, p_b, d_b)
+        differ(t + 1, p_b, d_b, masked)
         return 0
 
     pairs = (count + 1) // 2
-    lax.fori_loop(0, pairs, pair, 0)
+    lax.fori_loop(0, plain // 2, functools.partial(pair, False), 0)
+    lax.fori_loop(plain // 2, pairs, functools.partial(pair, True), 0)
     gather(2 * pairs - 1, p_b, d_b)
     copies = []
     if col == 0:
@@ -341,6 +361,15 @@
         copy.wait()
 
 
+def total_kernel(parts_ref, logit_ref, dk_ref, dv_ref, dl_ref):
+    total = parts_ref[0].astype(f32)
+    for n in range(1, NZ):
+        total = total + parts_ref[n].astype(f32)
+    dk_ref[0] = total[:SHARD]
+    dv_ref[0] = total[SHARD : 2 * SHARD]
+    dl_ref[...] = -jax.nn.sigmoid(logit_ref[...]) * total[2 * SHARD : 2 * SHARD + 1]
+
+
 VMEM = pl.BlockSpec(memory_space=pltpu.VMEM)
 SMEM = pl.BlockSpec(memory_space=pltpu.SMEM)
 HBM = pl.BlockSpec(memory_space=pltpu.HBM)
@@ -351,7 +380,6 @@
 
 
 MOST = 5 * NA
-ROOMY = grant(54)
 KEYS = SLOTS * HALF
 shaped = jax.ShapeDtypeStruct
 
@@ -360,27 +388,37 @@
     return pl.CostEstimate(flops=int(us * 1e9), bytes_accessed=2**20, transcendentals=0)
 
 
-def run_pack(where, keys, values, logits, block_order):
+def run_plan(where, block_order):
     return pl.pallas_call(
-        functools.partial(pack_kernel, where),
-        out_shape=(shaped((NZ, KV_ROWS, HD), bf16), shaped((8, SHARD), i32)),
-        in_specs=[VMEM] * 4,
-        out_specs=(VMEM, VMEM),
+        functools.partial(plan_kernel, where),
+        out_shape=shaped((8, SHARD), i32),
+        in_specs=[VMEM],
+        out_specs=VMEM,
+        compiler_params=grant(4),
+        cost_estimate=cost(12),
+        name="plan",
+    )(block_order.T)
+
+
+def run_pack(keys, values, logits):
+    return pl.pallas_call(
+        pack_kernel,
+        out_shape=shaped((NZ, KV_ROWS, HD), bf16),
+        in_specs=[VMEM] * 3,
+        out_specs=VMEM,
+        compiler_params=grant(4),
         name="pack",
-    )(keys, values, logits, block_order.T)
+    )(keys, values, logits)
 
 
 def run_cotangent(where, pieces, w_out):
-    rows, width = w_out.shape
     return pl.pallas_call(
         functools.partial(cotangent_kernel, where),
         out_shape=shaped((HEADS, SHARD, HD), bf16),
-        grid=(HEADS // 2,),
-        in_specs=[pl.BlockSpec((32, width), lambda i: (0, 0))] * 4
-        + [pl.BlockSpec((2 * HD, width), lambda i: (i, 0))],
-        out_specs=pl.BlockSpec((2, SHARD, HD), lambda i: (i, 0, 0)),
-        scratch_shapes=[pltpu.VMEM((SHARD, width), bf16)],
-        compiler_params=ROOMY,
+        in_specs=[VMEM] * 5,
+        out_specs=VMEM,
+        scratch_shapes=[pltpu.VMEM((SHARD, w_out.shape[1]), bf16)],
+        compiler_params=grant(8),
         cost_estimate=cost(5),
         name="cotangent",
     )(*pieces, w_out)
@@ -471,6 +509,17 @@
     )(plan, *rows, kv, *exps, *stats, *more)
 
 
+def run_total(parts, logits):
+    return pl.pallas_call(
+        total_kernel,
+        out_shape=(shaped((1, SHARD, HD), f32), shaped((1, SHARD, HD), f32), shaped((1, SHARD), f32)),
+        in_specs=[VMEM] * 2,
+        out_specs=(VMEM,) * 3,
+        compiler_params=grant(4),
+        name="total",
+    )(parts, logits)
+
+
 def from_y(x, r):
     return lax.ppermute(x, "y", [((i + r) % NA, i) for i in range(NA)])
 
@@ -492,8 +541,9 @@
 
 
 def per_device(queries, keys, values, evict_logits, block_order, grad_y, w_out):
-    packed, plan = run_pack(place, keys, values, evict_logits, block_order)
-    kv = lax.all_to_all(packed, "z", 0, 0, tiled=True)
+    plan = run_plan(place, block_order)
+    keys, plan = lax.optimization_barrier((keys, plan))
+    kv = lax.all_to_all(run_pack(keys, values, evict_logits), "z", 0, 0, tiled=True)
     over = swap(grad_y, "xh")
     pieces = (grad_y, over, swap(grad_y, "core"), swap(over, "core"))
     q_all = gather_y(queries)
@@ -509,17 +559,12 @@
     dkv_here = swap(dkv_other, "xl")
     *dq, dkv = run_backward(0, plan, rows, kv, exps0, stats, dq_sum)
     dkv = (dkv + dkv_here.astype(f32)).astype(bf16)
-    dkv = jnp.sum(lax.all_to_all(dkv, "z", 0, 0, tiled=True).astype(f32), axis=0)
+    dkv = lax.all_to_all(dkv, "z", 0, 0, tiled=True)
+    key_grad, value_grad, logit_grad = run_total(dkv, evict_logits)
     query_grad = dq[0].astype(f32)
     for r in range(1, NA):
         query_grad = query_grad + from_y(dq[r], NA - r).astype(f32)
-    logit_grad = -jax.nn.sigmoid(evict_logits[0]) * dkv[2 * SHARD]
-    return (
-        query_grad.astype(bf16),
-        dkv[None, :SHARD],
-        dkv[None, SHARD : 2 * SHARD],
-        logit_grad[None],
-    )
+    return query_grad.astype(bf16), key_grad, value_grad, logit_grad
 
 
 def solution(mesh):

time: 108 us -> 108 us (level)
  Pallas kernels: 45.2 us -> 40.3 us
  waiting for transfers between devices: 16.1 us -> 20.5 us
  local copies, waits for them, and re-layouts: 2.13 us -> 5.24 us
  starting transfers between devices: 40.4 us -> 39 us
    pallas_call x1, Pallas kernels: 7.74 us -> 3.58 us  [run_cotangent(): pl.pallas_call(functools.partial(cotangent_kernel, where), out_shape=shap...]
    unnamed x14, local copies, waits for them, and re-layouts: 1.48 us -> 5.24 us
    ppermute x5, waiting for transfers between devices: 3.85 us -> 5.74 us  [swap(): return lax.ppermute(x, axis, [(0, 1), (1, 0)])]
    ppermute x12, waiting for transfers between devices: 10.2 us -> 11.9 us  [from_y(): return lax.ppermute(x, 'y', [((i + r) % NA, i) for i in range(NA)])]
  transfers between devices with their start and end apart: 19 -> 19, of which waited for: 6 -> 7; matrix products, arithmetic and copies ran while one was open for 1% -> 1% of each run, Pallas kernels for 33% -> 27%
where the time goes in v2:
time: 108 us
  Pallas kernels  40.3 us (37%)
  starting transfers between devices  39 us (36%)
  waiting for transfers between devices  20.5 us (19%)
  local copies, waits for them, and re-layouts  5.24 us (5%)
  other arithmetic  1.77 us (2%)
    pallas_call x2, Pallas kernels, run_backward(): pl.pallas_call(functools.partial(backward_kernel, col), out_shape=out_sha...  19.9 us
    ppermute x12, starting transfers between devices, from_y(): return lax.ppermute(x, 'y', [((i + r) % NA, i) for i in range(NA)])  18.1 us
    pallas_call x2, Pallas kernels, run_forward(): pl.pallas_call(functools.partial(forward_kernel, col), out_shape=out_shap...  14.2 us
    ppermute x12, waiting for transfers between devices, from_y(): return lax.ppermute(x, 'y', [((i + r) % NA, i) for i in range(NA)])  11.9 us
    all_to_all x1, starting transfers between devices, per_device(): lax.all_to_all(run_pack(keys, values, evict_logits), 'z', 0, 0, tiled=True)  8.47 us
    all_to_all x1, starting transfers between devices, per_device(): dkv = lax.all_to_all(dkv, 'z', 0, 0, tiled=True)  6.63 us
    ppermute x5, starting transfers between devices, swap(): return lax.ppermute(x, axis, [(0, 1), (1, 0)])  5.85 us
    ppermute x5, waiting for transfers between devices, swap(): return lax.ppermute(x, axis, [(0, 1), (1, 0)])  5.74 us
  transfers between devices with their start and end apart: 19, of which 7 were waited for; matrix products, arithmetic and copies ran while one was open for 1% of the time, Pallas kernels for 27%

profile of v2, /device:TPU:2, one launch (start us, length us, event | category | flops | bytes accessed | tf_op | source)
XLA Modules:
  0.0 107.6 jit_solution(4684519487544463408)
XLA Ops:
  0.6 2.2 %collective-permute-start.4 = (bf16[32,5120]{1,0:T(8,128)(2,1)}, bf16[32,5120]{1,0:T(8,128)(2,1)S(1)}, u32[]{:S(2)}, u32[]{:S(2)}) collective-permute-start(bf16[32,5120]{1,0:T(8,128)(2,1)} %g0.1), channel_id=1, source_target_pairs={{0,2},{2,0},{1,3},{3,1},{4,6},{6,4},{5,7},{7,5},{8,10},{10,8},{9,1... | collective-permute-start | bytes 983048 | tf_op jit(solution)/shard_map/ppermute | solution.py:532
  5.2 8.5 %all-to-all-start = ((bf16[8,272,128]{2,1,0:T(8,128)(2,1)}), bf16[8,272,128]{2,1,0:T(8,128)(2,1)S(1)}, u32[]{:S(2)}, u32[]{:S(2)}) async-start(bf16[8,272,128]{2,1,0:T(8,128)(2,1)} %pack.1), calls=%async_computation | async-start | bytes 1114112 | tf_op jit(solution)/shard_map/all_to_all | solution.py:546
  14.3 3.2 %collective-permute-start.1 = (bf16[8,128,128]{2,1,0:T(8,128)(2,1)S(1)}, bf16[8,128,128]{2,1,0:T(8,128)(2,1)S(1)}, u32[]{:S(2)}, u32[]{:S(2)}) collective-permute-start(bf16[8,128,128]{2,1,0:T(8,128)(2,1)S(1)} %copy-done.5), channel_id=1, source_target_pairs={{128,0},{192,64},{0,128},{64,192},{129,1},{193,65},{1,129},{65,193... | collective-permute-start | bytes 786440 | tf_op jit(solution)/shard_map/ppermute | solution.py:524
  17.5 1.1 collective-permute-start
  18.5 1.0 collective-permute-start.2
  19.5 4.0 %copy-done.3 = bf16[1024,5120]{1,0:T(8,128)(2,1)S(1)} copy-done((bf16[1024,5120]{1,0:T(8,128)(2,1)S(1)}, bf16[1024,5120]{1,0:T(8,128)(2,1)}, u32[]{:S(2)}) %copy-start.3) | copy-done | bytes 10485784
  23.5 3.6 %cotangent.1.c0 = bf16[8,128,128]{2,1,0:T(8,128)(2,1)S(1)} custom-call(bf16[32,5120]{1,0:T(8,128)(2,1)S(1)} %copy-done.4, bf16[32,5120]{1,0:T(8,128)(2,1)S(1)} %collective-permute-done.4.g1, bf16[32,5120]{1,0:T(8,128)(2,1)S(1)} %collective-permute-done.5.g2, bf16[32,5120]{1,0:T(8,128)(2,1)S(1)} %collective-permute-done.6.g3, bf16[1024,5120]{1,0:T(8,128)(2,1)S(1)} %copy-done.3), custom_call_target="tpu_custom_call" | custom-call | flops 5000000000 | bytes 1048576 | tf_op jit(solution)/shard_map/cotangent/pallas_call | solution.py:415
  27.8 3.1 %collective-permute-start.8 = (bf16[8,128,128]{2,1,0:T(8,128)(2,1)S(1)}, bf16[8,128,128]{2,1,0:T(8,128)(2,1)S(1)}, u32[]{:S(2)}, u32[]{:S(2)}) collective-permute-start(bf16[8,128,128]{2,1,0:T(8,128)(2,1)S(1)} %cotangent.1.c0), channel_id=1, source_target_pairs={{128,0},{192,64},{0,128},{64,192},{129,1},{193,65},{1,129},{65,193... | collective-permute-start | bytes 786440 | tf_op jit(solution)/shard_map/ppermute | solution.py:524
  31.6 1.4 %collective-permute-start.3 = (bf16[8,272,128]{2,1,0:T(8,128)(2,1)S(1)}, bf16[8,272,128]{2,1,0:T(8,128)(2,1)S(1)}, u32[]{:S(2)}, u32[]{:S(2)}) collective-permute-start(bf16[8,272,128]{2,1,0:T(8,128)(2,1)S(1)} %all-to-all-done.refs_4_.refs_3_), channel_id=1, source_target_pairs={{0,4},{4,0},{1,5},{5,1},{2,6},{6,2},{3,7},{7,3},{8,12},{12,8},{9,1... | collective-permute-start | bytes 1671176 | tf_op jit(solution)/shard_map/ppermute | solution.py:532
  33.0 6.9 %forward0.1 = (f32[8,128,512]{2,1,0:T(8,128)S(1)}, f32[8,2,512]{2,1,0:T(2,128)S(1)}, f32[20,1,512]{2,1,0:T(1,128)S(1)}, bf16[20,256,512]{2,1,0:T(8,128)(2,1)S(1)...) custom-call(s32[8,128]{1,0:T(8,128)S(1)} %plan.1.plan_ref, bf16[8,128,128]{2,1,0:T(8,128)(2,1)S(1)} %copy-done.5, ...), custom_call_target="tpu_custom_call" | custom-call | flops 10000000000 | bytes 1048576 | tf_op jit(solution)/shard_map/forward0/pallas_call | solution.py:436
  39.9 5.7 %collective-permute-done.3.refs_1_.refs_3_ = bf16[8,272,128]{2,1,0:T(8,128)(2,1)S(1)} collective-permute-done((bf16[8,272,128]{2,1,0:T(8,128)(2,1)S(1)}, bf16[8,272,128]{2,1,0:T(8,128)(2,1)S(1)}, u32[]{:S(2)}, u32[]{:S(2)}) %collective-permute-start.3) | collective-permute-done | bytes 557088 | tf_op jit(solution)/shard_map/ppermute | solution.py:532
  45.6 7.3 %forward1.1 = (f32[8,128,512]{2,1,0:T(8,128)S(1)}, f32[8,2,512]{2,1,0:T(2,128)S(1)}, f32[20,1,512]{2,1,0:T(1,128)S(1)}, bf16[20,256,512]{2,1,0:T(8,128)(2,1)S(1)}) custom-call(s32[8,128]{1,0:T(8,128)S(1)} %plan.1.plan_ref, bf16[8,128,512]{2,1,0:T(8,128)(2,1)S(1)} %get-tuple-element.34.refs_0_, bf16[8,272,128]{2,1,0:T(8,128)(2,1)S(1)} %collective-permute-done.3.refs_1_.refs_3_), custom_call_target="tpu_custom_call" | custom-call | flops 10000000000 | bytes 1048576 | tf_op jit(solution)/shard_map/forward1/pallas_call | solution.py:436
  53.8 1.7 %collective-permute-start.12 = (f32[16,512]{1,0:T(8,128)S(1)}, f32[16,512]{1,0:T(8,128)S(1)}, u32[]{:S(2)}, u32[]{:S(2)}) collective-permute-start(f32[16,512]{1,0:T(8,128)S(1)} %get-tuple-element.41.refs_6_), channel_id=1, source_target_pairs={{192,0},{0,64},{64,128},{128,192},{193,1},{1,65},{65,129},{129,193... | collective-permute-start | bytes 98312 | tf_op jit(solution)/shard_map/ppermute | solution.py:524
  55.4 2.9 %collective-permute-start.11 = (f32[16,512]{1,0:T(8,128)S(1)}, f32[16,512]{1,0:T(8,128)S(1)}, u32[]{:S(2)}, u32[]{:S(2)}) collective-permute-start(f32[16,512]{1,0:T(8,128)S(1)} %get-tuple-element.41.refs_6_), channel_id=1, source_target_pairs={{128,0},{192,64},{0,128},{64,192},{129,1},{193,65},{1,129},{65,193... | collective-permute-start | bytes 98312 | tf_op jit(solution)/shard_map/ppermute | solution.py:524
  59.0 1.9 %collective-permute-done.11.refs_8_ = f32[16,512]{1,0:T(8,128)S(1)} collective-permute-done((f32[16,512]{1,0:T(8,128)S(1)}, f32[16,512]{1,0:T(8,128)S(1)}, u32[]{:S(2)}, u32[]{:S(2)}) %collective-permute-start.11) | collective-permute-done | bytes 32800 | tf_op jit(solution)/shard_map/ppermute | solution.py:524
  60.9 1.4 %collective-permute-done.10.refs_7_ = f32[16,512]{1,0:T(8,128)S(1)} collective-permute-done((f32[16,512]{1,0:T(8,128)S(1)}, f32[16,512]{1,0:T(8,128)S(1)}, u32[]{:S(2)}, u32[]{:S(2)}) %collective-permute-start.10) | collective-permute-done | bytes 32800 | tf_op jit(solution)/shard_map/ppermute | solution.py:524
  62.3 9.8 %backward1.1 = (f32[8,128,512]{2,1,0:T(8,128)S(1)}, bf16[8,272,128]{2,1,0:T(8,128)(2,1)S(1)}) custom-call(s32[8,128]{1,0:T(8,128)S(1)} %plan.1.plan_ref, bf16[8,512,128]{2,1,0:T(8,128)(2,1)S(1)} %get-tuple-element.31.refs_0_, bf16[8,512,128]{2,1,0:T(8,128)(2,1)S(1)} %get-tuple-element.37.refs_1_, bf16[8,128,512]{2,1,0:T(8,128)(2,1)S(1)} %get-tuple-element.38.refs_2_, ...), custom_call_target="tpu_custom_call" | custom-call | flops 15000000512 | bytes 1048576 | tf_op jit(solution)/shard_map/backward1/pallas_call | solution.py:489
  72.1 1.6 %collective-permute-start.16 = (bf16[8,272,128]{2,1,0:T(8,128)(2,1)S(1)}, bf16[8,272,128]{2,1,0:T(8,128)(2,1)S(1)}, u32[]{:S(2)}, u32[]{:S(2)}) collective-permute-start(bf16[8,272,128]{2,1,0:T(8,128)(2,1)S(1)} %get-tuple-element.50), channel_id=1, source_target_pairs={{0,4},{4,0},{1,5},{5,1},{2,6},{6,2},{3,7},{7,3},{8,12},{12,8},{9,1... | collective-permute-start | bytes 1671176 | tf_op jit(solution)/shard_map/ppermute | solution.py:532
  73.7 10.1 %backward0.1 = (bf16[8,128,128]{2,1,0:T(8,128)(2,1)S(1)}, bf16[8,128,128]{2,1,0:T(8,128)(2,1)S(1)}, bf16[8,128,128]{2,1,0:T(8,128)(2,1)S(1)}, bf16[8,128,128]{2,1,0:T(8,128)(2,1)S(1)}, f32[8,272,128]{2,1,0:T(8,128)S(1)}) custom-call(s32[8,128]{1,0:T(8,128)S(1)} %plan.1.plan_ref, bf16[8,512,128]{2,1,0:T(8,128)(2,1)S(1)} %get-tuple-element.31.refs_0_, ...), custom_call_target="tpu_custom_call" | custom-call | flops 15000000512 | bytes 1048576 | tf_op jit(solution)/shard_map/backward0/pallas_call | solution.py:489
  84.8 6.6 %all-to-all-start.1 = ((bf16[8,272,128]{2,1,0:T(8,128)(2,1)}), bf16[8,272,128]{2,1,0:T(8,128)(2,1)S(1)}, u32[]{:S(2)}, u32[]{:S(2)}) async-start(bf16[8,272,128]{2,1,0:T(8,128)(2,1)} %add_convert_fusion), calls=%async_computation.1 | async-start | bytes 1114112 | tf_op jit(solution)/shard_map/all_to_all | solution.py:562
  91.4 2.4 %collective-permute-start.14 = (bf16[8,128,128]{2,1,0:T(8,128)(2,1)S(1)}, bf16[8,128,128]{2,1,0:T(8,128)(2,1)S(1)}, u32[]{:S(2)}, u32[]{:S(2)}) collective-permute-start(bf16[8,128,128]{2,1,0:T(8,128)(2,1)S(1)} %get-tuple-element.47), channel_id=1, source_target_pairs={{128,0},{192,64},{0,128},{64,192},{129,1},{193,65},{1,129},{65,193... | collective-permute-start | bytes 786440 | tf_op jit(solution)/shard_map/ppermute | solution.py:524
  93.8 1.5 %collective-permute-start.15 = (bf16[8,128,128]{2,1,0:T(8,128)(2,1)S(1)}, bf16[8,128,128]{2,1,0:T(8,128)(2,1)S(1)}, u32[]{:S(2)}, u32[]{:S(2)}) collective-permute-start(bf16[8,128,128]{2,1,0:T(8,128)(2,1)S(1)} %get-tuple-element.48), channel_id=1, source_target_pairs={{64,0},{128,64},{192,128},{0,192},{65,1},{129,65},{193,129},{1,193... | collective-permute-start | bytes 786440 | tf_op jit(solution)/shard_map/ppermute | solution.py:524
  95.3 8.0 %collective-permute-done.13 = bf16[8,128,128]{2,1,0:T(8,128)(2,1)S(1)} collective-permute-done((bf16[8,128,128]{2,1,0:T(8,128)(2,1)S(1)}, bf16[8,128,128]{2,1,0:T(8,128)(2,1)S(1)}, u32[]{:S(2)}, u32[]{:S(2)}) %collective-permute-start.13) | collective-permute-done | bytes 262176 | tf_op jit(solution)/shard_map/ppermute | solution.py:524
  104.8 2.1 %all-to-all-done.1.parts_ref = bf16[8,272,128]{2,1,0:T(8,128)(2,1)S(1)} async-done(((bf16[8,272,128]{2,1,0:T(8,128)(2,1)}), bf16[8,272,128]{2,1,0:T(8,128)(2,1)S(1)}, u32[]{:S(2)}, u32[]{:S(2)}) %all-to-all-start.1) | async-done | bytes 557088 | tf_op jit(solution)/shard_map/all_to_all | solution.py:562
  (39 shorter events, 8.9 us)
Async XLA Ops:
  0.6 13.1 %collective-permute-start.4 = (bf16[32,5120]{1,0:T(8,128)(2,1)}, bf16[32,5120]{1,0:T(8,128)(2,1)S(1)}, u32[]{:S(2)}, u32[]{:S(2)}) collective-permute-start(bf16[32,5120]{1,0:T(8,128)(2,1)} %g0.1), channel_id=1, source_target_pairs={{0,2},{2,0},{1,3},{3,1},{4,6},{6,4},{5,7},{7,5},{8,10},{10,8},{9,1... | collective-permute-start | bytes 983048 | tf_op jit(solution)/shard_map/ppermute | solution.py:532
  3.5 0.8 copy-start.1
  3.5 0.8 copy-start.2
  3.5 10.1 %copy-start.4 = (bf16[32,5120]{1,0:T(8,128)(2,1)S(1)}, bf16[32,5120]{1,0:T(8,128)(2,1)}, u32[]{:S(2)}) copy-start(bf16[32,5120]{1,0:T(8,128)(2,1)} %g0.1) | copy-start | bytes 983044
  3.5 10.7 %copy-start.5 = (bf16[8,128,128]{2,1,0:T(8,128)(2,1)S(1)}, bf16[8,128,128]{2,1,0:T(8,128)(2,1)}, u32[]{:S(2)}) copy-start(bf16[8,128,128]{2,1,0:T(8,128)(2,1)} %refs_0_.1) | copy-start | bytes 786436
  5.2 26.4 %all-to-all-start = ((bf16[8,272,128]{2,1,0:T(8,128)(2,1)}), bf16[8,272,128]{2,1,0:T(8,128)(2,1)S(1)}, u32[]{:S(2)}, u32[]{:S(2)}) async-start(bf16[8,272,128]{2,1,0:T(8,128)(2,1)} %pack.1), calls=%async_computation | async-start | bytes 1114112 | tf_op jit(solution)/shard_map/all_to_all | solution.py:546
  13.7 5.8 %collective-permute-start.5 = (bf16[32,5120]{1,0:T(8,128)(2,1)S(1)}, bf16[32,5120]{1,0:T(8,128)(2,1)S(1)}, u32[]{:S(2)}, u32[]{:S(2)}) collective-permute-start(bf16[32,5120]{1,0:T(8,128)(2,1)S(1)} %copy-done.4), channel_id=1, source_target_pairs={{0,1},{1,0},{2,3},{3,2},{4,5},{5,4},{6,7},{7,6},{8,9},{9,8},{10,11... | collective-permute-start | bytes 983048 | tf_op jit(solution)/shard_map/ppermute | solution.py:532
  13.8 5.7 %collective-permute-start.6 = (bf16[32,5120]{1,0:T(8,128)(2,1)S(1)}, bf16[32,5120]{1,0:T(8,128)(2,1)S(1)}, u32[]{:S(2)}, u32[]{:S(2)}) collective-permute-start(bf16[32,5120]{1,0:T(8,128)(2,1)S(1)} %collective-permute-done.4.g1), channel_id=1, source_target_pairs={{0,1},{1,0},{2,3},{3,2},{4,5},{5,4},{6,7},{7,6},{8,9},{9,8},{10,11... | collective-permute-start | bytes 983048 | tf_op jit(solution)/shard_map/ppermute | solution.py:532
  14.3 16.6 %collective-permute-start.1 = (bf16[8,128,128]{2,1,0:T(8,128)(2,1)S(1)}, bf16[8,128,128]{2,1,0:T(8,128)(2,1)S(1)}, u32[]{:S(2)}, u32[]{:S(2)}) collective-permute-start(bf16[8,128,128]{2,1,0:T(8,128)(2,1)S(1)} %copy-done.5), channel_id=1, source_target_pairs={{128,0},{192,64},{0,128},{64,192},{129,1},{193,65},{1,129},{65,193... | collective-permute-start | bytes 786440 | tf_op jit(solution)/shard_map/ppermute | solution.py:524
  17.5 13.4 %collective-permute-start = (bf16[8,128,128]{2,1,0:T(8,128)(2,1)S(1)}, bf16[8,128,128]{2,1,0:T(8,128)(2,1)S(1)}, u32[]{:S(2)}, u32[]{:S(2)}) collective-permute-start(bf16[8,128,128]{2,1,0:T(8,128)(2,1)S(1)} %copy-done.5), channel_id=1, source_target_pairs={{64,0},{128,64},{192,128},{0,192},{65,1},{129,65},{193,129},{1,193... | collective-permute-start | bytes 786440 | tf_op jit(solution)/shard_map/ppermute | solution.py:524
  18.5 14.5 %collective-permute-start.2 = (bf16[8,128,128]{2,1,0:T(8,128)(2,1)S(1)}, bf16[8,128,128]{2,1,0:T(8,128)(2,1)S(1)}, u32[]{:S(2)}, u32[]{:S(2)}) collective-permute-start(bf16[8,128,128]{2,1,0:T(8,128)(2,1)S(1)} %copy-done.5), channel_id=1, source_target_pairs={{192,0},{0,64},{64,128},{128,192},{193,1},{1,65},{65,129},{129,193... | collective-permute-start | bytes 786440 | tf_op jit(solution)/shard_map/ppermute | solution.py:524
  19.5 4.0 %copy-start.3 = (bf16[1024,5120]{1,0:T(8,128)(2,1)S(1)}, bf16[1024,5120]{1,0:T(8,128)(2,1)}, u32[]{:S(2)}) copy-start(bf16[1024,5120]{1,0:T(8,128)(2,1)} %w_ref.1) | copy-start | bytes 31457284
  27.1 25.9 %collective-permute-start.9 = (bf16[8,128,128]{2,1,0:T(8,128)(2,1)S(1)}, bf16[8,128,128]{2,1,0:T(8,128)(2,1)S(1)}, u32[]{:S(2)}, u32[]{:S(2)}) collective-permute-start(bf16[8,128,128]{2,1,0:T(8,128)(2,1)S(1)} %cotangent.1.c0), channel_id=1, source_target_pairs={{192,0},{0,64},{64,128},{128,192},{193,1},{1,65},{65,129},{129,193... | collective-permute-start | bytes 786440 | tf_op jit(solution)/shard_map/ppermute | solution.py:524
  27.8 25.2 %collective-permute-start.8 = (bf16[8,128,128]{2,1,0:T(8,128)(2,1)S(1)}, bf16[8,128,128]{2,1,0:T(8,128)(2,1)S(1)}, u32[]{:S(2)}, u32[]{:S(2)}) collective-permute-start(bf16[8,128,128]{2,1,0:T(8,128)(2,1)S(1)} %cotangent.1.c0), channel_id=1, source_target_pairs={{128,0},{192,64},{0,128},{64,192},{129,1},{193,65},{1,129},{65,193... | collective-permute-start | bytes 786440 | tf_op jit(solution)/shard_map/ppermute | solution.py:524
  30.9 22.1 %collective-permute-start.7 = (bf16[8,128,128]{2,1,0:T(8,128)(2,1)S(1)}, bf16[8,128,128]{2,1,0:T(8,128)(2,1)S(1)}, u32[]{:S(2)}, u32[]{:S(2)}) collective-permute-start(bf16[8,128,128]{2,1,0:T(8,128)(2,1)S(1)} %cotangent.1.c0), channel_id=1, source_target_pairs={{64,0},{128,64},{192,128},{0,192},{65,1},{129,65},{193,129},{1,193... | collective-permute-start | bytes 786440 | tf_op jit(solution)/shard_map/ppermute | solution.py:524
  31.6 14.1 %collective-permute-start.3 = (bf16[8,272,128]{2,1,0:T(8,128)(2,1)S(1)}, bf16[8,272,128]{2,1,0:T(8,128)(2,1)S(1)}, u32[]{:S(2)}, u32[]{:S(2)}) collective-permute-start(bf16[8,272,128]{2,1,0:T(8,128)(2,1)S(1)} %all-to-all-done.refs_4_.refs_3_), channel_id=1, source_target_pairs={{0,4},{4,0},{1,5},{5,1},{2,6},{6,2},{3,7},{7,3},{8,12},{12,8},{9,1... | collective-permute-start | bytes 1671176 | tf_op jit(solution)/shard_map/ppermute | solution.py:532
  53.8 5.2 %collective-permute-start.12 = (f32[16,512]{1,0:T(8,128)S(1)}, f32[16,512]{1,0:T(8,128)S(1)}, u32[]{:S(2)}, u32[]{:S(2)}) collective-permute-start(f32[16,512]{1,0:T(8,128)S(1)} %get-tuple-element.41.refs_6_), channel_id=1, source_target_pairs={{192,0},{0,64},{64,128},{128,192},{193,1},{1,65},{65,129},{129,193... | collective-permute-start | bytes 98312 | tf_op jit(solution)/shard_map/ppermute | solution.py:524
  55.4 5.4 %collective-permute-start.11 = (f32[16,512]{1,0:T(8,128)S(1)}, f32[16,512]{1,0:T(8,128)S(1)}, u32[]{:S(2)}, u32[]{:S(2)}) collective-permute-start(f32[16,512]{1,0:T(8,128)S(1)} %get-tuple-element.41.refs_6_), channel_id=1, source_target_pairs={{128,0},{192,64},{0,128},{64,192},{129,1},{193,65},{1,129},{65,193... | collective-permute-start | bytes 98312 | tf_op jit(solution)/shard_map/ppermute | solution.py:524
  58.3 3.9 %collective-permute-start.10 = (f32[16,512]{1,0:T(8,128)S(1)}, f32[16,512]{1,0:T(8,128)S(1)}, u32[]{:S(2)}, u32[]{:S(2)}) collective-permute-start(f32[16,512]{1,0:T(8,128)S(1)} %get-tuple-element.41.refs_6_), channel_id=1, source_target_pairs={{64,0},{128,64},{192,128},{0,192},{65,1},{129,65},{193,129},{1,193... | collective-permute-start | bytes 98312 | tf_op jit(solution)/shard_map/ppermute | solution.py:524
  72.1 11.7 %collective-permute-start.16 = (bf16[8,272,128]{2,1,0:T(8,128)(2,1)S(1)}, bf16[8,272,128]{2,1,0:T(8,128)(2,1)S(1)}, u32[]{:S(2)}, u32[]{:S(2)}) collective-permute-start(bf16[8,272,128]{2,1,0:T(8,128)(2,1)S(1)} %get-tuple-element.50), channel_id=1, source_target_pairs={{0,4},{4,0},{1,5},{5,1},{2,6},{6,2},{3,7},{7,3},{8,12},{12,8},{9,1... | collective-permute-start | bytes 1671176 | tf_op jit(solution)/shard_map/ppermute | solution.py:532
  84.8 22.1 %all-to-all-start.1 = ((bf16[8,272,128]{2,1,0:T(8,128)(2,1)}), bf16[8,272,128]{2,1,0:T(8,128)(2,1)S(1)}, u32[]{:S(2)}, u32[]{:S(2)}) async-start(bf16[8,272,128]{2,1,0:T(8,128)(2,1)} %add_convert_fusion), calls=%async_computation.1 | async-start | bytes 1114112 | tf_op jit(solution)/shard_map/all_to_all | solution.py:562
  91.4 11.9 %collective-permute-start.13 = (bf16[8,128,128]{2,1,0:T(8,128)(2,1)S(1)}, bf16[8,128,128]{2,1,0:T(8,128)(2,1)S(1)}, u32[]{:S(2)}, u32[]{:S(2)}) collective-permute-start(bf16[8,128,128]{2,1,0:T(8,128)(2,1)S(1)} %get-tuple-element.46), channel_id=1, source_target_pairs={{192,0},{0,64},{64,128},{128,192},{193,1},{1,65},{65,129},{129,193... | collective-permute-start | bytes 786440 | tf_op jit(solution)/shard_map/ppermute | solution.py:524
  91.4 11.9 %collective-permute-start.14 = (bf16[8,128,128]{2,1,0:T(8,128)(2,1)S(1)}, bf16[8,128,128]{2,1,0:T(8,128)(2,1)S(1)}, u32[]{:S(2)}, u32[]{:S(2)}) collective-permute-start(bf16[8,128,128]{2,1,0:T(8,128)(2,1)S(1)} %get-tuple-element.47), channel_id=1, source_target_pairs={{128,0},{192,64},{0,128},{64,192},{129,1},{193,65},{1,129},{65,193... | collective-permute-start | bytes 786440 | tf_op jit(solution)/shard_map/ppermute | solution.py:524
  93.8 10.1 %collective-permute-start.15 = (bf16[8,128,128]{2,1,0:T(8,128)(2,1)S(1)}, bf16[8,128,128]{2,1,0:T(8,128)(2,1)S(1)}, u32[]{:S(2)}, u32[]{:S(2)}) collective-permute-start(bf16[8,128,128]{2,1,0:T(8,128)(2,1)S(1)} %get-tuple-element.48), channel_id=1, source_target_pairs={{64,0},{128,64},{192,128},{0,192},{65,1},{129,65},{193,129},{1,193... | collective-permute-start | bytes 786440 | tf_op jit(solution)/shard_map/ppermute | solution.py:524
  (2 other events, 1.4 us)

commit v3 on v2

--- a/solution.py
+++ b/solution.py
@@ -24,17 +24,17 @@
 QB = 2 * NA
 KV_ROWS = 2 * SHARD + 16
 
-STEP = 4
-CK = STEP * HALF
-PER_BLOCK = SLOTS // STEP
+FULL, PART = 4, 2
+CK = FULL * HALF
+PER_BLOCK = SLOTS // FULL
+UNITS = SLOTS // PART
 TILES = [slice(j * SHARD, (j + 1) * SHARD) for j in range(ROWS // SHARD)]
 WIDE = 256
 WIDE_TILES = [slice(j * WIDE, (j + 1) * WIDE) for j in range(ROWS // WIDE)]
 SKIP = 64
 HIDDEN = 1000
 
-QBLOCK_AT, SEEN_AT, SLOT_AT, POS_AT, FAR_AT = 0, 1, 3, 5, 7
-FAR = (WINDOW + 2 * HALF - 2) // HALF
+QBLOCK_AT, SEEN_AT, SLOT_AT, POS_AT = 0, 1, 3, 5
 
 NT = (((1,), (1,)), ((), ()))
 NN = (((1,), (0,)), ((), ()))
@@ -62,8 +62,6 @@
         x = xl if col == 0 else 1 - xl
         here = ((lane >> 4) == y) & ((lane & 1) == x)
         columns[SEEN_AT + col] = picked(here & (low <= q_block), 1.0) + picked(here & (high <= q_block), 1.0)
-        far = q_block - FAR
-        columns[FAR_AT + col] = picked(here & (low <= far), 1.0) + picked(here & (high <= far), 1.0)
         k_low = picked(here & (((lane >> 1) & (NZ - 1)) == sub), low)
         columns[SLOT_AT + col] = picked(here & (low < k_low), 1.0)
         rank = picked(k_low < low, 1.0, axis=0)
@@ -72,11 +70,8 @@
     return sum(jnp.where(at == n, value, 0.0) for n, value in columns.items()).astype(i32)
 
 
-def plan_kernel(where, blocks_ref, plan_ref):
+def pack_kernel(where, k_ref, v_ref, logit_ref, blocks_ref, out_ref, plan_ref):
     plan_ref[...] = plan_of(blocks_ref[...], *where())
-
-
-def pack_kernel(k_ref, v_ref, logit_ref, out_ref):
     logit = logit_ref[...]
     penalty = jnp.maximum(logit, 0.0) + jnp.log(1.0 + jnp.exp(-jnp.abs(logit)))
     upper = penalty.astype(bf16).astype(f32)
@@ -87,15 +82,25 @@
         out_ref[j, 2 * SHARD :, :] = tail
 
 
-def cotangent_kernel(where, g0, g1, g2, g3, w_ref, out_ref, rows):
+def cotangent_kernel(where, g0, g1, g2, g3, w_hbm, out_ref, rows, w_all, sems):
+    def fetch(h):
+        here = slice(h * HD, (h + 1) * HD)
+        return pltpu.make_async_copy(w_hbm.at[here, :], w_all.at[here, :], sems.at[h])
+
+    for h in range(3):
+        fetch(h).start()
     xh, core = where()
     pieces = ((xh, core, g0), (1 - xh, core, g1), (xh, 1 - core, g2), (1 - xh, 1 - core, g3))
     for a, b, ref in pieces:
         rows[pl.ds(pl.multiple_of((a * 2 + b) * 32, 32), 32), :] = ref[...]
-    for i in range(0, HEADS, 2):
-        cot = dot(rows[...], w_ref[i * HD : (i + 2) * HD, :], NT).astype(bf16)
-        out_ref[i] = cot[:, :HD]
-        out_ref[i + 1] = cot[:, HD:]
+    for h in range(HEADS):
+        fetch(h).wait()
+        if h + 3 < HEADS:
+            fetch(h + 3).start()
+        if h % 2 == 1:
+            cot = dot(rows[...], w_all[(h - 1) * HD : (h + 1) * HD, :], NT).astype(bf16)
+            out_ref[h - 1] = cot[:, :HD]
+            out_ref[h] = cot[:, HD:]
 
 
 def sort_keys(plan_ref, col, kv_ref, ks, vs, pen=None):
@@ -118,39 +123,52 @@
         dest[i] = src[i * SHARD : (i + 1) * SHARD, :].astype(f32).T.astype(bf16)
 
 
-def list_steps(plan_ref, col, pos, steps):
+def list_steps(plan_ref, col, pos, steps, parts):
     for n in range(NZ):
         low = plan_ref[n, POS_AT + col]
         pos[n] = low
         pos[SLOTS - 1 - n] = BLOCKS - 1 - low
-    count = jnp.int32(0)
-    far = [plan_ref[rh, FAR_AT + col] // STEP for rh in range(QB)]
+    n_full = jnp.int32(0)
+    n_part = jnp.int32(2)
     for rh in range(QB):
+        units = (plan_ref[rh, SEEN_AT + col] + PART - 1) // PART
+        groups = units // 2
         for c in range(PER_BLOCK):
-            steps[count] = rh * PER_BLOCK + c
-            count = count + (c < far[rh]).astype(i32)
-    plain = count
-    for rh in range(QB):
-        groups = (plan_ref[rh, SEEN_AT + col] + STEP - 1) // STEP
-        for c in range(PER_BLOCK):
-            steps[count] = rh * PER_BLOCK + c
-            count = count + ((c >= far[rh]) & (c < groups)).astype(i32)
-    last = steps[count - 1]
-    for i in range(3):
-        steps[count + i] = last + SKIP
-    return plain, count
-
-
-def step_of(steps, t):
-    v = steps[t]
-    rh = (v // PER_BLOCK) % QB
-    c = v % PER_BLOCK
-    return v, rh, c, pl.ds(pl.multiple_of(c * CK, CK), CK)
-
-
-def thresholds(plan_ref, pos, v, rh, c):
+            steps[n_full] = rh * PER_BLOCK + c
+            n_full = n_full + (c < groups).astype(i32)
+        parts[n_part] = rh * UNITS + units - 1
+        n_part = n_part + (units - 2 * groups)
+    last = steps[n_full - 1]
+    unit = (last // PER_BLOCK) * UNITS + 2 * (last % PER_BLOCK)
+    parts[0] = unit
+    parts[1] = unit + 1
+    odd = lax.rem(n_full, 2)
+    n_full = n_full - odd
+    from_part = 2 - 2 * odd
+    parts[n_part] = parts[n_part - 1] + SKIP
+    for i in range(2):
+        steps[n_full + i] = last
+        parts[n_part + 1 + i] = parts[n_part]
+    n_part = n_part - from_part
+    return n_full, n_part + lax.rem(n_part, 2), from_part
+
+
+def step_of(lists, size, t):
+    steps, parts, n_full, from_part = lists
+    if size == FULL:
+        v = steps[t]
+        return v, (v // PER_BLOCK) % QB, (v % PER_BLOCK) * FULL, 2 * t
+    v = parts[from_part + t]
+    return v, (v // UNITS) % QB, (v % UNITS) * PART, 2 * n_full + t
+
+
+def rows_at(first, size):
+    return pl.ds(pl.multiple_of(first * HALF, SHARD), size * HALF)
+
+
+def thresholds(plan_ref, pos, v, rh, first, size):
     q_block = plan_ref[rh, QBLOCK_AT]
-    ahead = [(q_block - pos[c * STEP + i]) * HALF for i in range(STEP)]
+    ahead = [(q_block - pos[first + i]) * HALF for i in range(size)]
     return [(jnp.where(v >= SKIP, HIDDEN, -d), WINDOW - d) for d in ahead]
 
 
@@ -159,13 +177,13 @@
     return lax.broadcasted_iota(i32, shape, 1) % HALF - lax.broadcasted_iota(i32, shape, 0)
 
 
-def block_rows(c, i):
-    return pl.ds(pl.multiple_of(c * CK + i * HALF, HALF), HALF)
-
-
-def turned_piece(ref, c):
-    n = CK // SHARD
-    return jnp.concatenate([ref[c * n + i] for i in range(n)], axis=1)
+def block_rows(first, i):
+    return pl.ds(pl.multiple_of((first + i) * HALF, HALF), HALF)
+
+
+def turned_piece(ref, first, size):
+    n = size // PART
+    return jnp.concatenate([ref[first // PART + i] for i in range(n)], axis=1)
 
 
 def load_rows(refs, dest):
@@ -179,8 +197,9 @@
         rows_in, (kv_ref, o_ref, st_ref, peaks, exps, qs, qt), refs = refs[:4], refs[4:11], refs[11:]
     else:
         (qt, kv_ref, o_ref, st_ref, peaks, exps), refs = refs[:6], refs[6:]
-    ks, vs, vt, pen, s_a, s_b, f_a, f_b, pos, steps = refs
-    plain, count = list_steps(plan_ref, col, pos, steps)
+    ks, vs, vt, pen, s_a, s_b, f_a, f_b, pos, steps, parts = refs
+    n_full, n_part, from_part = list_steps(plan_ref, col, pos, steps, parts)
+    lists = (steps, parts, n_full, from_part)
     if col == 0:
         load_rows(rows_in, qs)
         for rh in range(QB):
@@ -191,60 +210,63 @@
     for rh in range(QB):
         st_ref[rh, 0:1, :] = jnp.full((1, ROWS), LOWEST, f32)
         st_ref[rh, 1:2, :] = jnp.zeros((1, ROWS), f32)
-    exps[0] = jnp.zeros_like(exps[0])
-    f_b[...] = jnp.ones_like(f_b)
-
-    def score(t, s_ref):
-        _, rh, _, at = step_of(steps, t)
-        s_ref[...] = dot(ks[at, :], qt[rh], NN)
-
-    def soften(t, s_ref, f_ref, masked):
-        v, rh, c, _ = step_of(steps, t)
-        limits = thresholds(plan_ref, pos, v, rh, c)
+    def score(size, t, s_ref):
+        _, rh, first, _ = step_of(lists, size, t)
+        s_ref[: size * HALF, :] = dot(ks[rows_at(first, size), :], qt[rh], NN)
+
+    def soften(size, t, s_ref, f_ref):
+        v, rh, first, unit = step_of(lists, size, t)
+        limits = thresholds(plan_ref, pos, v, rh, first, size)
         offset = offsets()
         for lanes in TILES:
-            parts = []
+            tiles = []
             for i, (seen, late) in enumerate(limits):
                 s = s_ref[i * HALF : (i + 1) * HALF, lanes] * SCALE
-                penalty = pen[block_rows(c, i), :]
-                if masked:
-                    s = s - jnp.where(offset >= late, penalty, 0.0)
-                    parts.append(jnp.where(offset >= seen, s, LOWEST))
-                else:
-                    parts.append(s - penalty)
+                s = s - jnp.where(offset >= late, pen[block_rows(first, i), :], 0.0)
+                tiles.append(jnp.where(offset >= seen, s, LOWEST))
             peak = st_ref[rh, 0:1, lanes]
-            tops = functools.reduce(jnp.maximum, parts)
+            tops = functools.reduce(jnp.maximum, tiles)
             new_peak = jnp.maximum(peak, jnp.max(tops, axis=0, keepdims=True))
             factor = jnp.exp(peak - new_peak)
-            parts = [jnp.exp(s - new_peak) for s in parts]
-            total = jnp.sum(sum(parts), axis=0, keepdims=True)
-            for i, p in enumerate(parts):
-                exps[t, i * HALF : (i + 1) * HALF, lanes] = p.astype(bf16)
+            tiles = [jnp.exp(s - new_peak) for s in tiles]
+            total = jnp.sum(sum(tiles), axis=0, keepdims=True)
+            for i, p in enumerate(tiles):
+                here = slice((i % PART) * HALF, (i % PART + 1) * HALF)
+                exps[unit + i // PART, here, lanes] = p.astype(bf16)
             f_ref[0:1, lanes] = factor
-            peaks[t, 0:1, lanes] = new_peak
+            peaks[unit, 0:1, lanes] = new_peak
             st_ref[rh, 0:1, lanes] = new_peak
             st_ref[rh, 1:2, lanes] = st_ref[rh, 1:2, lanes] * factor + total
 
-    def attend(t, f_ref):
-        _, rh, c, _ = step_of(steps, t)
-        o_ref[rh] = o_ref[rh] * f_ref[0:1, :] + dot(turned_piece(vt, c), exps[t], NN)
-
-    score(0, s_a)
-
-    def pair(masked, i, _):
-        t = 2 * i
-        attend(jnp.maximum(t - 1, 0), f_b)
-        score(t + 1, s_b)
-        soften(t, s_a, f_a, masked)
-        attend(t, f_a)
-        score(t + 2, s_a)
-        soften(t + 1, s_b, f_b, masked)
-        return 0
-
-    pairs = (count + 1) // 2
-    lax.fori_loop(0, plain // 2, functools.partial(pair, False), 0)
-    lax.fori_loop(plain // 2, pairs, functools.partial(pair, True), 0)
-    attend(2 * pairs - 1, f_b)
+    def attend(size, t, f_ref):
+        _, rh, first, unit = step_of(lists, size, t)
+        p = exps[pl.ds(unit, size // PART)].reshape(size * HALF, ROWS)
+        o_ref[rh] = o_ref[rh] * f_ref[0:1, :] + dot(turned_piece(vt, first, size), p, NN)
+
+    def run(size, count):
+        start = 0 if size == FULL else 2 * n_full
+        exps[pl.ds(start, size // PART)] = jnp.zeros((size // PART, PART * HALF, ROWS), bf16)
+        f_b[...] = jnp.ones_like(f_b)
+        score(size, 0, s_a)
+
+        def pair(i, _):
+            t = 2 * i
+            attend(size, jnp.maximum(t - 1, 0), f_b)
+            score(size, t + 1, s_b)
+            soften(size, t, s_a, f_a)
+            attend(size, t, f_a)
+            score(size, t + 2, s_a)
+            soften(size, t + 1, s_b, f_b)
+            return 0
+
+        lax.fori_loop(0, count // 2, pair, 0)
+        attend(size, count - 1, f_b)
+
+    run(FULL, n_full)
+
+    @pl.when(n_part > 0)
+    def _():
+        run(PART, n_part)
 
 
 def weigh_kernel(o0, st0, o1, st1, c0, c1, c2, c3, out_ref, cs, ct):
@@ -286,58 +308,69 @@
     else:
         (dq_before,), dq_out, (dkv_ref,), refs = refs[:1], refs[1:5], refs[5:6], refs[6:]
         (dq, turned, sems), refs = refs[:3], refs[3:]
-    ks, vs, kt, dk, dv, dl, stats, p_a, p_b, d_a, d_b, pos, steps = refs
-    plain, count = list_steps(plan_ref, col, pos, steps)
+    ks, vs, kt, dk, dv, dl, stats, p_a, p_b, d_a, d_b, pos, steps, parts = refs
+    n_full, n_part, from_part = list_steps(plan_ref, col, pos, steps, parts)
+    lists = (steps, parts, n_full, from_part)
     sort_keys(plan_ref, col, kv_ref, ks, vs)
     turn(ks, kt)
-    for ref in (dk, dv, dl, p_b, d_b):
+    for ref in (dk, dv, dl):
         ref[...] = jnp.zeros_like(ref)
     dq[...] = jnp.zeros_like(dq) if col == 1 else dq_before[...]
     merge_stats(pieces, stats)
 
-    def differ(t, p_ref, d_ref, masked):
-        v, rh, c, _ = step_of(steps, t)
+    def differ(size, t, p_ref, d_ref):
+        v, rh, first, unit = step_of(lists, size, t)
         offset = offsets()
-        limits = thresholds(plan_ref, pos, v, rh, c)
-        shares = [jnp.exp(peaks[t, 0:1, lanes] - stats[rh, 0:1, lanes]) for lanes in TILES]
-        for first in range(0, STEP, 2):
-            blocks = (first, first + 1)
-            late_sums = [dl[block_rows(c, i), :] for i in blocks]
-            at = pl.ds(pl.multiple_of(c * CK + first * HALF, SHARD), 2 * HALF)
+        limits = thresholds(plan_ref, pos, v, rh, first, size)
+        shares = [jnp.exp(peaks[unit, 0:1, lanes] - stats[rh, 0:1, lanes]) for lanes in TILES]
+        for half in range(size // PART):
+            blocks = range(half * PART, (half + 1) * PART)
+            late_sums = [dl[block_rows(first, i), :] for i in blocks]
+            at = rows_at(first + half * PART, PART)
             for wide in WIDE_TILES:
                 grad = dot(vs[at, :], ct[rh, :, wide], NN)
                 for n, i in enumerate(blocks):
                     rows = slice(i * HALF, (i + 1) * HALF)
+                    inner = slice(n * HALF, (n + 1) * HALF)
                     for j in range(WIDE // SHARD):
                         here = slice(j * SHARD, (j + 1) * SHARD)
                         lanes = slice(wide.start + here.start, wide.start + here.stop)
-                        p = exps[t, rows, lanes].astype(f32) * shares[lanes.start // SHARD]
-                        d = p * (grad[n * HALF : (n + 1) * HALF, here] - stats[rh, 1:2, lanes])
-                        late = jnp.where(offset >= limits[i][1], d, 0.0) if masked else d
-                        late_sums[n] = late_sums[n] + late
+                        p = exps[unit + half, inner, lanes].astype(f32) * shares[lanes.start // SHARD]
+                        d = p * (grad[inner, here] - stats[rh, 1:2, lanes])
+                        late_sums[n] = late_sums[n] + jnp.where(offset >= limits[i][1], d, 0.0)
                         p_ref[rows, lanes] = p.astype(bf16)
                         d_ref[rows, lanes] = d.astype(bf16)
             for n, i in enumerate(blocks):
-                dl[block_rows(c, i), :] = late_sums[n]
-
-    def gather(t, p_ref, d_ref):
-        _, rh, c, at = step_of(steps, t)
-        dk[at, :] += dot(d_ref[...], qs[rh], NN)
-        dv[at, :] += dot(p_ref[...], cs[rh], NN)
-        dq[rh] += dot(turned_piece(kt, c), d_ref[...], NN)
-
-    def pair(masked, i, _):
-        t = 2 * i
-        gather(jnp.maximum(t - 1, 0), p_b, d_b)
-        differ(t, p_a, d_a, masked)
-        gather(t, p_a, d_a)
-        differ(t + 1, p_b, d_b, masked)
-        return 0
-
-    pairs = (count + 1) // 2
-    lax.fori_loop(0, plain // 2, functools.partial(pair, False), 0)
-    lax.fori_loop(plain // 2, pairs, functools.partial(pair, True), 0)
-    gather(2 * pairs - 1, p_b, d_b)
+                dl[block_rows(first, i), :] = late_sums[n]
+
+    def gather(size, t, p_ref, d_ref):
+        _, rh, first, _ = step_of(lists, size, t)
+        at, rows = rows_at(first, size), size * HALF
+        dk[at, :] += dot(d_ref[:rows, :], qs[rh], NN)
+        dv[at, :] += dot(p_ref[:rows, :], cs[rh], NN)
+        dq[rh] += dot(turned_piece(kt, first, size), d_ref[:rows, :], NN)
+
+    def run(size, count):
+        for ref in (p_b, d_b):
+            ref[...] = jnp.zeros_like(ref)
+
+        def pair(i, _):
+            t = 2 * i
+            gather(size, jnp.maximum(t - 1, 0), p_b, d_b)
+            differ(size, t, p_a, d_a)
+            gather(size, t, p_a, d_a)
+            differ(size, t + 1, p_b, d_b)
+            return 0
+
+        lax.fori_loop(0, count // 2, pair, 0)
+        gather(size, count - 1, p_b, d_b)
+
+    run(FULL, n_full)
+
+    @pl.when(n_part > 0)
+    def _():
+        run(PART, n_part)
+
     copies = []
     if col == 0:
         for r, ref in enumerate(dq_out):
@@ -379,7 +412,7 @@
     return pltpu.CompilerParams(vmem_limit_bytes=mib * 1024 * 1024)
 
 
-MOST = 5 * NA
+MOST = 9 * NA
 KEYS = SLOTS * HALF
 shaped = jax.ShapeDtypeStruct
 
@@ -388,37 +421,28 @@
     return pl.CostEstimate(flops=int(us * 1e9), bytes_accessed=2**20, transcendentals=0)
 
 
-def run_plan(where, block_order):
+def run_pack(where, keys, values, logits, block_order):
     return pl.pallas_call(
-        functools.partial(plan_kernel, where),
-        out_shape=shaped((8, SHARD), i32),
-        in_specs=[VMEM],
-        out_specs=VMEM,
-        compiler_params=grant(4),
-        cost_estimate=cost(12),
-        name="plan",
-    )(block_order.T)
-
-
-def run_pack(keys, values, logits):
-    return pl.pallas_call(
-        pack_kernel,
-        out_shape=shaped((NZ, KV_ROWS, HD), bf16),
-        in_specs=[VMEM] * 3,
-        out_specs=VMEM,
-        compiler_params=grant(4),
+        functools.partial(pack_kernel, where),
+        out_shape=(shaped((NZ, KV_ROWS, HD), bf16), shaped((8, SHARD), i32)),
+        in_specs=[VMEM] * 4,
+        out_specs=(VMEM, VMEM),
         name="pack",
-    )(keys, values, logits)
+    )(keys, values, logits, block_order.T)
 
 
 def run_cotangent(where, pieces, w_out):
     return pl.pallas_call(
         functools.partial(cotangent_kernel, where),
         out_shape=shaped((HEADS, SHARD, HD), bf16),
-        in_specs=[VMEM] * 5,
+        in_specs=[VMEM] * 4 + [pl.BlockSpec(memory_space=pl.ANY)],
         out_specs=VMEM,
-        scratch_shapes=[pltpu.VMEM((SHARD, w_out.shape[1]), bf16)],
-        compiler_params=grant(8),
+        scratch_shapes=[
+            pltpu.VMEM((SHARD, w_out.shape[1]), bf16),
+            pltpu.VMEM(w_out.shape, bf16),
+            pltpu.SemaphoreType.DMA((HEADS,)),
+        ],
+        compiler_params=grant(52),
         cost_estimate=cost(5),
         name="cotangent",
     )(*pieces, w_out)
@@ -429,7 +453,7 @@
         shaped((QB, HD, ROWS), f32),
         shaped((QB, 2, ROWS), f32),
         shaped((MOST, 1, ROWS), f32),
-        shaped((MOST, CK, ROWS), bf16),
+        shaped((MOST, PART * HALF, ROWS), bf16),
     )
     if col == 0:
         out_shape += (shaped((QB, ROWS, HD), bf16), shaped((QB, HD, ROWS), bf16))
@@ -449,6 +473,7 @@
             pltpu.VMEM((8, ROWS), f32),
             pltpu.SMEM((SLOTS,), i32),
             pltpu.SMEM((QB * PER_BLOCK + 3,), i32),
+            pltpu.SMEM((2 + QB + 3,), i32),
         ],
         compiler_params=grant(14),
         cost_estimate=cost(10),
@@ -502,7 +527,7 @@
             pltpu.VMEM((QB, 2, ROWS), f32),
         ]
         + [pltpu.VMEM((CK, ROWS), bf16)] * 4
-        + [pltpu.SMEM((SLOTS,), i32), pltpu.SMEM((QB * PER_BLOCK + 3,), i32)],
+        + [pltpu.SMEM((SLOTS,), i32), pltpu.SMEM((QB * PER_BLOCK + 3,), i32), pltpu.SMEM((2 + QB + 3,), i32)],
         compiler_params=grant(18),
         cost_estimate=cost(15),
         name=f"backward{col}",
@@ -541,9 +566,8 @@
 
 
 def per_device(queries, keys, values, evict_logits, block_order, grad_y, w_out):
-    plan = run_plan(place, block_order)
-    keys, plan = lax.optimization_barrier((keys, plan))
-    kv = lax.all_to_all(run_pack(keys, values, evict_logits), "z", 0, 0, tiled=True)
+    packed, plan = run_pack(place, keys, values, evict_logits, block_order)
+    kv = lax.all_to_all(packed, "z", 0, 0, tiled=True)
     over = swap(grad_y, "xh")
     pieces = (grad_y, over, swap(grad_y, "core"), swap(over, "core"))
     q_all = gather_y(queries)

time: 108 us -> 108 us (level)
  Pallas kernels: 40.3 us -> 46.2 us
  local copies, waits for them, and re-layouts: 5.24 us -> 0.99 us
  waiting for transfers between devices: 20.5 us -> 16.9 us
    pallas_call x1, Pallas kernels: 3.58 us -> 7.97 us  [run_cotangent(): pl.pallas_call(functools.partial(cotangent_kernel, where), out_shape=shap...]
    unnamed x14 -> x8, local copies, waits for them, and re-layouts: 5.24 us -> 0.99 us
    ppermute x5, waiting for transfers between devices: 5.74 us -> 4.14 us  [swap(): return lax.ppermute(x, axis, [(0, 1), (1, 0)])]
    ppermute x12, starting transfers between devices: 18.1 us -> 19.4 us  [from_y(): return lax.ppermute(x, 'y', [((i + r) % NA, i) for i in range(NA)])]
    ppermute x12, waiting for transfers between devices: 11.9 us -> 10.7 us  [from_y(): return lax.ppermute(x, 'y', [((i + r) % NA, i) for i in range(NA)])]
  transfers between devices with their start and end apart: 19 -> 19, of which waited for: 7 -> 7; matrix products, arithmetic and copies ran while one was open for 1% -> 1% of each run, Pallas kernels for 27% -> 33%
where the time goes in v3:
time: 108 us; the launch traced here: 107 us
  Pallas kernels  46.2 us (43%)
  starting transfers between devices  39.9 us (37%)
  waiting for transfers between devices  16.9 us (16%)
  other arithmetic  1.77 us (2%)
    pallas_call x2, Pallas kernels, run_backward(): pl.pallas_call(functools.partial(backward_kernel, col), out_shape=out_sha...  20.1 us
    ppermute x12, starting transfers between devices, from_y(): return lax.ppermute(x, 'y', [((i + r) % NA, i) for i in range(NA)])  19.4 us
    pallas_call x2, Pallas kernels, run_forward(): pl.pallas_call(functools.partial(forward_kernel, col), out_shape=out_shap...  15.1 us
    ppermute x12, waiting for transfers between devices, from_y(): return lax.ppermute(x, 'y', [((i + r) % NA, i) for i in range(NA)])  10.7 us
    all_to_all x1, starting transfers between devices, per_device(): kv = lax.all_to_all(packed, 'z', 0, 0, tiled=True)  8.6 us
    pallas_call x1, Pallas kernels, run_cotangent(): pl.pallas_call(functools.partial(cotangent_kernel, where), out_shape=shap...  7.97 us
    ppermute x5, starting transfers between devices, swap(): return lax.ppermute(x, axis, [(0, 1), (1, 0)])  5.96 us
    all_to_all x1, starting transfers between devices, per_device(): dkv = lax.all_to_all(dkv, 'z', 0, 0, tiled=True)  5.92 us
  transfers between devices with their start and end apart: 19, of which 7 were waited for; matrix products, arithmetic and copies ran while one was open for 1% of the time, Pallas kernels for 33%

profile of v3, /device:TPU:2, one launch (start us, length us, event | category | flops | bytes accessed | tf_op | source)
XLA Modules:
  0.0 106.5 jit_solution(576529830138015339)
XLA Ops:
  0.6 2.2 %collective-permute-start.4 = (bf16[32,5120]{1,0:T(8,128)(2,1)}, bf16[32,5120]{1,0:T(8,128)(2,1)S(1)}, u32[]{:S(2)}, u32[]{:S(2)}) collective-permute-start(bf16[32,5120]{1,0:T(8,128)(2,1)} %g0.1), channel_id=1, source_target_pairs={{0,2},{2,0},{1,3},{3,1},{4,6},{6,4},{5,7},{7,5},{8,10},{10,8},{9,1... | collective-permute-start | bytes 983048 | tf_op jit(solution)/shard_map/ppermute | solution.py:557
  2.8 1.7 %pack.1 = (bf16[8,272,128]{2,1,0:T(8,128)(2,1)}, s32[8,128]{1,0:T(8,128)}) custom-call(bf16[1,128,128]{2,1,0:T(8,128)(2,1)} %k_ref.1, bf16[1,128,128]{2,1,0:T(8,128)(2,1)} %v_ref.1, f32[1,128]{1,0:T(1,128)} %logit_ref.3, s32[2,64]{1,0:T(2,128)} %bitcast.1), custom_call_target="tpu_custom_call" | custom-call | tf_op jit(solution)/shard_map/pack/pallas_call | solution.py:425
  4.6 8.6 %all-to-all-start = ((bf16[8,272,128]{2,1,0:T(8,128)(2,1)}), bf16[8,272,128]{2,1,0:T(8,128)(2,1)S(1)}, u32[]{:S(2)}, u32[]{:S(2)}) async-start(bf16[8,272,128]{2,1,0:T(8,128)(2,1)} %get-tuple-element.30), calls=%async_computation | async-start | bytes 1114112 | tf_op jit(solution)/shard_map/all_to_all | solution.py:570
  13.7 3.2 %collective-permute-start.1 = (bf16[8,128,128]{2,1,0:T(8,128)(2,1)}, bf16[8,128,128]{2,1,0:T(8,128)(2,1)S(1)}, u32[]{:S(2)}, u32[]{:S(2)}) collective-permute-start(bf16[8,128,128]{2,1,0:T(8,128)(2,1)} %refs_0_.1), channel_id=1, source_target_pairs={{128,0},{192,64},{0,128},{64,192},{129,1},{193,65},{1,129},{65,193... | collective-permute-start | bytes 786440 | tf_op jit(solution)/shard_map/ppermute | solution.py:549
  16.9 1.1 collective-permute-start
  17.9 1.0 collective-permute-start.2
  19.9 8.0 %cotangent.1.c0 = bf16[8,128,128]{2,1,0:T(8,128)(2,1)S(1)} custom-call(bf16[32,5120]{1,0:T(8,128)(2,1)S(1)} %copy-done.1, bf16[32,5120]{1,0:T(8,128)(2,1)S(1)} %collective-permute-done.4.g1, bf16[32,5120]{1,0:T(8,128)(2,1)S(1)} %collective-permute-done.5.g2, bf16[32,5120]{1,0:T(8,128)(2,1)S(1)} %collective-permute-done.6.g3, bf16[1024,5120]{1,0:T(8,128)(2,1)} %w_hbm.1), custom_call_target="tpu_custom_call" | custom-call | flops 5000000000 | bytes 1048576 | tf_op jit(solution)/shard_map/cotangent/pallas_call | solution.py:435
  28.6 3.0 %collective-permute-start.8 = (bf16[8,128,128]{2,1,0:T(8,128)(2,1)S(1)}, bf16[8,128,128]{2,1,0:T(8,128)(2,1)S(1)}, u32[]{:S(2)}, u32[]{:S(2)}) collective-permute-start(bf16[8,128,128]{2,1,0:T(8,128)(2,1)S(1)} %cotangent.1.c0), channel_id=1, source_target_pairs={{128,0},{192,64},{0,128},{64,192},{129,1},{193,65},{1,129},{65,193... | collective-permute-start | bytes 786440 | tf_op jit(solution)/shard_map/ppermute | solution.py:549
  31.7 1.5 %collective-permute-start.3 = (bf16[8,272,128]{2,1,0:T(8,128)(2,1)S(1)}, bf16[8,272,128]{2,1,0:T(8,128)(2,1)S(1)}, u32[]{:S(2)}, u32[]{:S(2)}) collective-permute-start(bf16[8,272,128]{2,1,0:T(8,128)(2,1)S(1)} %all-to-all-done.refs_4_.refs_3_), channel_id=1, source_target_pairs={{0,4},{4,0},{1,5},{5,1},{2,6},{6,2},{3,7},{7,3},{8,12},{12,8},{9,1... | collective-permute-start | bytes 1671176 | tf_op jit(solution)/shard_map/ppermute | solution.py:557
  33.2 7.8 %forward0.1 = (f32[8,128,512]{2,1,0:T(8,128)S(1)}, f32[8,2,512]{2,1,0:T(2,128)S(1)}, f32[36,1,512]{2,1,0:T(1,128)S(1)}, bf16[36,128,512]{2,1,0:T(8,128)(2,1)S(1)...) custom-call(s32[8,128]{1,0:T(8,128)S(1)} %copy-done.3, bf16[8,128,128]{2,1,0:T(8,128)(2,1)S(1)} %copy-done.2, ...), custom_call_target="tpu_custom_call" | custom-call | flops 10000000000 | bytes 1048576 | tf_op jit(solution)/shard_map/forward0/pallas_call | solution.py:460
  41.0 4.1 %collective-permute-done.3.refs_1_.refs_3_ = bf16[8,272,128]{2,1,0:T(8,128)(2,1)S(1)} collective-permute-done((bf16[8,272,128]{2,1,0:T(8,128)(2,1)S(1)}, bf16[8,272,128]{2,1,0:T(8,128)(2,1)S(1)}, u32[]{:S(2)}, u32[]{:S(2)}) %collective-permute-start.3) | collective-permute-done | bytes 557088 | tf_op jit(solution)/shard_map/ppermute | solution.py:557
  45.1 7.3 %forward1.1 = (f32[8,128,512]{2,1,0:T(8,128)S(1)}, f32[8,2,512]{2,1,0:T(2,128)S(1)}, f32[36,1,512]{2,1,0:T(1,128)S(1)}, bf16[36,128,512]{2,1,0:T(8,128)(2,1)S(1)}) custom-call(s32[8,128]{1,0:T(8,128)S(1)} %copy-done.3, bf16[8,128,512]{2,1,0:T(8,128)(2,1)S(1)} %get-tuple-element.34.refs_0_, bf16[8,272,128]{2,1,0:T(8,128)(2,1)S(1)} %collective-permute-done.3.refs_1_.refs_3_), custom_call_target="tpu_custom_call" | custom-call | flops 10000000000 | bytes 1048576 | tf_op jit(solution)/shard_map/forward1/pallas_call | solution.py:460
  53.2 1.7 %collective-permute-start.12 = (f32[16,512]{1,0:T(8,128)S(1)}, f32[16,512]{1,0:T(8,128)S(1)}, u32[]{:S(2)}, u32[]{:S(2)}) collective-permute-start(f32[16,512]{1,0:T(8,128)S(1)} %get-tuple-element.41.refs_6_), channel_id=1, source_target_pairs={{192,0},{0,64},{64,128},{128,192},{193,1},{1,65},{65,129},{129,193... | collective-permute-start | bytes 98312 | tf_op jit(solution)/shard_map/ppermute | solution.py:549
  54.8 3.3 %collective-permute-start.11 = (f32[16,512]{1,0:T(8,128)S(1)}, f32[16,512]{1,0:T(8,128)S(1)}, u32[]{:S(2)}, u32[]{:S(2)}) collective-permute-start(f32[16,512]{1,0:T(8,128)S(1)} %get-tuple-element.41.refs_6_), channel_id=1, source_target_pairs={{128,0},{192,64},{0,128},{64,192},{129,1},{193,65},{1,129},{65,193... | collective-permute-start | bytes 98312 | tf_op jit(solution)/shard_map/ppermute | solution.py:549
  59.1 1.3 %collective-permute-done.11.refs_8_ = f32[16,512]{1,0:T(8,128)S(1)} collective-permute-done((f32[16,512]{1,0:T(8,128)S(1)}, f32[16,512]{1,0:T(8,128)S(1)}, u32[]{:S(2)}, u32[]{:S(2)}) %collective-permute-start.11) | collective-permute-done | bytes 32800 | tf_op jit(solution)/shard_map/ppermute | solution.py:549
  60.4 1.7 %collective-permute-done.10.refs_7_ = f32[16,512]{1,0:T(8,128)S(1)} collective-permute-done((f32[16,512]{1,0:T(8,128)S(1)}, f32[16,512]{1,0:T(8,128)S(1)}, u32[]{:S(2)}, u32[]{:S(2)}) %collective-permute-start.10) | collective-permute-done | bytes 32800 | tf_op jit(solution)/shard_map/ppermute | solution.py:549
  62.0 9.3 %backward1.1 = (f32[8,128,512]{2,1,0:T(8,128)S(1)}, bf16[8,272,128]{2,1,0:T(8,128)(2,1)S(1)}) custom-call(s32[8,128]{1,0:T(8,128)S(1)} %copy-done.3, bf16[8,512,128]{2,1,0:T(8,128)(2,1)S(1)} %get-tuple-element.31.refs_0_, bf16[8,512,128]{2,1,0:T(8,128)(2,1)S(1)} %get-tuple-element.37.refs_1_, bf16[8,128,512]{2,1,0:T(8,128)(2,1)S(1)} %get-tuple-element.38.refs_2_, ...), custom_call_target="tpu_custom_call" | custom-call | flops 15000000512 | bytes 1048576 | tf_op jit(solution)/shard_map/backward1/pallas_call | solution.py:514
  71.3 1.7 %collective-permute-start.16 = (bf16[8,272,128]{2,1,0:T(8,128)(2,1)S(1)}, bf16[8,272,128]{2,1,0:T(8,128)(2,1)S(1)}, u32[]{:S(2)}, u32[]{:S(2)}) collective-permute-start(bf16[8,272,128]{2,1,0:T(8,128)(2,1)S(1)} %get-tuple-element.50), channel_id=1, source_target_pairs={{0,4},{4,0},{1,5},{5,1},{2,6},{6,2},{3,7},{7,3},{8,12},{12,8},{9,1... | collective-permute-start | bytes 1671176 | tf_op jit(solution)/shard_map/ppermute | solution.py:557
  73.1 10.8 %backward0.1 = (bf16[8,128,128]{2,1,0:T(8,128)(2,1)S(1)}, bf16[8,128,128]{2,1,0:T(8,128)(2,1)S(1)}, bf16[8,128,128]{2,1,0:T(8,128)(2,1)S(1)}, bf16[8,128,128]{2,1,0:T(8,128)(2,1)S(1)}, f32[8,272,128]{2,1,0:T(8,128)S(1)}) custom-call(s32[8,128]{1,0:T(8,128)S(1)} %copy-done.3, bf16[8,512,128]{2,1,0:T(8,128)(2,1)S(1)} %get-tuple-element.31.refs_0_, ...), custom_call_target="tpu_custom_call" | custom-call | flops 15000000512 | bytes 1048576 | tf_op jit(solution)/shard_map/backward0/pallas_call | solution.py:514
  84.8 5.9 %all-to-all-start.1 = ((bf16[8,272,128]{2,1,0:T(8,128)(2,1)}), bf16[8,272,128]{2,1,0:T(8,128)(2,1)S(1)}, u32[]{:S(2)}, u32[]{:S(2)}) async-start(bf16[8,272,128]{2,1,0:T(8,128)(2,1)} %add_convert_fusion), calls=%async_computation.1 | async-start | bytes 1114112 | tf_op jit(solution)/shard_map/all_to_all | solution.py:586
  90.7 4.5 %collective-permute-start.14 = (bf16[8,128,128]{2,1,0:T(8,128)(2,1)S(1)}, bf16[8,128,128]{2,1,0:T(8,128)(2,1)S(1)}, u32[]{:S(2)}, u32[]{:S(2)}) collective-permute-start(bf16[8,128,128]{2,1,0:T(8,128)(2,1)S(1)} %get-tuple-element.47), channel_id=1, source_target_pairs={{128,0},{192,64},{0,128},{64,192},{129,1},{193,65},{1,129},{65,193... | collective-permute-start | bytes 786440 | tf_op jit(solution)/shard_map/ppermute | solution.py:549
  95.2 4.6 %collective-permute-done.13 = bf16[8,128,128]{2,1,0:T(8,128)(2,1)S(1)} collective-permute-done((bf16[8,128,128]{2,1,0:T(8,128)(2,1)S(1)}, bf16[8,128,128]{2,1,0:T(8,128)(2,1)S(1)}, u32[]{:S(2)}, u32[]{:S(2)}) %collective-permute-start.13) | collective-permute-done | bytes 262176 | tf_op jit(solution)/shard_map/ppermute | solution.py:549
  99.8 2.8 %collective-permute-done.14 = bf16[8,128,128]{2,1,0:T(8,128)(2,1)S(1)} collective-permute-done((bf16[8,128,128]{2,1,0:T(8,128)(2,1)S(1)}, bf16[8,128,128]{2,1,0:T(8,128)(2,1)S(1)}, u32[]{:S(2)}, u32[]{:S(2)}) %collective-permute-start.14) | collective-permute-done | bytes 262176 | tf_op jit(solution)/shard_map/ppermute | solution.py:549
  103.7 2.1 %all-to-all-done.1.parts_ref = bf16[8,272,128]{2,1,0:T(8,128)(2,1)S(1)} async-done(((bf16[8,272,128]{2,1,0:T(8,128)(2,1)}), bf16[8,272,128]{2,1,0:T(8,128)(2,1)S(1)}, u32[]{:S(2)}, u32[]{:S(2)}) %all-to-all-start.1) | async-done | bytes 557088 | tf_op jit(solution)/shard_map/all_to_all | solution.py:586
  (32 shorter events, 6.7 us)
Async XLA Ops:
  0.6 12.5 %collective-permute-start.4 = (bf16[32,5120]{1,0:T(8,128)(2,1)}, bf16[32,5120]{1,0:T(8,128)(2,1)S(1)}, u32[]{:S(2)}, u32[]{:S(2)}) collective-permute-start(bf16[32,5120]{1,0:T(8,128)(2,1)} %g0.1), channel_id=1, source_target_pairs={{0,2},{2,0},{1,3},{3,1},{4,6},{6,4},{5,7},{7,5},{8,10},{10,8},{9,1... | collective-permute-start | bytes 983048 | tf_op jit(solution)/shard_map/ppermute | solution.py:557
  4.6 28.6 %copy-start.2 = (bf16[8,128,128]{2,1,0:T(8,128)(2,1)S(1)}, bf16[8,128,128]{2,1,0:T(8,128)(2,1)}, u32[]{:S(2)}) copy-start(bf16[8,128,128]{2,1,0:T(8,128)(2,1)} %refs_0_.1) | copy-start | bytes 786436
  4.6 28.6 %copy-start.3 = (s32[8,128]{1,0:T(8,128)S(1)}, s32[8,128]{1,0:T(8,128)}, u32[]{:S(2)}) copy-start(s32[8,128]{1,0:T(8,128)} %get-tuple-element.29.plan_ref) | copy-start | bytes 12292
  4.6 27.1 %all-to-all-start = ((bf16[8,272,128]{2,1,0:T(8,128)(2,1)}), bf16[8,272,128]{2,1,0:T(8,128)(2,1)S(1)}, u32[]{:S(2)}, u32[]{:S(2)}) async-start(bf16[8,272,128]{2,1,0:T(8,128)(2,1)} %get-tuple-element.30), calls=%async_computation | async-start | bytes 1114112 | tf_op jit(solution)/shard_map/all_to_all | solution.py:570
  13.2 5.7 %collective-permute-start.5 = (bf16[32,5120]{1,0:T(8,128)(2,1)}, bf16[32,5120]{1,0:T(8,128)(2,1)S(1)}, u32[]{:S(2)}, u32[]{:S(2)}) collective-permute-start(bf16[32,5120]{1,0:T(8,128)(2,1)} %g0.1), channel_id=1, source_target_pairs={{0,1},{1,0},{2,3},{3,2},{4,5},{5,4},{6,7},{7,6},{8,9},{9,8},{10,11... | collective-permute-start | bytes 983048 | tf_op jit(solution)/shard_map/ppermute | solution.py:557
  13.2 5.7 %collective-permute-start.6 = (bf16[32,5120]{1,0:T(8,128)(2,1)S(1)}, bf16[32,5120]{1,0:T(8,128)(2,1)S(1)}, u32[]{:S(2)}, u32[]{:S(2)}) collective-permute-start(bf16[32,5120]{1,0:T(8,128)(2,1)S(1)} %collective-permute-done.4.g1), channel_id=1, source_target_pairs={{0,1},{1,0},{2,3},{3,2},{4,5},{5,4},{6,7},{7,6},{8,9},{9,8},{10,11... | collective-permute-start | bytes 983048 | tf_op jit(solution)/shard_map/ppermute | solution.py:557
  13.7 18.0 %collective-permute-start.1 = (bf16[8,128,128]{2,1,0:T(8,128)(2,1)}, bf16[8,128,128]{2,1,0:T(8,128)(2,1)S(1)}, u32[]{:S(2)}, u32[]{:S(2)}) collective-permute-start(bf16[8,128,128]{2,1,0:T(8,128)(2,1)} %refs_0_.1), channel_id=1, source_target_pairs={{128,0},{192,64},{0,128},{64,192},{129,1},{193,65},{1,129},{65,193... | collective-permute-start | bytes 786440 | tf_op jit(solution)/shard_map/ppermute | solution.py:549
  16.9 14.8 %collective-permute-start = (bf16[8,128,128]{2,1,0:T(8,128)(2,1)}, bf16[8,128,128]{2,1,0:T(8,128)(2,1)S(1)}, u32[]{:S(2)}, u32[]{:S(2)}) collective-permute-start(bf16[8,128,128]{2,1,0:T(8,128)(2,1)} %refs_0_.1), channel_id=1, source_target_pairs={{64,0},{128,64},{192,128},{0,192},{65,1},{129,65},{193,129},{1,193... | collective-permute-start | bytes 786440 | tf_op jit(solution)/shard_map/ppermute | solution.py:549
  17.9 15.3 %collective-permute-start.2 = (bf16[8,128,128]{2,1,0:T(8,128)(2,1)}, bf16[8,128,128]{2,1,0:T(8,128)(2,1)S(1)}, u32[]{:S(2)}, u32[]{:S(2)}) collective-permute-start(bf16[8,128,128]{2,1,0:T(8,128)(2,1)} %refs_0_.1), channel_id=1, source_target_pairs={{192,0},{0,64},{64,128},{128,192},{193,1},{1,65},{65,129},{129,193... | collective-permute-start | bytes 786440 | tf_op jit(solution)/shard_map/ppermute | solution.py:549
  18.9 1.0 copy-start.1
  27.9 24.6 %collective-permute-start.9 = (bf16[8,128,128]{2,1,0:T(8,128)(2,1)S(1)}, bf16[8,128,128]{2,1,0:T(8,128)(2,1)S(1)}, u32[]{:S(2)}, u32[]{:S(2)}) collective-permute-start(bf16[8,128,128]{2,1,0:T(8,128)(2,1)S(1)} %cotangent.1.c0), channel_id=1, source_target_pairs={{192,0},{0,64},{64,128},{128,192},{193,1},{1,65},{65,129},{129,193... | collective-permute-start | bytes 786440 | tf_op jit(solution)/shard_map/ppermute | solution.py:549
  28.6 23.8 %collective-permute-start.8 = (bf16[8,128,128]{2,1,0:T(8,128)(2,1)S(1)}, bf16[8,128,128]{2,1,0:T(8,128)(2,1)S(1)}, u32[]{:S(2)}, u32[]{:S(2)}) collective-permute-start(bf16[8,128,128]{2,1,0:T(8,128)(2,1)S(1)} %cotangent.1.c0), channel_id=1, source_target_pairs={{128,0},{192,64},{0,128},{64,192},{129,1},{193,65},{1,129},{65,193... | collective-permute-start | bytes 786440 | tf_op jit(solution)/shard_map/ppermute | solution.py:549
  31.7 20.8 %collective-permute-start.7 = (bf16[8,128,128]{2,1,0:T(8,128)(2,1)S(1)}, bf16[8,128,128]{2,1,0:T(8,128)(2,1)S(1)}, u32[]{:S(2)}, u32[]{:S(2)}) collective-permute-start(bf16[8,128,128]{2,1,0:T(8,128)(2,1)S(1)} %cotangent.1.c0), channel_id=1, source_target_pairs={{64,0},{128,64},{192,128},{0,192},{65,1},{129,65},{193,129},{1,193... | collective-permute-start | bytes 786440 | tf_op jit(solution)/shard_map/ppermute | solution.py:549
  31.7 13.5 %collective-permute-start.3 = (bf16[8,272,128]{2,1,0:T(8,128)(2,1)S(1)}, bf16[8,272,128]{2,1,0:T(8,128)(2,1)S(1)}, u32[]{:S(2)}, u32[]{:S(2)}) collective-permute-start(bf16[8,272,128]{2,1,0:T(8,128)(2,1)S(1)} %all-to-all-done.refs_4_.refs_3_), channel_id=1, source_target_pairs={{0,4},{4,0},{1,5},{5,1},{2,6},{6,2},{3,7},{7,3},{8,12},{12,8},{9,1... | collective-permute-start | bytes 1671176 | tf_op jit(solution)/shard_map/ppermute | solution.py:557
  53.2 5.9 %collective-permute-start.12 = (f32[16,512]{1,0:T(8,128)S(1)}, f32[16,512]{1,0:T(8,128)S(1)}, u32[]{:S(2)}, u32[]{:S(2)}) collective-permute-start(f32[16,512]{1,0:T(8,128)S(1)} %get-tuple-element.41.refs_6_), channel_id=1, source_target_pairs={{192,0},{0,64},{64,128},{128,192},{193,1},{1,65},{65,129},{129,193... | collective-permute-start | bytes 98312 | tf_op jit(solution)/shard_map/ppermute | solution.py:549
  54.8 5.5 %collective-permute-start.11 = (f32[16,512]{1,0:T(8,128)S(1)}, f32[16,512]{1,0:T(8,128)S(1)}, u32[]{:S(2)}, u32[]{:S(2)}) collective-permute-start(f32[16,512]{1,0:T(8,128)S(1)} %get-tuple-element.41.refs_6_), channel_id=1, source_target_pairs={{128,0},{192,64},{0,128},{64,192},{129,1},{193,65},{1,129},{65,193... | collective-permute-start | bytes 98312 | tf_op jit(solution)/shard_map/ppermute | solution.py:549
  58.1 3.9 %collective-permute-start.10 = (f32[16,512]{1,0:T(8,128)S(1)}, f32[16,512]{1,0:T(8,128)S(1)}, u32[]{:S(2)}, u32[]{:S(2)}) collective-permute-start(f32[16,512]{1,0:T(8,128)S(1)} %get-tuple-element.41.refs_6_), channel_id=1, source_target_pairs={{64,0},{128,64},{192,128},{0,192},{65,1},{129,65},{193,129},{1,193... | collective-permute-start | bytes 98312 | tf_op jit(solution)/shard_map/ppermute | solution.py:549
  71.3 12.5 %collective-permute-start.16 = (bf16[8,272,128]{2,1,0:T(8,128)(2,1)S(1)}, bf16[8,272,128]{2,1,0:T(8,128)(2,1)S(1)}, u32[]{:S(2)}, u32[]{:S(2)}) collective-permute-start(bf16[8,272,128]{2,1,0:T(8,128)(2,1)S(1)} %get-tuple-element.50), channel_id=1, source_target_pairs={{0,4},{4,0},{1,5},{5,1},{2,6},{6,2},{3,7},{7,3},{8,12},{12,8},{9,1... | collective-permute-start | bytes 1671176 | tf_op jit(solution)/shard_map/ppermute | solution.py:557
  83.8 22.0 %copy-start = (f32[1,128]{1,0:T(1,128)S(1)}, f32[1,128]{1,0:T(1,128)}, u32[]{:S(2)}) copy-start(f32[1,128]{1,0:T(1,128)} %logit_ref.3) | copy-start | bytes 1540
  84.8 21.0 %all-to-all-start.1 = ((bf16[8,272,128]{2,1,0:T(8,128)(2,1)}), bf16[8,272,128]{2,1,0:T(8,128)(2,1)S(1)}, u32[]{:S(2)}, u32[]{:S(2)}) async-start(bf16[8,272,128]{2,1,0:T(8,128)(2,1)} %add_convert_fusion), calls=%async_computation.1 | async-start | bytes 1114112 | tf_op jit(solution)/shard_map/all_to_all | solution.py:586
  90.7 9.1 %collective-permute-start.13 = (bf16[8,128,128]{2,1,0:T(8,128)(2,1)S(1)}, bf16[8,128,128]{2,1,0:T(8,128)(2,1)S(1)}, u32[]{:S(2)}, u32[]{:S(2)}) collective-permute-start(bf16[8,128,128]{2,1,0:T(8,128)(2,1)S(1)} %get-tuple-element.46), channel_id=1, source_target_pairs={{192,0},{0,64},{64,128},{128,192},{193,1},{1,65},{65,129},{129,193... | collective-permute-start | bytes 786440 | tf_op jit(solution)/shard_map/ppermute | solution.py:549
  90.7 11.9 %collective-permute-start.14 = (bf16[8,128,128]{2,1,0:T(8,128)(2,1)S(1)}, bf16[8,128,128]{2,1,0:T(8,128)(2,1)S(1)}, u32[]{:S(2)}, u32[]{:S(2)}) collective-permute-start(bf16[8,128,128]{2,1,0:T(8,128)(2,1)S(1)} %get-tuple-element.47), channel_id=1, source_target_pairs={{128,0},{192,64},{0,128},{64,192},{129,1},{193,65},{1,129},{65,193... | collective-permute-start | bytes 786440 | tf_op jit(solution)/shard_map/ppermute | solution.py:549
  95.2 7.7 %collective-permute-start.15 = (bf16[8,128,128]{2,1,0:T(8,128)(2,1)S(1)}, bf16[8,128,128]{2,1,0:T(8,128)(2,1)S(1)}, u32[]{:S(2)}, u32[]{:S(2)}) collective-permute-start(bf16[8,128,128]{2,1,0:T(8,128)(2,1)S(1)} %get-tuple-element.48), channel_id=1, source_target_pairs={{64,0},{128,64},{192,128},{0,192},{65,1},{129,65},{193,129},{1,193... | collective-permute-start | bytes 786440 | tf_op jit(solution)/shard_map/ppermute | solution.py:549

commit v4 on v2

--- a/solution.py
+++ b/solution.py
@@ -30,11 +30,13 @@
 TILES = [slice(j * SHARD, (j + 1) * SHARD) for j in range(ROWS // SHARD)]
 WIDE = 256
 WIDE_TILES = [slice(j * WIDE, (j + 1) * WIDE) for j in range(ROWS // WIDE)]
+STREAMS = (0, 1)
+QS = QB // 2
+LIST = 24
 SKIP = 64
 HIDDEN = 1000
 
-QBLOCK_AT, SEEN_AT, SLOT_AT, POS_AT, FAR_AT = 0, 1, 3, 5, 7
-FAR = (WINDOW + 2 * HALF - 2) // HALF
+QBLOCK_AT, SEEN_AT, SLOT_AT, POS_AT = 0, 1, 3, 5
 
 NT = (((1,), (1,)), ((), ()))
 NN = (((1,), (0,)), ((), ()))
@@ -62,8 +64,6 @@
         x = xl if col == 0 else 1 - xl
         here = ((lane >> 4) == y) & ((lane & 1) == x)
         columns[SEEN_AT + col] = picked(here & (low <= q_block), 1.0) + picked(here & (high <= q_block), 1.0)
-        far = q_block - FAR
-        columns[FAR_AT + col] = picked(here & (low <= far), 1.0) + picked(here & (high <= far), 1.0)
         k_low = picked(here & (((lane >> 1) & (NZ - 1)) == sub), low)
         columns[SLOT_AT + col] = picked(here & (low < k_low), 1.0)
         rank = picked(k_low < low, 1.0, axis=0)
@@ -123,26 +123,24 @@
         low = plan_ref[n, POS_AT + col]
         pos[n] = low
         pos[SLOTS - 1 - n] = BLOCKS - 1 - low
-    count = jnp.int32(0)
-    far = [plan_ref[rh, FAR_AT + col] // STEP for rh in range(QB)]
-    for rh in range(QB):
-        for c in range(PER_BLOCK):
-            steps[count] = rh * PER_BLOCK + c
-            count = count + (c < far[rh]).astype(i32)
-    plain = count
-    for rh in range(QB):
-        groups = (plan_ref[rh, SEEN_AT + col] + STEP - 1) // STEP
-        for c in range(PER_BLOCK):
-            steps[count] = rh * PER_BLOCK + c
-            count = count + ((c >= far[rh]) & (c < groups)).astype(i32)
-    last = steps[count - 1]
-    for i in range(3):
-        steps[count + i] = last + SKIP
-    return plain, count
-
-
-def step_of(steps, t):
-    v = steps[t]
+    counts = []
+    for stream in STREAMS:
+        count = jnp.int32(0)
+        for rh in range(stream * QS, (stream + 1) * QS):
+            groups = (plan_ref[rh, SEEN_AT + col] + STEP - 1) // STEP
+            for c in range(PER_BLOCK):
+                steps[stream * LIST + count] = rh * PER_BLOCK + c
+                count = count + (c < groups).astype(i32)
+        last = steps[stream * LIST + count - 1]
+        for i in range(5):
+            steps[stream * LIST + count + i] = last + SKIP
+        counts.append(count)
+    count = jnp.maximum(*counts)
+    return count + lax.rem(count, 2)
+
+
+def step_of(steps, stream, t):
+    v = steps[stream * LIST + t]
     rh = (v // PER_BLOCK) % QB
     c = v % PER_BLOCK
     return v, rh, c, pl.ds(pl.multiple_of(c * CK, CK), CK)
@@ -176,90 +174,100 @@
 
 def forward_kernel(col, plan_ref, *refs):
     if col == 0:
-        rows_in, (kv_ref, o_ref, st_ref, peaks, exps, qs, qt), refs = refs[:4], refs[4:11], refs[11:]
+        rows_in, kv_ref, refs = refs[:4], refs[4], refs[5:]
     else:
-        (qt, kv_ref, o_ref, st_ref, peaks, exps), refs = refs[:6], refs[6:]
-    ks, vs, vt, pen, s_a, s_b, f_a, f_b, pos, steps = refs
-    plain, count = list_steps(plan_ref, col, pos, steps)
+        (qt, kv_ref), refs = refs[:2], refs[2:]
+    os, sts, peaks, exps, refs = refs[:2], refs[2:4], refs[4:6], refs[6:8], refs[8:]
+    if col == 0:
+        (qs, qt), refs = refs[:2], refs[2:]
+    ks, vs, vt, pen, s_0, s_1, s_2, s_3, f_0, f_1, f_2, f_3, pos, steps = refs
+    s_even, s_odd, f_even, f_odd = (s_0, s_1), (s_2, s_3), (f_0, f_1), (f_2, f_3)
+    count = list_steps(plan_ref, col, pos, steps)
     if col == 0:
         load_rows(rows_in, qs)
         for rh in range(QB):
             qt[rh] = qs[rh].astype(f32).T.astype(bf16)
     sort_keys(plan_ref, col, kv_ref, ks, vs, pen)
     turn(vs, vt)
-    o_ref[...] = jnp.zeros_like(o_ref)
-    for rh in range(QB):
-        st_ref[rh, 0:1, :] = jnp.full((1, ROWS), LOWEST, f32)
-        st_ref[rh, 1:2, :] = jnp.zeros((1, ROWS), f32)
-    exps[0] = jnp.zeros_like(exps[0])
-    f_b[...] = jnp.ones_like(f_b)
-
-    def score(t, s_ref):
-        _, rh, _, at = step_of(steps, t)
-        s_ref[...] = dot(ks[at, :], qt[rh], NN)
-
-    def soften(t, s_ref, f_ref, masked):
-        v, rh, c, _ = step_of(steps, t)
+    for n in STREAMS:
+        os[n][...] = jnp.zeros_like(os[n])
+        for rh in range(QS):
+            sts[n][rh, 0:1, :] = jnp.full((1, ROWS), LOWEST, f32)
+            sts[n][rh, 1:2, :] = jnp.zeros((1, ROWS), f32)
+        exps[n][0] = jnp.zeros_like(exps[n][0])
+        f_odd[n][...] = jnp.ones_like(f_odd[n])
+
+    def score(n, t, s_refs):
+        _, rh, _, at = step_of(steps, n, t)
+        s_refs[n][...] = dot(ks[at, :], qt[rh], NN)
+
+    def soften(n, t, s_refs, f_refs):
+        v, rh, c, _ = step_of(steps, n, t)
         limits = thresholds(plan_ref, pos, v, rh, c)
         offset = offsets()
+        st = sts[n]
+        rh = rh - n * QS
         for lanes in TILES:
             parts = []
             for i, (seen, late) in enumerate(limits):
-                s = s_ref[i * HALF : (i + 1) * HALF, lanes] * SCALE
-                penalty = pen[block_rows(c, i), :]
-                if masked:
-                    s = s - jnp.where(offset >= late, penalty, 0.0)
-                    parts.append(jnp.where(offset >= seen, s, LOWEST))
-                else:
-                    parts.append(s - penalty)
-            peak = st_ref[rh, 0:1, lanes]
+                s = s_refs[n][i * HALF : (i + 1) * HALF, lanes] * SCALE
+                s = s - jnp.where(offset >= late, pen[block_rows(c, i), :], 0.0)
+                parts.append(jnp.where(offset >= seen, s, LOWEST))
+            peak = st[rh, 0:1, lanes]
             tops = functools.reduce(jnp.maximum, parts)
             new_peak = jnp.maximum(peak, jnp.max(tops, axis=0, keepdims=True))
             factor = jnp.exp(peak - new_peak)
             parts = [jnp.exp(s - new_peak) for s in parts]
             total = jnp.sum(sum(parts), axis=0, keepdims=True)
             for i, p in enumerate(parts):
-                exps[t, i * HALF : (i + 1) * HALF, lanes] = p.astype(bf16)
-            f_ref[0:1, lanes] = factor
-            peaks[t, 0:1, lanes] = new_peak
-            st_ref[rh, 0:1, lanes] = new_peak
-            st_ref[rh, 1:2, lanes] = st_ref[rh, 1:2, lanes] * factor + total
-
-    def attend(t, f_ref):
-        _, rh, c, _ = step_of(steps, t)
-        o_ref[rh] = o_ref[rh] * f_ref[0:1, :] + dot(turned_piece(vt, c), exps[t], NN)
-
-    score(0, s_a)
-
-    def pair(masked, i, _):
+                exps[n][t, i * HALF : (i + 1) * HALF, lanes] = p.astype(bf16)
+            f_refs[n][0:1, lanes] = factor
+            peaks[n][t, 0:1, lanes] = new_peak
+            st[rh, 0:1, lanes] = new_peak
+            st[rh, 1:2, lanes] = st[rh, 1:2, lanes] * factor + total
+
+    def attend(n, t, f_refs):
+        _, rh, c, _ = step_of(steps, n, t)
+        rh = rh - n * QS
+        os[n][rh] = os[n][rh] * f_refs[n][0:1, :] + dot(turned_piece(vt, c), exps[n][t], NN)
+
+    def both(work, *args):
+        for n in STREAMS:
+            work(n, *args)
+
+    both(score, 0, s_even)
+
+    def pair(i, _):
         t = 2 * i
-        attend(jnp.maximum(t - 1, 0), f_b)
-        score(t + 1, s_b)
-        soften(t, s_a, f_a, masked)
-        attend(t, f_a)
-        score(t + 2, s_a)
-        soften(t + 1, s_b, f_b, masked)
+        both(attend, jnp.maximum(t - 1, 0), f_odd)
+        both(score, t + 1, s_odd)
+        both(soften, t, s_even, f_even)
+        both(attend, t, f_even)
+        both(score, t + 2, s_even)
+        both(soften, t + 1, s_odd, f_odd)
         return 0
 
-    pairs = (count + 1) // 2
-    lax.fori_loop(0, plain // 2, functools.partial(pair, False), 0)
-    lax.fori_loop(plain // 2, pairs, functools.partial(pair, True), 0)
-    attend(2 * pairs - 1, f_b)
-
-
-def weigh_kernel(o0, st0, o1, st1, c0, c1, c2, c3, out_ref, cs, ct):
-    for r, ref in enumerate((c0, c1, c2, c3)):
+    lax.fori_loop(0, count // 2, pair, 0)
+    both(attend, count - 1, f_odd)
+
+
+def weigh_kernel(*refs):
+    sums, pieces, (out_ref, cs, ct) = (refs[:4], refs[4:8]), refs[8:12], refs[12:]
+    for r, ref in enumerate(pieces):
         for half in range(2):
             rh = 2 * r + half
+            n, inner = rh // QS, rh % QS
+            o0, o1 = (column[n] for column in sums)
+            st0, st1 = (column[2 + n] for column in sums)
             rows = ref[:, half * HALF : (half + 1) * HALF, :].reshape(ROWS, HD)
             cot = rows.astype(f32).T
             cs[rh] = rows
             ct[rh] = cot.astype(bf16)
-            peak = jnp.maximum(st0[rh, 0:1, :], st1[rh, 0:1, :])
-            f0, f1 = (jnp.exp(st[rh, 0:1, :] - peak) for st in (st0, st1))
-            total = st0[rh, 1:2, :] * f0 + st1[rh, 1:2, :] * f1
+            peak = jnp.maximum(st0[inner, 0:1, :], st1[inner, 0:1, :])
+            f0, f1 = (jnp.exp(st[inner, 0:1, :] - peak) for st in (st0, st1))
+            total = st0[inner, 1:2, :] * f0 + st1[inner, 1:2, :] * f1
             seen = total > 0.0
-            weighted = jnp.sum(cot * (o0[rh] * f0 + o1[rh] * f1), axis=0, keepdims=True)
+            weighted = jnp.sum(cot * (o0[inner] * f0 + o1[inner] * f1), axis=0, keepdims=True)
             safe = jnp.where(seen, total, 1.0)
             out_ref[rh : rh + 1, :] = jnp.where(seen, peak + jnp.log(safe), LOWEST)
             out_ref[QB + rh : QB + rh + 1, :] = weighted / safe
@@ -280,69 +288,72 @@
 
 
 def backward_kernel(col, plan_ref, *refs):
-    (qs, cs, ct, kv_ref, peaks, exps), pieces, refs = refs[:6], refs[6:10], refs[10:]
+    (qs, cs, ct, kv_ref), peaks, exps, pieces, refs = refs[:4], refs[4:6], refs[6:8], refs[8:12], refs[12:]
     if col == 1:
-        (dq, dkv_ref), refs = refs[:2], refs[2:]
+        dq, dkv_ref, refs = refs[:2], refs[2], refs[3:]
     else:
-        (dq_before,), dq_out, (dkv_ref,), refs = refs[:1], refs[1:5], refs[5:6], refs[6:]
-        (dq, turned, sems), refs = refs[:3], refs[3:]
-    ks, vs, kt, dk, dv, dl, stats, p_a, p_b, d_a, d_b, pos, steps = refs
-    plain, count = list_steps(plan_ref, col, pos, steps)
+        dq_before, dq_out, dkv_ref, dq, refs = refs[:2], refs[2:6], refs[6], refs[7:9], refs[9:]
+        (turned, sems), refs = refs[:2], refs[2:]
+    (ks, vs, kt, stats), dk, dv, dl, refs = refs[:4], refs[4:6], refs[6:8], refs[8:10], refs[10:]
+    p_even, p_odd, d_even, d_odd, (pos, steps) = refs[:2], refs[2:4], refs[4:6], refs[6:8], refs[8:]
+    count = list_steps(plan_ref, col, pos, steps)
     sort_keys(plan_ref, col, kv_ref, ks, vs)
     turn(ks, kt)
-    for ref in (dk, dv, dl, p_b, d_b):
+    for ref in dk + dv + dl + p_odd + d_odd:
         ref[...] = jnp.zeros_like(ref)
-    dq[...] = jnp.zeros_like(dq) if col == 1 else dq_before[...]
+    for n in STREAMS:
+        dq[n][...] = jnp.zeros_like(dq[n]) if col == 1 else dq_before[n][...]
     merge_stats(pieces, stats)
 
-    def differ(t, p_ref, d_ref, masked):
-        v, rh, c, _ = step_of(steps, t)
+    def differ(n, t, p_refs, d_refs):
+        v, rh, c, _ = step_of(steps, n, t)
         offset = offsets()
         limits = thresholds(plan_ref, pos, v, rh, c)
-        shares = [jnp.exp(peaks[t, 0:1, lanes] - stats[rh, 0:1, lanes]) for lanes in TILES]
+        shares = [jnp.exp(peaks[n][t, 0:1, lanes] - stats[rh, 0:1, lanes]) for lanes in TILES]
         for first in range(0, STEP, 2):
             blocks = (first, first + 1)
-            late_sums = [dl[block_rows(c, i), :] for i in blocks]
+            late_sums = [dl[n][block_rows(c, i), :] for i in blocks]
             at = pl.ds(pl.multiple_of(c * CK + first * HALF, SHARD), 2 * HALF)
             for wide in WIDE_TILES:
                 grad = dot(vs[at, :], ct[rh, :, wide], NN)
-                for n, i in enumerate(blocks):
+                for m, i in enumerate(blocks):
                     rows = slice(i * HALF, (i + 1) * HALF)
                     for j in range(WIDE // SHARD):
                         here = slice(j * SHARD, (j + 1) * SHARD)
                         lanes = slice(wide.start + here.start, wide.start + here.stop)
-                        p = exps[t, rows, lanes].astype(f32) * shares[lanes.start // SHARD]
-                        d = p * (grad[n * HALF : (n + 1) * HALF, here] - stats[rh, 1:2, lanes])
-                        late = jnp.where(offset >= limits[i][1], d, 0.0) if masked else d
-                        late_sums[n] = late_sums[n] + late
-                        p_ref[rows, lanes] = p.astype(bf16)
-                        d_ref[rows, lanes] = d.astype(bf16)
-            for n, i in enumerate(blocks):
-                dl[block_rows(c, i), :] = late_sums[n]
-
-    def gather(t, p_ref, d_ref):
-        _, rh, c, at = step_of(steps, t)
-        dk[at, :] += dot(d_ref[...], qs[rh], NN)
-        dv[at, :] += dot(p_ref[...], cs[rh], NN)
-        dq[rh] += dot(turned_piece(kt, c), d_ref[...], NN)
-
-    def pair(masked, i, _):
+                        p = exps[n][t, rows, lanes].astype(f32) * shares[lanes.start // SHARD]
+                        d = p * (grad[m * HALF : (m + 1) * HALF, here] - stats[rh, 1:2, lanes])
+                        late_sums[m] = late_sums[m] + jnp.where(offset >= limits[i][1], d, 0.0)
+                        p_refs[n][rows, lanes] = p.astype(bf16)
+                        d_refs[n][rows, lanes] = d.astype(bf16)
+            for m, i in enumerate(blocks):
+                dl[n][block_rows(c, i), :] = late_sums[m]
+
+    def gather(n, t, p_refs, d_refs):
+        _, rh, c, at = step_of(steps, n, t)
+        dk[n][at, :] += dot(d_refs[n][...], qs[rh], NN)
+        dv[n][at, :] += dot(p_refs[n][...], cs[rh], NN)
+        dq[n][rh - n * QS] += dot(turned_piece(kt, c), d_refs[n][...], NN)
+
+    def both(work, *args):
+        for n in STREAMS:
+            work(n, *args)
+
+    def pair(i, _):
         t = 2 * i
-        gather(jnp.maximum(t - 1, 0), p_b, d_b)
-        differ(t, p_a, d_a, masked)
-        gather(t, p_a, d_a)
-        differ(t + 1, p_b, d_b, masked)
+        both(gather, jnp.maximum(t - 1, 0), p_odd, d_odd)
+        both(differ, t, p_even, d_even)
+        both(gather, t, p_even, d_even)
+        both(differ, t + 1, p_odd, d_odd)
         return 0
 
-    pairs = (count + 1) // 2
-    lax.fori_loop(0, plain // 2, functools.partial(pair, False), 0)
-    lax.fori_loop(plain // 2, pairs, functools.partial(pair, True), 0)
-    gather(2 * pairs - 1, p_b, d_b)
+    lax.fori_loop(0, count // 2, pair, 0)
+    both(gather, count - 1, p_odd, d_odd)
     copies = []
     if col == 0:
         for r, ref in enumerate(dq_out):
             for half in range(2):
-                rows = (dq[2 * r + half].T * SCALE).astype(bf16)
+                rows = (dq[r // 2][2 * (r % 2) + half].T * SCALE).astype(bf16)
                 turned[r, :, half * HALF : (half + 1) * HALF, :] = rows.reshape(HEADS, HALF, HD)
             copies.append(pltpu.make_async_copy(turned.at[r], ref, sems.at[r]))
             copies[-1].start()
@@ -350,9 +361,11 @@
         low = plan_ref[j, SLOT_AT + col]
         spots = [pl.ds(pl.multiple_of(slot * HALF, HALF), HALF) for slot in (low, SLOTS - 1 - low)]
         for half, at in enumerate(spots):
-            dkv_ref[j, half * HALF : (half + 1) * HALF, :] = (dk[at, :] * SCALE).astype(dkv_ref.dtype)
-            dkv_ref[j, SHARD + half * HALF : SHARD + (half + 1) * HALF, :] = dv[at, :].astype(dkv_ref.dtype)
-        late = jnp.concatenate([dl[at, :] for at in spots], axis=0)
+            key_sum = (dk[0][at, :] + dk[1][at, :]) * SCALE
+            value_sum = dv[0][at, :] + dv[1][at, :]
+            dkv_ref[j, half * HALF : (half + 1) * HALF, :] = key_sum.astype(dkv_ref.dtype)
+            dkv_ref[j, SHARD + half * HALF : SHARD + (half + 1) * HALF, :] = value_sum.astype(dkv_ref.dtype)
+        late = jnp.concatenate([dl[0][at, :] + dl[1][at, :] for at in spots], axis=0)
         total = jnp.sum(late.T, axis=0, keepdims=True)
         dkv_ref[j, 2 * SHARD : 2 * SHARD + 16, :] = jnp.concatenate(
             [total, jnp.zeros((15, SHARD), f32)], axis=0
@@ -379,7 +392,7 @@
     return pltpu.CompilerParams(vmem_limit_bytes=mib * 1024 * 1024)
 
 
-MOST = 5 * NA
+MOST = 5 * NA // 2
 KEYS = SLOTS * HALF
 shaped = jax.ShapeDtypeStruct
 
@@ -426,14 +439,14 @@
 
 def run_forward(col, plan, q, kv):
     out_shape = (
-        shaped((QB, HD, ROWS), f32),
-        shaped((QB, 2, ROWS), f32),
-        shaped((MOST, 1, ROWS), f32),
-        shaped((MOST, CK, ROWS), bf16),
+        (shaped((QS, HD, ROWS), f32),) * 2
+        + (shaped((QS, 2, ROWS), f32),) * 2
+        + (shaped((MOST, 1, ROWS), f32),) * 2
+        + (shaped((MOST, CK, ROWS), bf16),) * 2
     )
     if col == 0:
         out_shape += (shaped((QB, ROWS, HD), bf16), shaped((QB, HD, ROWS), bf16))
-    o, st, peaks, exps, *turned = pl.pallas_call(
+    out = pl.pallas_call(
         functools.partial(forward_kernel, col),
         out_shape=out_shape,
         in_specs=[SMEM] + [VMEM] * (len(q) + 1),
@@ -443,18 +456,15 @@
             pltpu.VMEM((KEYS, HD), bf16),
             pltpu.VMEM((KEYS // SHARD, HD, SHARD), bf16),
             pltpu.VMEM((KEYS, SHARD), f32),
-            pltpu.VMEM((CK, ROWS), f32),
-            pltpu.VMEM((CK, ROWS), f32),
-            pltpu.VMEM((8, ROWS), f32),
-            pltpu.VMEM((8, ROWS), f32),
-            pltpu.SMEM((SLOTS,), i32),
-            pltpu.SMEM((QB * PER_BLOCK + 3,), i32),
-        ],
-        compiler_params=grant(14),
+        ]
+        + [pltpu.VMEM((CK, ROWS), f32)] * 4
+        + [pltpu.VMEM((8, ROWS), f32)] * 4
+        + [pltpu.SMEM((SLOTS,), i32), pltpu.SMEM((2 * LIST,), i32)],
+        compiler_params=grant(16),
         cost_estimate=cost(10),
         name=f"forward{col}",
     )(plan, *q, kv)
-    return (o, st), (peaks, exps), turned
+    return out[:4], out[4:8], out[8:]
 
 
 def run_weigh(sums, cot):
@@ -465,22 +475,21 @@
             shaped((QB, ROWS, HD), bf16),
             shaped((QB, HD, ROWS), bf16),
         ),
-        in_specs=[VMEM] * 8,
+        in_specs=[VMEM] * 12,
         out_specs=(VMEM,) * 3,
         compiler_params=grant(8),
         name="weigh",
     )(*sums, *cot)
 
 
-def run_backward(col, plan, rows, kv, exps, stats, dq_sum=None):
+def run_backward(col, plan, rows, kv, exps, stats, dq_sum=()):
+    sums = [pltpu.VMEM((QS, HD, ROWS), f32)] * 2
     if col == 1:
-        more, scratch = (), []
-        out_shape = (shaped((QB, HD, ROWS), f32), shaped((NZ, KV_ROWS, HD), bf16))
-        out_specs = (VMEM, VMEM)
+        scratch = []
+        out_shape = (shaped((QS, HD, ROWS), f32),) * 2 + (shaped((NZ, KV_ROWS, HD), bf16),)
+        out_specs = (VMEM,) * 3
     else:
-        more = (dq_sum,)
-        scratch = [
-            pltpu.VMEM((QB, HD, ROWS), f32),
+        scratch = sums + [
             pltpu.VMEM((NA, HEADS, SHARD, HD), bf16),
             pltpu.SemaphoreType.DMA((NA,)),
         ]
@@ -489,24 +498,22 @@
     return pl.pallas_call(
         functools.partial(backward_kernel, col),
         out_shape=out_shape,
-        in_specs=[SMEM] + [VMEM] * (10 + len(more)),
+        in_specs=[SMEM] + [VMEM] * (12 + len(dq_sum)),
         out_specs=out_specs,
         scratch_shapes=scratch
         + [
             pltpu.VMEM((KEYS, HD), bf16),
             pltpu.VMEM((KEYS, HD), bf16),
             pltpu.VMEM((KEYS // SHARD, HD, SHARD), bf16),
-            pltpu.VMEM((KEYS, HD), f32),
-            pltpu.VMEM((KEYS, HD), f32),
-            pltpu.VMEM((KEYS, SHARD), f32),
             pltpu.VMEM((QB, 2, ROWS), f32),
         ]
-        + [pltpu.VMEM((CK, ROWS), bf16)] * 4
-        + [pltpu.SMEM((SLOTS,), i32), pltpu.SMEM((QB * PER_BLOCK + 3,), i32)],
-        compiler_params=grant(18),
+        + [pltpu.VMEM((KEYS, HD), f32)] * 6
+        + [pltpu.VMEM((CK, ROWS), bf16)] * 8
+        + [pltpu.SMEM((SLOTS,), i32), pltpu.SMEM((2 * LIST,), i32)],
+        compiler_params=grant(22),
         cost_estimate=cost(15),
         name=f"backward{col}",
-    )(plan, *rows, kv, *exps, *stats, *more)
+    )(plan, *rows, kv, *exps, *stats, *dq_sum)
 
 
 def run_total(parts, logits):
@@ -555,7 +562,7 @@
     stats, cs, ct = run_weigh((*sums0, *sums1), cot_all)
     rows = (qs, cs, ct)
     stats = gather_y(stats)
-    dq_sum, dkv_other = run_backward(1, plan, rows, kv_other, exps1, stats)
+    *dq_sum, dkv_other = run_backward(1, plan, rows, kv_other, exps1, stats)
     dkv_here = swap(dkv_other, "xl")
     *dq, dkv = run_backward(0, plan, rows, kv, exps0, stats, dq_sum)
     dkv = (dkv + dkv_here.astype(f32)).astype(bf16)

time: 108 us -> 108 us (level)
  waiting for transfers between devices: 20.5 us -> 18.6 us
  Pallas kernels: 40.3 us -> 41.8 us
    pallas_call x2, Pallas kernels: 14.2 us -> 16.8 us  [run_forward(): pl.pallas_call(functools.partial(forward_kernel, col), out_shape=out_shap...]
    ppermute x5, waiting for transfers between devices: 5.74 us -> 4.34 us  [swap(): return lax.ppermute(x, axis, [(0, 1), (1, 0)])]
  transfers between devices with their start and end apart: 19 -> 19, of which waited for: 7 -> 8; matrix products, arithmetic and copies ran while one was open for 1% -> 1% of each run, Pallas kernels for 27% -> 29%
where the time goes in v4:
time: 108 us
  Pallas kernels  41.8 us (39%)
  starting transfers between devices  39.6 us (37%)
  waiting for transfers between devices  18.6 us (17%)
  local copies, waits for them, and re-layouts  5.24 us (5%)
  other arithmetic  1.77 us (2%)
    pallas_call x2, Pallas kernels, run_backward(): pl.pallas_call(functools.partial(backward_kernel, col), out_shape=out_sha...  18.9 us
    ppermute x12, starting transfers between devices, from_y(): return lax.ppermute(x, 'y', [((i + r) % NA, i) for i in range(NA)])  18.8 us
    pallas_call x2, Pallas kernels, run_forward(): pl.pallas_call(functools.partial(forward_kernel, col), out_shape=out_shap...  16.8 us
    ppermute x12, waiting for transfers between devices, from_y(): return lax.ppermute(x, 'y', [((i + r) % NA, i) for i in range(NA)])  11.5 us
    all_to_all x1, starting transfers between devices, per_device(): lax.all_to_all(run_pack(keys, values, evict_logits), 'z', 0, 0, tiled=True)  8.47 us
    all_to_all x1, starting transfers between devices, per_device(): dkv = lax.all_to_all(dkv, 'z', 0, 0, tiled=True)  6.54 us
    ppermute x5, starting transfers between devices, swap(): return lax.ppermute(x, axis, [(0, 1), (1, 0)])  5.75 us
    unnamed x14, local copies, waits for them, and re-layouts  5.24 us
  transfers between devices with their start and end apart: 19, of which 8 were waited for; matrix products, arithmetic and copies ran while one was open for 1% of the time, Pallas kernels for 29%

profile of v4, /device:TPU:2, one launch (start us, length us, event | category | flops | bytes accessed | tf_op | source)
XLA Modules:
  0.0 107.7 jit_solution(13319192245319535117)
XLA Ops:
  0.6 2.2 %collective-permute-start.4 = (bf16[32,5120]{1,0:T(8,128)(2,1)}, bf16[32,5120]{1,0:T(8,128)(2,1)S(1)}, u32[]{:S(2)}, u32[]{:S(2)}) collective-permute-start(bf16[32,5120]{1,0:T(8,128)(2,1)} %g0.1), channel_id=1, source_target_pairs={{0,2},{2,0},{1,3},{3,1},{4,6},{6,4},{5,7},{7,5},{8,10},{10,8},{9,1... | collective-permute-start | bytes 983048 | tf_op jit(solution)/shard_map/ppermute | solution.py:539
  5.2 8.5 %all-to-all-start = ((bf16[8,272,128]{2,1,0:T(8,128)(2,1)}), bf16[8,272,128]{2,1,0:T(8,128)(2,1)S(1)}, u32[]{:S(2)}, u32[]{:S(2)}) async-start(bf16[8,272,128]{2,1,0:T(8,128)(2,1)} %pack.1), calls=%async_computation | async-start | bytes 1114112 | tf_op jit(solution)/shard_map/all_to_all | solution.py:553
  14.3 3.2 %collective-permute-start.1 = (bf16[8,128,128]{2,1,0:T(8,128)(2,1)S(1)}, bf16[8,128,128]{2,1,0:T(8,128)(2,1)S(1)}, u32[]{:S(2)}, u32[]{:S(2)}) collective-permute-start(bf16[8,128,128]{2,1,0:T(8,128)(2,1)S(1)} %copy-done.5), channel_id=1, source_target_pairs={{128,0},{192,64},{0,128},{64,192},{129,1},{193,65},{1,129},{65,193... | collective-permute-start | bytes 786440 | tf_op jit(solution)/shard_map/ppermute | solution.py:531
  17.5 1.1 collective-permute-start
  19.5 4.0 %copy-done.3 = bf16[1024,5120]{1,0:T(8,128)(2,1)S(1)} copy-done((bf16[1024,5120]{1,0:T(8,128)(2,1)S(1)}, bf16[1024,5120]{1,0:T(8,128)(2,1)}, u32[]{:S(2)}) %copy-start.3) | copy-done | bytes 10485784
  23.5 3.6 %cotangent.1.refs_8_ = bf16[8,128,128]{2,1,0:T(8,128)(2,1)S(1)} custom-call(bf16[32,5120]{1,0:T(8,128)(2,1)S(1)} %copy-done.4, bf16[32,5120]{1,0:T(8,128)(2,1)S(1)} %collective-permute-done.4.g1, bf16[32,5120]{1,0:T(8,128)(2,1)S(1)} %collective-permute-done.5.g2, bf16[32,5120]{1,0:T(8,128)(2,1)S(1)} %collective-permute-done.6.g3, ...), custom_call_target="tpu_custom_call" | custom-call | flops 5000000000 | bytes 1048576 | tf_op jit(solution)/shard_map/cotangent/pallas_call | solution.py:428
  27.8 3.1 %collective-permute-start.8 = (bf16[8,128,128]{2,1,0:T(8,128)(2,1)S(1)}, bf16[8,128,128]{2,1,0:T(8,128)(2,1)S(1)}, u32[]{:S(2)}, u32[]{:S(2)}) collective-permute-start(bf16[8,128,128]{2,1,0:T(8,128)(2,1)S(1)} %cotangent.1.refs_8_), channel_id=1, source_target_pairs={{128,0},{192,64},{0,128},{64,192},{129,1},{193,65},{1,129},{65,193... | collective-permute-start | bytes 786440 | tf_op jit(solution)/shard_map/ppermute | solution.py:531
  31.6 1.4 %collective-permute-start.3 = (bf16[8,272,128]{2,1,0:T(8,128)(2,1)S(1)}, bf16[8,272,128]{2,1,0:T(8,128)(2,1)S(1)}, u32[]{:S(2)}, u32[]{:S(2)}) collective-permute-start(bf16[8,272,128]{2,1,0:T(8,128)(2,1)S(1)} %all-to-all-done.refs_4_.refs_3_), channel_id=1, source_target_pairs={{0,4},{4,0},{1,5},{5,1},{2,6},{6,2},{3,7},{7,3},{8,12},{12,8},{9,1... | collective-permute-start | bytes 1671176 | tf_op jit(solution)/shard_map/ppermute | solution.py:539
  33.0 8.4 %forward0.1 = (f32[4,128,512]{2,1,0:T(8,128)S(1)}, f32[4,128,512]{2,1,0:T(8,128)S(1)}, f32[4,2,512]{2,1,0:T(2,128)S(1)}, f32[4,2,512]{2,1,0:T(2,128)S(1)}, f32[1...) custom-call(s32[8,128]{1,0:T(8,128)S(1)} %plan.1.plan_ref, ...), custom_call_target="tpu_custom_call" | custom-call | flops 10000000000 | bytes 1048576 | tf_op jit(solution)/shard_map/forward0/pallas_call | solution.py:449
  41.5 4.2 %collective-permute-done.3.refs_1_.refs_3_ = bf16[8,272,128]{2,1,0:T(8,128)(2,1)S(1)} collective-permute-done((bf16[8,272,128]{2,1,0:T(8,128)(2,1)S(1)}, bf16[8,272,128]{2,1,0:T(8,128)(2,1)S(1)}, u32[]{:S(2)}, u32[]{:S(2)}) %collective-permute-start.3) | collective-permute-done | bytes 557088 | tf_op jit(solution)/shard_map/ppermute | solution.py:539
  45.6 8.3 %forward1.1 = (f32[4,128,512]{2,1,0:T(8,128)S(1)}, f32[4,128,512]{2,1,0:T(8,128)S(1)}, f32[4,2,512]{2,1,0:T(2,128)S(1)}, f32[4,2,512]{2,1,0:T(2,128)S(1)}, f32[1...) custom-call(s32[8,128]{1,0:T(8,128)S(1)} %plan.1.plan_ref, ...), custom_call_target="tpu_custom_call" | custom-call | flops 10000000000 | bytes 1048576 | tf_op jit(solution)/shard_map/forward1/pallas_call | solution.py:449
  54.8 1.7 %collective-permute-start.12 = (f32[16,512]{1,0:T(8,128)S(1)}, f32[16,512]{1,0:T(8,128)S(1)}, u32[]{:S(2)}, u32[]{:S(2)}) collective-permute-start(f32[16,512]{1,0:T(8,128)S(1)} %get-tuple-element.56.refs_8_), channel_id=1, source_target_pairs={{192,0},{0,64},{64,128},{128,192},{193,1},{1,65},{65,129},{129,193... | collective-permute-start | bytes 98312 | tf_op jit(solution)/shard_map/ppermute | solution.py:531
  56.4 2.9 %collective-permute-start.11 = (f32[16,512]{1,0:T(8,128)S(1)}, f32[16,512]{1,0:T(8,128)S(1)}, u32[]{:S(2)}, u32[]{:S(2)}) collective-permute-start(f32[16,512]{1,0:T(8,128)S(1)} %get-tuple-element.56.refs_8_), channel_id=1, source_target_pairs={{128,0},{192,64},{0,128},{64,192},{129,1},{193,65},{1,129},{65,193... | collective-permute-start | bytes 98312 | tf_op jit(solution)/shard_map/ppermute | solution.py:531
  59.3 1.3 %collective-permute-start.10 = (f32[16,512]{1,0:T(8,128)S(1)}, f32[16,512]{1,0:T(8,128)S(1)}, u32[]{:S(2)}, u32[]{:S(2)}) collective-permute-start(f32[16,512]{1,0:T(8,128)S(1)} %get-tuple-element.56.refs_8_), channel_id=1, source_target_pairs={{64,0},{128,64},{192,128},{0,192},{65,1},{129,65},{193,129},{1,193... | collective-permute-start | bytes 98312 | tf_op jit(solution)/shard_map/ppermute | solution.py:531
  60.7 1.2 %collective-permute-done.11.refs_10_ = f32[16,512]{1,0:T(8,128)S(1)} collective-permute-done((f32[16,512]{1,0:T(8,128)S(1)}, f32[16,512]{1,0:T(8,128)S(1)}, u32[]{:S(2)}, u32[]{:S(2)}) %collective-permute-start.11) | collective-permute-done | bytes 32800 | tf_op jit(solution)/shard_map/ppermute | solution.py:531
  61.9 1.4 %collective-permute-done.10.refs_9_ = f32[16,512]{1,0:T(8,128)S(1)} collective-permute-done((f32[16,512]{1,0:T(8,128)S(1)}, f32[16,512]{1,0:T(8,128)S(1)}, u32[]{:S(2)}, u32[]{:S(2)}) %collective-permute-start.10) | collective-permute-done | bytes 32800 | tf_op jit(solution)/shard_map/ppermute | solution.py:531
  63.3 9.1 %backward1.1 = (f32[4,128,512]{2,1,0:T(8,128)S(1)}, f32[4,128,512]{2,1,0:T(8,128)S(1)}, bf16[8,272,128]{2,1,0:T(8,128)(2,1)S(1)}) custom-call(s32[8,128]{1,0:T(8,128)S(1)} %plan.1.plan_ref, bf16[8,512,128]{2,1,0:T(8,128)(2,1)S(1)} %get-tuple-element.40.refs_0_, bf16[8,512,128]{2,1,0:T(8,128)(2,1)S(1)} %get-tuple-element.50.refs_1_, ...), custom_call_target="tpu_custom_call" | custom-call | flops 15000000512 | bytes 1048576 | tf_op jit(solution)/shard_map/backward1/pallas_call | solution.py:498
  72.3 1.5 %collective-permute-start.16 = (bf16[8,272,128]{2,1,0:T(8,128)(2,1)S(1)}, bf16[8,272,128]{2,1,0:T(8,128)(2,1)S(1)}, u32[]{:S(2)}, u32[]{:S(2)}) collective-permute-start(bf16[8,272,128]{2,1,0:T(8,128)(2,1)S(1)} %get-tuple-element.68), channel_id=1, source_target_pairs={{0,4},{4,0},{1,5},{5,1},{2,6},{6,2},{3,7},{7,3},{8,12},{12,8},{9,1... | collective-permute-start | bytes 1671176 | tf_op jit(solution)/shard_map/ppermute | solution.py:539
  73.8 9.8 %backward0.1 = (bf16[8,128,128]{2,1,0:T(8,128)(2,1)S(1)}, bf16[8,128,128]{2,1,0:T(8,128)(2,1)S(1)}, bf16[8,128,128]{2,1,0:T(8,128)(2,1)S(1)}, bf16[8,128,128]{2,1,0:T(8,128)(2,1)S(1)}, f32[8,272,128]{2,1,0:T(8,128)S(1)}) custom-call(s32[8,128]{1,0:T(8,128)S(1)} %plan.1.plan_ref, bf16[8,512,128]{2,1,0:T(8,128)(2,1)S(1)} %get-tuple-element.40.refs_0_, ...), custom_call_target="tpu_custom_call" | custom-call | flops 15000000512 | bytes 1048576 | tf_op jit(solution)/shard_map/backward0/pallas_call | solution.py:498
  84.8 6.5 %all-to-all-start.1 = ((bf16[8,272,128]{2,1,0:T(8,128)(2,1)}), bf16[8,272,128]{2,1,0:T(8,128)(2,1)S(1)}, u32[]{:S(2)}, u32[]{:S(2)}) async-start(bf16[8,272,128]{2,1,0:T(8,128)(2,1)} %add_convert_fusion), calls=%async_computation.1 | async-start | bytes 1114112 | tf_op jit(solution)/shard_map/all_to_all | solution.py:569
  91.3 2.4 %collective-permute-start.14 = (bf16[8,128,128]{2,1,0:T(8,128)(2,1)S(1)}, bf16[8,128,128]{2,1,0:T(8,128)(2,1)S(1)}, u32[]{:S(2)}, u32[]{:S(2)}) collective-permute-start(bf16[8,128,128]{2,1,0:T(8,128)(2,1)S(1)} %get-tuple-element.65), channel_id=1, source_target_pairs={{128,0},{192,64},{0,128},{64,192},{129,1},{193,65},{1,129},{65,193... | collective-permute-start | bytes 786440 | tf_op jit(solution)/shard_map/ppermute | solution.py:531
  93.7 1.5 %collective-permute-start.15 = (bf16[8,128,128]{2,1,0:T(8,128)(2,1)S(1)}, bf16[8,128,128]{2,1,0:T(8,128)(2,1)S(1)}, u32[]{:S(2)}, u32[]{:S(2)}) collective-permute-start(bf16[8,128,128]{2,1,0:T(8,128)(2,1)S(1)} %get-tuple-element.66), channel_id=1, source_target_pairs={{64,0},{128,64},{192,128},{0,192},{65,1},{129,65},{193,129},{1,193... | collective-permute-start | bytes 786440 | tf_op jit(solution)/shard_map/ppermute | solution.py:531
  95.2 8.3 %collective-permute-done.13 = bf16[8,128,128]{2,1,0:T(8,128)(2,1)S(1)} collective-permute-done((bf16[8,128,128]{2,1,0:T(8,128)(2,1)S(1)}, bf16[8,128,128]{2,1,0:T(8,128)(2,1)S(1)}, u32[]{:S(2)}, u32[]{:S(2)}) %collective-permute-start.13) | collective-permute-done | bytes 262176 | tf_op jit(solution)/shard_map/ppermute | solution.py:531
  104.9 2.1 %all-to-all-done.1.parts_ref = bf16[8,272,128]{2,1,0:T(8,128)(2,1)S(1)} async-done(((bf16[8,272,128]{2,1,0:T(8,128)(2,1)}), bf16[8,272,128]{2,1,0:T(8,128)(2,1)S(1)}, u32[]{:S(2)}, u32[]{:S(2)}) %all-to-all-start.1) | async-done | bytes 557088 | tf_op jit(solution)/shard_map/all_to_all | solution.py:569
  (39 shorter events, 9.4 us)
Async XLA Ops:
  0.6 13.1 %collective-permute-start.4 = (bf16[32,5120]{1,0:T(8,128)(2,1)}, bf16[32,5120]{1,0:T(8,128)(2,1)S(1)}, u32[]{:S(2)}, u32[]{:S(2)}) collective-permute-start(bf16[32,5120]{1,0:T(8,128)(2,1)} %g0.1), channel_id=1, source_target_pairs={{0,2},{2,0},{1,3},{3,1},{4,6},{6,4},{5,7},{7,5},{8,10},{10,8},{9,1... | collective-permute-start | bytes 983048 | tf_op jit(solution)/shard_map/ppermute | solution.py:539
  3.5 0.8 copy-start.1
  3.5 0.8 copy-start.2
  3.5 10.1 %copy-start.4 = (bf16[32,5120]{1,0:T(8,128)(2,1)S(1)}, bf16[32,5120]{1,0:T(8,128)(2,1)}, u32[]{:S(2)}) copy-start(bf16[32,5120]{1,0:T(8,128)(2,1)} %g0.1) | copy-start | bytes 983044
  3.5 10.7 %copy-start.5 = (bf16[8,128,128]{2,1,0:T(8,128)(2,1)S(1)}, bf16[8,128,128]{2,1,0:T(8,128)(2,1)}, u32[]{:S(2)}) copy-start(bf16[8,128,128]{2,1,0:T(8,128)(2,1)} %refs_0_.1) | copy-start | bytes 786436
  5.2 26.4 %all-to-all-start = ((bf16[8,272,128]{2,1,0:T(8,128)(2,1)}), bf16[8,272,128]{2,1,0:T(8,128)(2,1)S(1)}, u32[]{:S(2)}, u32[]{:S(2)}) async-start(bf16[8,272,128]{2,1,0:T(8,128)(2,1)} %pack.1), calls=%async_computation | async-start | bytes 1114112 | tf_op jit(solution)/shard_map/all_to_all | solution.py:553
  13.7 5.8 %collective-permute-start.5 = (bf16[32,5120]{1,0:T(8,128)(2,1)S(1)}, bf16[32,5120]{1,0:T(8,128)(2,1)S(1)}, u32[]{:S(2)}, u32[]{:S(2)}) collective-permute-start(bf16[32,5120]{1,0:T(8,128)(2,1)S(1)} %copy-done.4), channel_id=1, source_target_pairs={{0,1},{1,0},{2,3},{3,2},{4,5},{5,4},{6,7},{7,6},{8,9},{9,8},{10,11... | collective-permute-start | bytes 983048 | tf_op jit(solution)/shard_map/ppermute | solution.py:539
  13.8 5.7 %collective-permute-start.6 = (bf16[32,5120]{1,0:T(8,128)(2,1)S(1)}, bf16[32,5120]{1,0:T(8,128)(2,1)S(1)}, u32[]{:S(2)}, u32[]{:S(2)}) collective-permute-start(bf16[32,5120]{1,0:T(8,128)(2,1)S(1)} %collective-permute-done.4.g1), channel_id=1, source_target_pairs={{0,1},{1,0},{2,3},{3,2},{4,5},{5,4},{6,7},{7,6},{8,9},{9,8},{10,11... | collective-permute-start | bytes 983048 | tf_op jit(solution)/shard_map/ppermute | solution.py:539
  14.3 16.6 %collective-permute-start.1 = (bf16[8,128,128]{2,1,0:T(8,128)(2,1)S(1)}, bf16[8,128,128]{2,1,0:T(8,128)(2,1)S(1)}, u32[]{:S(2)}, u32[]{:S(2)}) collective-permute-start(bf16[8,128,128]{2,1,0:T(8,128)(2,1)S(1)} %copy-done.5), channel_id=1, source_target_pairs={{128,0},{192,64},{0,128},{64,192},{129,1},{193,65},{1,129},{65,193... | collective-permute-start | bytes 786440 | tf_op jit(solution)/shard_map/ppermute | solution.py:531
  17.5 13.4 %collective-permute-start = (bf16[8,128,128]{2,1,0:T(8,128)(2,1)S(1)}, bf16[8,128,128]{2,1,0:T(8,128)(2,1)S(1)}, u32[]{:S(2)}, u32[]{:S(2)}) collective-permute-start(bf16[8,128,128]{2,1,0:T(8,128)(2,1)S(1)} %copy-done.5), channel_id=1, source_target_pairs={{64,0},{128,64},{192,128},{0,192},{65,1},{129,65},{193,129},{1,193... | collective-permute-start | bytes 786440 | tf_op jit(solution)/shard_map/ppermute | solution.py:531
  18.5 14.5 %collective-permute-start.2 = (bf16[8,128,128]{2,1,0:T(8,128)(2,1)S(1)}, bf16[8,128,128]{2,1,0:T(8,128)(2,1)S(1)}, u32[]{:S(2)}, u32[]{:S(2)}) collective-permute-start(bf16[8,128,128]{2,1,0:T(8,128)(2,1)S(1)} %copy-done.5), channel_id=1, source_target_pairs={{192,0},{0,64},{64,128},{128,192},{193,1},{1,65},{65,129},{129,193... | collective-permute-start | bytes 786440 | tf_op jit(solution)/shard_map/ppermute | solution.py:531
  19.5 4.0 %copy-start.3 = (bf16[1024,5120]{1,0:T(8,128)(2,1)S(1)}, bf16[1024,5120]{1,0:T(8,128)(2,1)}, u32[]{:S(2)}) copy-start(bf16[1024,5120]{1,0:T(8,128)(2,1)} %w_ref.1) | copy-start | bytes 31457284
  27.1 26.9 %collective-permute-start.9 = (bf16[8,128,128]{2,1,0:T(8,128)(2,1)S(1)}, bf16[8,128,128]{2,1,0:T(8,128)(2,1)S(1)}, u32[]{:S(2)}, u32[]{:S(2)}) collective-permute-start(bf16[8,128,128]{2,1,0:T(8,128)(2,1)S(1)} %cotangent.1.refs_8_), channel_id=1, source_target_pairs={{192,0},{0,64},{64,128},{128,192},{193,1},{1,65},{65,129},{129,193... | collective-permute-start | bytes 786440 | tf_op jit(solution)/shard_map/ppermute | solution.py:531
  27.8 26.2 %collective-permute-start.8 = (bf16[8,128,128]{2,1,0:T(8,128)(2,1)S(1)}, bf16[8,128,128]{2,1,0:T(8,128)(2,1)S(1)}, u32[]{:S(2)}, u32[]{:S(2)}) collective-permute-start(bf16[8,128,128]{2,1,0:T(8,128)(2,1)S(1)} %cotangent.1.refs_8_), channel_id=1, source_target_pairs={{128,0},{192,64},{0,128},{64,192},{129,1},{193,65},{1,129},{65,193... | collective-permute-start | bytes 786440 | tf_op jit(solution)/shard_map/ppermute | solution.py:531
  30.9 23.1 %collective-permute-start.7 = (bf16[8,128,128]{2,1,0:T(8,128)(2,1)S(1)}, bf16[8,128,128]{2,1,0:T(8,128)(2,1)S(1)}, u32[]{:S(2)}, u32[]{:S(2)}) collective-permute-start(bf16[8,128,128]{2,1,0:T(8,128)(2,1)S(1)} %cotangent.1.refs_8_), channel_id=1, source_target_pairs={{64,0},{128,64},{192,128},{0,192},{65,1},{129,65},{193,129},{1,193... | collective-permute-start | bytes 786440 | tf_op jit(solution)/shard_map/ppermute | solution.py:531
  31.6 14.1 %collective-permute-start.3 = (bf16[8,272,128]{2,1,0:T(8,128)(2,1)S(1)}, bf16[8,272,128]{2,1,0:T(8,128)(2,1)S(1)}, u32[]{:S(2)}, u32[]{:S(2)}) collective-permute-start(bf16[8,272,128]{2,1,0:T(8,128)(2,1)S(1)} %all-to-all-done.refs_4_.refs_3_), channel_id=1, source_target_pairs={{0,4},{4,0},{1,5},{5,1},{2,6},{6,2},{3,7},{7,3},{8,12},{12,8},{9,1... | collective-permute-start | bytes 1671176 | tf_op jit(solution)/shard_map/ppermute | solution.py:539
  54.8 5.9 %collective-permute-start.12 = (f32[16,512]{1,0:T(8,128)S(1)}, f32[16,512]{1,0:T(8,128)S(1)}, u32[]{:S(2)}, u32[]{:S(2)}) collective-permute-start(f32[16,512]{1,0:T(8,128)S(1)} %get-tuple-element.56.refs_8_), channel_id=1, source_target_pairs={{192,0},{0,64},{64,128},{128,192},{193,1},{1,65},{65,129},{129,193... | collective-permute-start | bytes 98312 | tf_op jit(solution)/shard_map/ppermute | solution.py:531
  56.4 5.4 %collective-permute-start.11 = (f32[16,512]{1,0:T(8,128)S(1)}, f32[16,512]{1,0:T(8,128)S(1)}, u32[]{:S(2)}, u32[]{:S(2)}) collective-permute-start(f32[16,512]{1,0:T(8,128)S(1)} %get-tuple-element.56.refs_8_), channel_id=1, source_target_pairs={{128,0},{192,64},{0,128},{64,192},{129,1},{193,65},{1,129},{65,193... | collective-permute-start | bytes 98312 | tf_op jit(solution)/shard_map/ppermute | solution.py:531
  59.3 3.9 %collective-permute-start.10 = (f32[16,512]{1,0:T(8,128)S(1)}, f32[16,512]{1,0:T(8,128)S(1)}, u32[]{:S(2)}, u32[]{:S(2)}) collective-permute-start(f32[16,512]{1,0:T(8,128)S(1)} %get-tuple-element.56.refs_8_), channel_id=1, source_target_pairs={{64,0},{128,64},{192,128},{0,192},{65,1},{129,65},{193,129},{1,193... | collective-permute-start | bytes 98312 | tf_op jit(solution)/shard_map/ppermute | solution.py:531
  72.3 11.5 %collective-permute-start.16 = (bf16[8,272,128]{2,1,0:T(8,128)(2,1)S(1)}, bf16[8,272,128]{2,1,0:T(8,128)(2,1)S(1)}, u32[]{:S(2)}, u32[]{:S(2)}) collective-permute-start(bf16[8,272,128]{2,1,0:T(8,128)(2,1)S(1)} %get-tuple-element.68), channel_id=1, source_target_pairs={{0,4},{4,0},{1,5},{5,1},{2,6},{6,2},{3,7},{7,3},{8,12},{12,8},{9,1... | collective-permute-start | bytes 1671176 | tf_op jit(solution)/shard_map/ppermute | solution.py:539
  84.8 22.3 %all-to-all-start.1 = ((bf16[8,272,128]{2,1,0:T(8,128)(2,1)}), bf16[8,272,128]{2,1,0:T(8,128)(2,1)S(1)}, u32[]{:S(2)}, u32[]{:S(2)}) async-start(bf16[8,272,128]{2,1,0:T(8,128)(2,1)} %add_convert_fusion), calls=%async_computation.1 | async-start | bytes 1114112 | tf_op jit(solution)/shard_map/all_to_all | solution.py:569
  91.3 12.1 %collective-permute-start.13 = (bf16[8,128,128]{2,1,0:T(8,128)(2,1)S(1)}, bf16[8,128,128]{2,1,0:T(8,128)(2,1)S(1)}, u32[]{:S(2)}, u32[]{:S(2)}) collective-permute-start(bf16[8,128,128]{2,1,0:T(8,128)(2,1)S(1)} %get-tuple-element.64), channel_id=1, source_target_pairs={{192,0},{0,64},{64,128},{128,192},{193,1},{1,65},{65,129},{129,193... | collective-permute-start | bytes 786440 | tf_op jit(solution)/shard_map/ppermute | solution.py:531
  91.3 12.1 %collective-permute-start.14 = (bf16[8,128,128]{2,1,0:T(8,128)(2,1)S(1)}, bf16[8,128,128]{2,1,0:T(8,128)(2,1)S(1)}, u32[]{:S(2)}, u32[]{:S(2)}) collective-permute-start(bf16[8,128,128]{2,1,0:T(8,128)(2,1)S(1)} %get-tuple-element.65), channel_id=1, source_target_pairs={{128,0},{192,64},{0,128},{64,192},{129,1},{193,65},{1,129},{65,193... | collective-permute-start | bytes 786440 | tf_op jit(solution)/shard_map/ppermute | solution.py:531
  93.7 10.4 %collective-permute-start.15 = (bf16[8,128,128]{2,1,0:T(8,128)(2,1)S(1)}, bf16[8,128,128]{2,1,0:T(8,128)(2,1)S(1)}, u32[]{:S(2)}, u32[]{:S(2)}) collective-permute-start(bf16[8,128,128]{2,1,0:T(8,128)(2,1)S(1)} %get-tuple-element.66), channel_id=1, source_target_pairs={{64,0},{128,64},{192,128},{0,192},{65,1},{129,65},{193,129},{1,193... | collective-permute-start | bytes 786440 | tf_op jit(solution)/shard_map/ppermute | solution.py:531
  (2 other events, 1.4 us)

commit v5 on v2

--- a/solution.py
+++ b/solution.py
@@ -30,6 +30,10 @@
 TILES = [slice(j * SHARD, (j + 1) * SHARD) for j in range(ROWS // SHARD)]
 WIDE = 256
 WIDE_TILES = [slice(j * WIDE, (j + 1) * WIDE) for j in range(ROWS // WIDE)]
+STREAMS = (0, 1)
+QS = QB // 2
+LIST = 24
+COUNT_AT, KEPT_AT, LISTED_AT, LISTS = 2 * LIST, 64, 128, 256
 SKIP = 64
 HIDDEN = 1000
 
@@ -118,11 +122,25 @@
         dest[i] = src[i * SHARD : (i + 1) * SHARD, :].astype(f32).T.astype(bf16)
 
 
-def list_steps(plan_ref, col, pos, steps):
+class Part:
+    def __init__(self, ref, start):
+        self.ref, self.start = ref, start
+
+    def __getitem__(self, i):
+        return self.ref[self.start + i]
+
+    def __setitem__(self, i, value):
+        self.ref[self.start + i] = value
+
+
+def list_positions(plan_ref, col, pos):
     for n in range(NZ):
         low = plan_ref[n, POS_AT + col]
         pos[n] = low
         pos[SLOTS - 1 - n] = BLOCKS - 1 - low
+
+
+def list_steps(plan_ref, col, steps):
     count = jnp.int32(0)
     far = [plan_ref[rh, FAR_AT + col] // STEP for rh in range(QB)]
     for rh in range(QB):
@@ -141,6 +159,23 @@
     return plain, count
 
 
+def list_streams(plan_ref, col, steps):
+    counts = []
+    for stream in STREAMS:
+        count = jnp.int32(0)
+        for rh in range(stream * QS, (stream + 1) * QS):
+            groups = (plan_ref[rh, SEEN_AT + col] + STEP - 1) // STEP
+            for c in range(PER_BLOCK):
+                steps[stream * LIST + count] = rh * PER_BLOCK + c
+                count = count + (c < groups).astype(i32)
+        last = steps[stream * LIST + count - 1]
+        for i in range(5):
+            steps[stream * LIST + count + i] = last + SKIP
+        counts.append(count)
+    count = jnp.maximum(*counts)
+    return count + lax.rem(count, 2)
+
+
 def step_of(steps, t):
     v = steps[t]
     rh = (v // PER_BLOCK) % QB
@@ -148,6 +183,27 @@
     return v, rh, c, pl.ds(pl.multiple_of(c * CK, CK), CK)
 
 
+def lists_kernel(plan_ref, *refs):
+    for col, ref in enumerate(refs):
+        plain, total = list_steps(plan_ref, col, Part(ref, LISTED_AT))
+
+        def note(t, _):
+            ref[KEPT_AT + ref[LISTED_AT + t]] = t
+            return 0
+
+        lax.fori_loop(0, total, note, 0)
+        ref[COUNT_AT] = list_streams(plan_ref, col, ref)
+        ref[COUNT_AT + 1] = plain
+        ref[COUNT_AT + 2] = total
+
+
+def stream_step(steps, stream, t):
+    v = steps[stream * LIST + t]
+    rh = (v // PER_BLOCK) % QB
+    c = v % PER_BLOCK
+    return v, rh, c, pl.ds(pl.multiple_of(c * CK, CK), CK)
+
+
 def thresholds(plan_ref, pos, v, rh, c):
     q_block = plan_ref[rh, QBLOCK_AT]
     ahead = [(q_block - pos[c * STEP + i]) * HALF for i in range(STEP)]
@@ -178,9 +234,13 @@
     if col == 0:
         rows_in, (kv_ref, o_ref, st_ref, peaks, exps, qs, qt), refs = refs[:4], refs[4:11], refs[11:]
     else:
-        (qt, kv_ref, o_ref, st_ref, peaks, exps), refs = refs[:6], refs[6:]
+        (qt, kv_ref, lists, o_ref, st_ref, peaks, exps), refs = refs[:7], refs[7:]
     ks, vs, vt, pen, s_a, s_b, f_a, f_b, pos, steps = refs
-    plain, count = list_steps(plan_ref, col, pos, steps)
+    list_positions(plan_ref, col, pos)
+    if col == 0:
+        plain, count = list_steps(plan_ref, col, steps)
+    else:
+        steps, plain, count = Part(lists, LISTED_AT), lists[COUNT_AT + 1], lists[COUNT_AT + 2]
     if col == 0:
         load_rows(rows_in, qs)
         for rh in range(QB):
@@ -265,84 +325,95 @@
             out_ref[QB + rh : QB + rh + 1, :] = weighted / safe
 
 
+def combine(parts):
+    peak = functools.reduce(jnp.maximum, [norm for norm, _ in parts])
+    shares = [jnp.exp(norm - peak) for norm, _ in parts]
+    total = sum(shares)
+    return peak + jnp.log(total), sum(share * mean for share, (_, mean) in zip(shares, parts)) / total
+
+
+def row_pair(ref, n):
+    return ref[n : n + 1, :], ref[QB + n : QB + n + 1, :]
+
+
 def merge_stats(pieces, stats):
-    for r in range(NA):
-        for half in range(2):
-            rh = 2 * r + half
-            parts = [(ref, 2 * ((r - t) % NA) + half) for t, ref in enumerate(pieces)]
-            norms = [ref[n : n + 1, :] for ref, n in parts]
-            means = [ref[QB + n : QB + n + 1, :] for ref, n in parts]
-            peak = functools.reduce(jnp.maximum, norms)
-            shares = [jnp.exp(norm - peak) for norm in norms]
-            total = sum(shares)
-            stats[rh, 0:1, :] = peak + jnp.log(total)
-            stats[rh, 1:2, :] = sum(share * mean for share, mean in zip(shares, means)) / total
-
-
-def backward_kernel(col, plan_ref, *refs):
+    for rh in range(QB):
+        norm, mean = combine([row_pair(ref, (rh - 2 * t) % QB) for t, ref in enumerate(pieces)])
+        stats[rh, 0:1, :] = norm
+        stats[rh, 1:2, :] = mean
+
+
+def backward_kernel(col, plan_ref, steps, *refs):
     (qs, cs, ct, kv_ref, peaks, exps), pieces, refs = refs[:6], refs[6:10], refs[10:]
     if col == 1:
-        (dq, dkv_ref), refs = refs[:2], refs[2:]
+        dq, dkv_ref, refs = refs[:2], refs[2], refs[3:]
     else:
-        (dq_before,), dq_out, (dkv_ref,), refs = refs[:1], refs[1:5], refs[5:6], refs[6:]
-        (dq, turned, sems), refs = refs[:3], refs[3:]
-    ks, vs, kt, dk, dv, dl, stats, p_a, p_b, d_a, d_b, pos, steps = refs
-    plain, count = list_steps(plan_ref, col, pos, steps)
+        dq_before, dq_out, dkv_ref, dq, refs = refs[:2], refs[2:6], refs[6], refs[7:9], refs[9:]
+        (turned, sems), refs = refs[:2], refs[2:]
+    (ks, vs, kt, stats), dk, dv, dl, refs = refs[:4], refs[4:6], refs[6:8], refs[8:10], refs[10:]
+    p_even, p_odd, d_even, d_odd, refs = refs[:2], refs[2:4], refs[4:6], refs[6:8], refs[8:]
+    (pos,) = refs
+    list_positions(plan_ref, col, pos)
+    kept_at, count = Part(steps, KEPT_AT), steps[COUNT_AT]
     sort_keys(plan_ref, col, kv_ref, ks, vs)
     turn(ks, kt)
-    for ref in (dk, dv, dl, p_b, d_b):
+    for ref in dk + dv + dl + p_odd + d_odd:
         ref[...] = jnp.zeros_like(ref)
-    dq[...] = jnp.zeros_like(dq) if col == 1 else dq_before[...]
+    for n in STREAMS:
+        dq[n][...] = jnp.zeros_like(dq[n]) if col == 1 else dq_before[n][...]
     merge_stats(pieces, stats)
 
-    def differ(t, p_ref, d_ref, masked):
-        v, rh, c, _ = step_of(steps, t)
+    def differ(n, t, p_refs, d_refs):
+        v, rh, c, _ = stream_step(steps, n, t)
         offset = offsets()
         limits = thresholds(plan_ref, pos, v, rh, c)
-        shares = [jnp.exp(peaks[t, 0:1, lanes] - stats[rh, 0:1, lanes]) for lanes in TILES]
+        kept = kept_at[v % SKIP]
+        shares = [jnp.exp(peaks[kept, 0:1, lanes] - stats[rh, 0:1, lanes]) for lanes in TILES]
+        shares = [jnp.where(v >= SKIP, 0.0, share) for share in shares]
         for first in range(0, STEP, 2):
             blocks = (first, first + 1)
-            late_sums = [dl[block_rows(c, i), :] for i in blocks]
+            late_sums = [dl[n][block_rows(c, i), :] for i in blocks]
             at = pl.ds(pl.multiple_of(c * CK + first * HALF, SHARD), 2 * HALF)
             for wide in WIDE_TILES:
                 grad = dot(vs[at, :], ct[rh, :, wide], NN)
-                for n, i in enumerate(blocks):
+                for m, i in enumerate(blocks):
                     rows = slice(i * HALF, (i + 1) * HALF)
                     for j in range(WIDE // SHARD):
                         here = slice(j * SHARD, (j + 1) * SHARD)
                         lanes = slice(wide.start + here.start, wide.start + here.stop)
-                        p = exps[t, rows, lanes].astype(f32) * shares[lanes.start // SHARD]
-                        d = p * (grad[n * HALF : (n + 1) * HALF, here] - stats[rh, 1:2, lanes])
-                        late = jnp.where(offset >= limits[i][1], d, 0.0) if masked else d
-                        late_sums[n] = late_sums[n] + late
-                        p_ref[rows, lanes] = p.astype(bf16)
-                        d_ref[rows, lanes] = d.astype(bf16)
-            for n, i in enumerate(blocks):
-                dl[block_rows(c, i), :] = late_sums[n]
-
-    def gather(t, p_ref, d_ref):
-        _, rh, c, at = step_of(steps, t)
-        dk[at, :] += dot(d_ref[...], qs[rh], NN)
-        dv[at, :] += dot(p_ref[...], cs[rh], NN)
-        dq[rh] += dot(turned_piece(kt, c), d_ref[...], NN)
-
-    def pair(masked, i, _):
+                        p = exps[kept, rows, lanes].astype(f32) * shares[lanes.start // SHARD]
+                        d = p * (grad[m * HALF : (m + 1) * HALF, here] - stats[rh, 1:2, lanes])
+                        late_sums[m] = late_sums[m] + jnp.where(offset >= limits[i][1], d, 0.0)
+                        p_refs[n][rows, lanes] = p.astype(bf16)
+                        d_refs[n][rows, lanes] = d.astype(bf16)
+            for m, i in enumerate(blocks):
+                dl[n][block_rows(c, i), :] = late_sums[m]
+
+    def gather(n, t, p_refs, d_refs):
+        _, rh, c, at = stream_step(steps, n, t)
+        dk[n][at, :] += dot(d_refs[n][...], qs[rh], NN)
+        dv[n][at, :] += dot(p_refs[n][...], cs[rh], NN)
+        dq[n][rh - n * QS] += dot(turned_piece(kt, c), d_refs[n][...], NN)
+
+    def both(work, *args):
+        for n in STREAMS:
+            work(n, *args)
+
+    def pair(i, _):
         t = 2 * i
-        gather(jnp.maximum(t - 1, 0), p_b, d_b)
-        differ(t, p_a, d_a, masked)
-        gather(t, p_a, d_a)
-        differ(t + 1, p_b, d_b, masked)
+        both(gather, jnp.maximum(t - 1, 0), p_odd, d_odd)
+        both(differ, t, p_even, d_even)
+        both(gather, t, p_even, d_even)
+        both(differ, t + 1, p_odd, d_odd)
         return 0
 
-    pairs = (count + 1) // 2
-    lax.fori_loop(0, plain // 2, functools.partial(pair, False), 0)
-    lax.fori_loop(plain // 2, pairs, functools.partial(pair, True), 0)
-    gather(2 * pairs - 1, p_b, d_b)
+    lax.fori_loop(0, count // 2, pair, 0)
+    both(gather, count - 1, p_odd, d_odd)
     copies = []
     if col == 0:
         for r, ref in enumerate(dq_out):
             for half in range(2):
-                rows = (dq[2 * r + half].T * SCALE).astype(bf16)
+                rows = (dq[r // 2][2 * (r % 2) + half].T * SCALE).astype(bf16)
                 turned[r, :, half * HALF : (half + 1) * HALF, :] = rows.reshape(HEADS, HALF, HD)
             copies.append(pltpu.make_async_copy(turned.at[r], ref, sems.at[r]))
             copies[-1].start()
@@ -350,9 +421,11 @@
         low = plan_ref[j, SLOT_AT + col]
         spots = [pl.ds(pl.multiple_of(slot * HALF, HALF), HALF) for slot in (low, SLOTS - 1 - low)]
         for half, at in enumerate(spots):
-            dkv_ref[j, half * HALF : (half + 1) * HALF, :] = (dk[at, :] * SCALE).astype(dkv_ref.dtype)
-            dkv_ref[j, SHARD + half * HALF : SHARD + (half + 1) * HALF, :] = dv[at, :].astype(dkv_ref.dtype)
-        late = jnp.concatenate([dl[at, :] for at in spots], axis=0)
+            key_sum = (dk[0][at, :] + dk[1][at, :]) * SCALE
+            value_sum = dv[0][at, :] + dv[1][at, :]
+            dkv_ref[j, half * HALF : (half + 1) * HALF, :] = key_sum.astype(dkv_ref.dtype)
+            dkv_ref[j, SHARD + half * HALF : SHARD + (half + 1) * HALF, :] = value_sum.astype(dkv_ref.dtype)
+        late = jnp.concatenate([dl[0][at, :] + dl[1][at, :] for at in spots], axis=0)
         total = jnp.sum(late.T, axis=0, keepdims=True)
         dkv_ref[j, 2 * SHARD : 2 * SHARD + 16, :] = jnp.concatenate(
             [total, jnp.zeros((15, SHARD), f32)], axis=0
@@ -424,7 +497,7 @@
     )(*pieces, w_out)
 
 
-def run_forward(col, plan, q, kv):
+def run_forward(col, plan, q, kv, lists=()):
     out_shape = (
         shaped((QB, HD, ROWS), f32),
         shaped((QB, 2, ROWS), f32),
@@ -436,7 +509,7 @@
     o, st, peaks, exps, *turned = pl.pallas_call(
         functools.partial(forward_kernel, col),
         out_shape=out_shape,
-        in_specs=[SMEM] + [VMEM] * (len(q) + 1),
+        in_specs=[SMEM] + [VMEM] * (len(q) + 1) + [SMEM] * len(lists),
         out_specs=(VMEM,) * len(out_shape),
         scratch_shapes=[
             pltpu.VMEM((KEYS, HD), bf16),
@@ -453,7 +526,7 @@
         compiler_params=grant(14),
         cost_estimate=cost(10),
         name=f"forward{col}",
-    )(plan, *q, kv)
+    )(plan, *q, kv, *lists)
     return (o, st), (peaks, exps), turned
 
 
@@ -472,15 +545,14 @@
     )(*sums, *cot)
 
 
-def run_backward(col, plan, rows, kv, exps, stats, dq_sum=None):
+def run_backward(col, plan, lists, rows, kv, exps, stats, dq_sum=()):
+    sums = [pltpu.VMEM((QS, HD, ROWS), f32)] * 2
     if col == 1:
-        more, scratch = (), []
-        out_shape = (shaped((QB, HD, ROWS), f32), shaped((NZ, KV_ROWS, HD), bf16))
-        out_specs = (VMEM, VMEM)
+        scratch = []
+        out_shape = (shaped((QS, HD, ROWS), f32),) * 2 + (shaped((NZ, KV_ROWS, HD), bf16),)
+        out_specs = (VMEM,) * 3
     else:
-        more = (dq_sum,)
-        scratch = [
-            pltpu.VMEM((QB, HD, ROWS), f32),
+        scratch = sums + [
             pltpu.VMEM((NA, HEADS, SHARD, HD), bf16),
             pltpu.SemaphoreType.DMA((NA,)),
         ]
@@ -489,24 +561,34 @@
     return pl.pallas_call(
         functools.partial(backward_kernel, col),
         out_shape=out_shape,
-        in_specs=[SMEM] + [VMEM] * (10 + len(more)),
+        in_specs=[SMEM] * 2 + [VMEM] * (10 + len(dq_sum)),
         out_specs=out_specs,
         scratch_shapes=scratch
         + [
             pltpu.VMEM((KEYS, HD), bf16),
             pltpu.VMEM((KEYS, HD), bf16),
             pltpu.VMEM((KEYS // SHARD, HD, SHARD), bf16),
-            pltpu.VMEM((KEYS, HD), f32),
-            pltpu.VMEM((KEYS, HD), f32),
-            pltpu.VMEM((KEYS, SHARD), f32),
             pltpu.VMEM((QB, 2, ROWS), f32),
         ]
-        + [pltpu.VMEM((CK, ROWS), bf16)] * 4
-        + [pltpu.SMEM((SLOTS,), i32), pltpu.SMEM((QB * PER_BLOCK + 3,), i32)],
-        compiler_params=grant(18),
+        + [pltpu.VMEM((KEYS, HD), f32)] * 6
+        + [pltpu.VMEM((CK, ROWS), bf16)] * 8
+        + [pltpu.SMEM((SLOTS,), i32)],
+        compiler_params=grant(22),
         cost_estimate=cost(15),
         name=f"backward{col}",
-    )(plan, *rows, kv, *exps, *stats, *more)
+    )(plan, lists, *rows, kv, *exps, *stats, *dq_sum)
+
+
+def run_lists(plan):
+    return pl.pallas_call(
+        lists_kernel,
+        out_shape=(shaped((LISTS,), i32),) * 2,
+        in_specs=[SMEM],
+        out_specs=(SMEM,) * 2,
+        compiler_params=grant(4),
+        cost_estimate=cost(2),
+        name="lists",
+    )(plan)
 
 
 def run_total(parts, logits):
@@ -551,13 +633,15 @@
     kv_other = swap(kv, "xl")
     cot_all = gather_y(cot)
     sums0, exps0, (qs, qt) = run_forward(0, plan, q_all, kv)
-    sums1, exps1, _ = run_forward(1, plan, (qt,), kv_other)
+    qt, plan = lax.optimization_barrier((qt, plan))
+    lists0, lists1 = run_lists(plan)
+    sums1, exps1, _ = run_forward(1, plan, (qt,), kv_other, (lists1,))
     stats, cs, ct = run_weigh((*sums0, *sums1), cot_all)
     rows = (qs, cs, ct)
     stats = gather_y(stats)
-    dq_sum, dkv_other = run_backward(1, plan, rows, kv_other, exps1, stats)
+    *dq_sum, dkv_other = run_backward(1, plan, lists1, rows, kv_other, exps1, stats)
     dkv_here = swap(dkv_other, "xl")
-    *dq, dkv = run_backward(0, plan, rows, kv, exps0, stats, dq_sum)
+    *dq, dkv = run_backward(0, plan, lists0, rows, kv, exps0, stats, dq_sum)
     dkv = (dkv + dkv_here.astype(f32)).astype(bf16)
     dkv = lax.all_to_all(dkv, "z", 0, 0, tiled=True)
     key_grad, value_grad, logit_grad = run_total(dkv, evict_logits)

time: 108 us -> 107 us (level)
  waiting for transfers between devices: 20.5 us -> 17.3 us
  Pallas kernels: 40.3 us -> 41.4 us
    ppermute x5, waiting for transfers between devices: 5.74 us -> 3.24 us  [swap(): return lax.ppermute(x, axis, [(0, 1), (1, 0)])]
    pallas_call x0 -> x1, Pallas kernels: none -> 2.27 us  [run_lists(): pl.pallas_call(lists_kernel, out_shape=(shaped((LISTS,), i32),) * 2, in_s...]
    pallas_call x2, Pallas kernels: 19.9 us -> 18.3 us  [run_backward(): pl.pallas_call(functools.partial(backward_kernel, col), out_shape=out_sha...]
  transfers between devices with their start and end apart: 19 -> 19, of which waited for: 7 -> 8; matrix products, arithmetic and copies ran while one was open for 1% -> 1% of each run, Pallas kernels for 27% -> 29%
where the time goes in v5:
time: 107 us; the launch traced here: 106 us
  Pallas kernels  41.4 us (39%)
  starting transfers between devices  39.9 us (37%)
  waiting for transfers between devices  17.3 us (16%)
  local copies, waits for them, and re-layouts  5.24 us (5%)
  other arithmetic  1.77 us (2%)
    ppermute x12, starting transfers between devices, from_y(): return lax.ppermute(x, 'y', [((i + r) % NA, i) for i in range(NA)])  18.8 us
    pallas_call x2, Pallas kernels, run_backward(): pl.pallas_call(functools.partial(backward_kernel, col), out_shape=out_sha...  18.3 us
    pallas_call x2, Pallas kernels, run_forward(): pl.pallas_call(functools.partial(forward_kernel, col), out_shape=out_shap...  14.6 us
    ppermute x12, waiting for transfers between devices, from_y(): return lax.ppermute(x, 'y', [((i + r) % NA, i) for i in range(NA)])  11.3 us
    all_to_all x1, starting transfers between devices, per_device(): lax.all_to_all(run_pack(keys, values, evict_logits), 'z', 0, 0, tiled=True)  8.47 us
    all_to_all x1, starting transfers between devices, per_device(): dkv = lax.all_to_all(dkv, 'z', 0, 0, tiled=True)  6.94 us
    ppermute x5, starting transfers between devices, swap(): return lax.ppermute(x, axis, [(0, 1), (1, 0)])  5.74 us
    unnamed x14, local copies, waits for them, and re-layouts  5.24 us
  transfers between devices with their start and end apart: 19, of which 8 were waited for; matrix products, arithmetic and copies ran while one was open for 1% of the time, Pallas kernels for 29%

profile of v5, /device:TPU:2, one launch (start us, length us, event | category | flops | bytes accessed | tf_op | source)
XLA Modules:
  0.0 106.3 jit_solution(4486374143893365863)
XLA Ops:
  0.6 2.2 %collective-permute-start.4 = (bf16[32,5120]{1,0:T(8,128)(2,1)}, bf16[32,5120]{1,0:T(8,128)(2,1)S(1)}, u32[]{:S(2)}, u32[]{:S(2)}) collective-permute-start(bf16[32,5120]{1,0:T(8,128)(2,1)} %g0.1), channel_id=1, source_target_pairs={{0,2},{2,0},{1,3},{3,1},{4,6},{6,4},{5,7},{7,5},{8,10},{10,8},{9,1... | collective-permute-start | bytes 983048 | tf_op jit(solution)/shard_map/ppermute | solution.py:614
  5.2 8.5 %all-to-all-start = ((bf16[8,272,128]{2,1,0:T(8,128)(2,1)}), bf16[8,272,128]{2,1,0:T(8,128)(2,1)S(1)}, u32[]{:S(2)}, u32[]{:S(2)}) async-start(bf16[8,272,128]{2,1,0:T(8,128)(2,1)} %pack.1), calls=%async_computation | async-start | bytes 1114112 | tf_op jit(solution)/shard_map/all_to_all | solution.py:628
  14.3 3.2 %collective-permute-start.1 = (bf16[8,128,128]{2,1,0:T(8,128)(2,1)S(1)}, bf16[8,128,128]{2,1,0:T(8,128)(2,1)S(1)}, u32[]{:S(2)}, u32[]{:S(2)}) collective-permute-start(bf16[8,128,128]{2,1,0:T(8,128)(2,1)S(1)} %copy-done.5), channel_id=1, source_target_pairs={{128,0},{192,64},{0,128},{64,192},{129,1},{193,65},{1,129},{65,193... | collective-permute-start | bytes 786440 | tf_op jit(solution)/shard_map/ppermute | solution.py:606
  17.5 1.1 collective-permute-start
  19.5 4.0 %copy-done.3 = bf16[1024,5120]{1,0:T(8,128)(2,1)S(1)} copy-done((bf16[1024,5120]{1,0:T(8,128)(2,1)S(1)}, bf16[1024,5120]{1,0:T(8,128)(2,1)}, u32[]{:S(2)}) %copy-start.3) | copy-done | bytes 10485784
  23.5 3.6 %cotangent.1.c0 = bf16[8,128,128]{2,1,0:T(8,128)(2,1)S(1)} custom-call(bf16[32,5120]{1,0:T(8,128)(2,1)S(1)} %copy-done.4, bf16[32,5120]{1,0:T(8,128)(2,1)S(1)} %collective-permute-done.4.g1, bf16[32,5120]{1,0:T(8,128)(2,1)S(1)} %collective-permute-done.5.g2, bf16[32,5120]{1,0:T(8,128)(2,1)S(1)} %collective-permute-done.6.g3, bf16[1024,5120]{1,0:T(8,128)(2,1)S(1)} %copy-done.3), custom_call_target="tpu_custom_call" | custom-call | flops 5000000000 | bytes 1048576 | tf_op jit(solution)/shard_map/cotangent/pallas_call | solution.py:488
  27.8 3.0 %collective-permute-start.8 = (bf16[8,128,128]{2,1,0:T(8,128)(2,1)S(1)}, bf16[8,128,128]{2,1,0:T(8,128)(2,1)S(1)}, u32[]{:S(2)}, u32[]{:S(2)}) collective-permute-start(bf16[8,128,128]{2,1,0:T(8,128)(2,1)S(1)} %cotangent.1.c0), channel_id=1, source_target_pairs={{128,0},{192,64},{0,128},{64,192},{129,1},{193,65},{1,129},{65,193... | collective-permute-start | bytes 786440 | tf_op jit(solution)/shard_map/ppermute | solution.py:606
  31.6 1.4 %collective-permute-start.3 = (bf16[8,272,128]{2,1,0:T(8,128)(2,1)S(1)}, bf16[8,272,128]{2,1,0:T(8,128)(2,1)S(1)}, u32[]{:S(2)}, u32[]{:S(2)}) collective-permute-start(bf16[8,272,128]{2,1,0:T(8,128)(2,1)S(1)} %all-to-all-done.refs_4_.refs_3_), channel_id=1, source_target_pairs={{0,4},{4,0},{1,5},{5,1},{2,6},{6,2},{3,7},{7,3},{8,12},{12,8},{9,1... | collective-permute-start | bytes 1671176 | tf_op jit(solution)/shard_map/ppermute | solution.py:614
  33.0 7.5 %forward0.1 = (f32[8,128,512]{2,1,0:T(8,128)S(1)}, f32[8,2,512]{2,1,0:T(2,128)S(1)}, f32[20,1,512]{2,1,0:T(1,128)S(1)}, bf16[20,256,512]{2,1,0:T(8,128)(2,1)S(1)...) custom-call(s32[8,128]{1,0:T(8,128)S(1)} %plan.1.plan_ref, bf16[8,128,128]{2,1,0:T(8,128)(2,1)S(1)} %copy-done.5, ...), custom_call_target="tpu_custom_call" | custom-call | flops 10000000000 | bytes 1048576 | tf_op jit(solution)/shard_map/forward0/pallas_call | solution.py:509
  40.5 2.3 %lists.1 = (s32[256]{0:T(256)S(1)}, s32[256]{0:T(256)S(1)}) custom-call(s32[8,128]{1,0:T(8,128)S(1)} %plan.1.plan_ref), custom_call_target="tpu_custom_call" | custom-call | flops 2000000000 | bytes 1048576 | tf_op jit(solution)/shard_map/lists/pallas_call | solution.py:583
  42.8 2.9 %collective-permute-done.3.refs_1_.refs_3_ = bf16[8,272,128]{2,1,0:T(8,128)(2,1)S(1)} collective-permute-done((bf16[8,272,128]{2,1,0:T(8,128)(2,1)S(1)}, bf16[8,272,128]{2,1,0:T(8,128)(2,1)S(1)}, u32[]{:S(2)}, u32[]{:S(2)}) %collective-permute-start.3) | collective-permute-done | bytes 557088 | tf_op jit(solution)/shard_map/ppermute | solution.py:614
  45.7 7.1 %forward1.1 = (f32[8,128,512]{2,1,0:T(8,128)S(1)}, f32[8,2,512]{2,1,0:T(2,128)S(1)}, f32[20,1,512]{2,1,0:T(1,128)S(1)}, bf16[20,256,512]{2,1,0:T(8,128)(2,1)S(1)}) custom-call(s32[8,128]{1,0:T(8,128)S(1)} %plan.1.plan_ref, bf16[8,128,512]{2,1,0:T(8,128)(2,1)S(1)} %get-tuple-element.42.refs_0_, ...), custom_call_target="tpu_custom_call" | custom-call | flops 10000000000 | bytes 1048576 | tf_op jit(solution)/shard_map/forward1/pallas_call | solution.py:509
  53.6 1.0 collective-permute-start.12
  54.6 3.5 %collective-permute-start.11 = (f32[16,512]{1,0:T(8,128)S(1)}, f32[16,512]{1,0:T(8,128)S(1)}, u32[]{:S(2)}, u32[]{:S(2)}) collective-permute-start(f32[16,512]{1,0:T(8,128)S(1)} %get-tuple-element.50.refs_6_), channel_id=1, source_target_pairs={{128,0},{192,64},{0,128},{64,192},{129,1},{193,65},{1,129},{65,193... | collective-permute-start | bytes 98312 | tf_op jit(solution)/shard_map/ppermute | solution.py:606
  58.1 1.4 %collective-permute-start.10 = (f32[16,512]{1,0:T(8,128)S(1)}, f32[16,512]{1,0:T(8,128)S(1)}, u32[]{:S(2)}, u32[]{:S(2)}) collective-permute-start(f32[16,512]{1,0:T(8,128)S(1)} %get-tuple-element.50.refs_6_), channel_id=1, source_target_pairs={{64,0},{128,64},{192,128},{0,192},{65,1},{129,65},{193,129},{1,193... | collective-permute-start | bytes 98312 | tf_op jit(solution)/shard_map/ppermute | solution.py:606
  60.4 1.7 %collective-permute-done.10.refs_7_ = f32[16,512]{1,0:T(8,128)S(1)} collective-permute-done((f32[16,512]{1,0:T(8,128)S(1)}, f32[16,512]{1,0:T(8,128)S(1)}, u32[]{:S(2)}, u32[]{:S(2)}) %collective-permute-start.10) | collective-permute-done | bytes 32800 | tf_op jit(solution)/shard_map/ppermute | solution.py:606
  62.1 8.7 %backward1.1 = (f32[4,128,512]{2,1,0:T(8,128)S(1)}, f32[4,128,512]{2,1,0:T(8,128)S(1)}, bf16[8,272,128]{2,1,0:T(8,128)(2,1)S(1)}) custom-call(s32[8,128]{1,0:T(8,128)S(1)} %plan.1.plan_ref, s32[256]{0:T(256)S(1)} %get-tuple-element.43.refs_2_.steps, bf16[8,512,128]{2,1,0:T(8,128)(2,1)S(1)} %get-tuple-element.39.refs_0_, ...), custom_call_target="tpu_custom_call" | custom-call | flops 15000000512 | bytes 1048576 | tf_op jit(solution)/shard_map/backward1/pallas_call | solution.py:561
  70.8 1.5 %collective-permute-start.16 = (bf16[8,272,128]{2,1,0:T(8,128)(2,1)S(1)}, bf16[8,272,128]{2,1,0:T(8,128)(2,1)S(1)}, u32[]{:S(2)}, u32[]{:S(2)}) collective-permute-start(bf16[8,272,128]{2,1,0:T(8,128)(2,1)S(1)} %get-tuple-element.60), channel_id=1, source_target_pairs={{0,4},{4,0},{1,5},{5,1},{2,6},{6,2},{3,7},{7,3},{8,12},{12,8},{9,1... | collective-permute-start | bytes 1671176 | tf_op jit(solution)/shard_map/ppermute | solution.py:614
  72.3 9.6 %backward0.1 = (bf16[8,128,128]{2,1,0:T(8,128)(2,1)S(1)}, bf16[8,128,128]{2,1,0:T(8,128)(2,1)S(1)}, bf16[8,128,128]{2,1,0:T(8,128)(2,1)S(1)}, bf16[8,128,128]{2,1,0:T(8,128)(2,1)S(1)}, f32[8,272,128]{2,1,0:T(8,128)S(1)}) custom-call(s32[8,128]{1,0:T(8,128)S(1)} %plan.1.plan_ref, s32[256]{0:T(256)S(1)} %get-tuple-element.38.steps, ...), custom_call_target="tpu_custom_call" | custom-call | flops 15000000512 | bytes 1048576 | tf_op jit(solution)/shard_map/backward0/pallas_call | solution.py:561
  83.2 6.9 %all-to-all-start.1 = ((bf16[8,272,128]{2,1,0:T(8,128)(2,1)}), bf16[8,272,128]{2,1,0:T(8,128)(2,1)S(1)}, u32[]{:S(2)}, u32[]{:S(2)}) async-start(bf16[8,272,128]{2,1,0:T(8,128)(2,1)} %add_convert_fusion), calls=%async_computation.1 | async-start | bytes 1114112 | tf_op jit(solution)/shard_map/all_to_all | solution.py:646
  90.2 2.4 %collective-permute-start.14 = (bf16[8,128,128]{2,1,0:T(8,128)(2,1)S(1)}, bf16[8,128,128]{2,1,0:T(8,128)(2,1)S(1)}, u32[]{:S(2)}, u32[]{:S(2)}) collective-permute-start(bf16[8,128,128]{2,1,0:T(8,128)(2,1)S(1)} %get-tuple-element.57), channel_id=1, source_target_pairs={{128,0},{192,64},{0,128},{64,192},{129,1},{193,65},{1,129},{65,193... | collective-permute-start | bytes 786440 | tf_op jit(solution)/shard_map/ppermute | solution.py:606
  92.5 1.5 %collective-permute-start.15 = (bf16[8,128,128]{2,1,0:T(8,128)(2,1)S(1)}, bf16[8,128,128]{2,1,0:T(8,128)(2,1)S(1)}, u32[]{:S(2)}, u32[]{:S(2)}) collective-permute-start(bf16[8,128,128]{2,1,0:T(8,128)(2,1)S(1)} %get-tuple-element.58), channel_id=1, source_target_pairs={{64,0},{128,64},{192,128},{0,192},{65,1},{129,65},{193,129},{1,193... | collective-permute-start | bytes 786440 | tf_op jit(solution)/shard_map/ppermute | solution.py:606
  94.0 8.1 %collective-permute-done.13 = bf16[8,128,128]{2,1,0:T(8,128)(2,1)S(1)} collective-permute-done((bf16[8,128,128]{2,1,0:T(8,128)(2,1)S(1)}, bf16[8,128,128]{2,1,0:T(8,128)(2,1)S(1)}, u32[]{:S(2)}, u32[]{:S(2)}) %collective-permute-start.13) | collective-permute-done | bytes 262176 | tf_op jit(solution)/shard_map/ppermute | solution.py:606
  103.6 2.1 %all-to-all-done.1.parts_ref = bf16[8,272,128]{2,1,0:T(8,128)(2,1)S(1)} async-done(((bf16[8,272,128]{2,1,0:T(8,128)(2,1)}), bf16[8,272,128]{2,1,0:T(8,128)(2,1)S(1)}, u32[]{:S(2)}, u32[]{:S(2)}) %all-to-all-start.1) | async-done | bytes 557088 | tf_op jit(solution)/shard_map/all_to_all | solution.py:646
  (40 shorter events, 10.5 us)
Async XLA Ops:
  0.6 13.2 %collective-permute-start.4 = (bf16[32,5120]{1,0:T(8,128)(2,1)}, bf16[32,5120]{1,0:T(8,128)(2,1)S(1)}, u32[]{:S(2)}, u32[]{:S(2)}) collective-permute-start(bf16[32,5120]{1,0:T(8,128)(2,1)} %g0.1), channel_id=1, source_target_pairs={{0,2},{2,0},{1,3},{3,1},{4,6},{6,4},{5,7},{7,5},{8,10},{10,8},{9,1... | collective-permute-start | bytes 983048 | tf_op jit(solution)/shard_map/ppermute | solution.py:614
  3.5 0.8 copy-start.1
  3.5 0.8 copy-start.2
  3.5 10.1 %copy-start.4 = (bf16[32,5120]{1,0:T(8,128)(2,1)S(1)}, bf16[32,5120]{1,0:T(8,128)(2,1)}, u32[]{:S(2)}) copy-start(bf16[32,5120]{1,0:T(8,128)(2,1)} %g0.1) | copy-start | bytes 983044
  3.5 10.7 %copy-start.5 = (bf16[8,128,128]{2,1,0:T(8,128)(2,1)S(1)}, bf16[8,128,128]{2,1,0:T(8,128)(2,1)}, u32[]{:S(2)}) copy-start(bf16[8,128,128]{2,1,0:T(8,128)(2,1)} %refs_0_.1) | copy-start | bytes 786436
  5.2 26.4 %all-to-all-start = ((bf16[8,272,128]{2,1,0:T(8,128)(2,1)}), bf16[8,272,128]{2,1,0:T(8,128)(2,1)S(1)}, u32[]{:S(2)}, u32[]{:S(2)}) async-start(bf16[8,272,128]{2,1,0:T(8,128)(2,1)} %pack.1), calls=%async_computation | async-start | bytes 1114112 | tf_op jit(solution)/shard_map/all_to_all | solution.py:628
  13.7 5.8 %collective-permute-start.5 = (bf16[32,5120]{1,0:T(8,128)(2,1)S(1)}, bf16[32,5120]{1,0:T(8,128)(2,1)S(1)}, u32[]{:S(2)}, u32[]{:S(2)}) collective-permute-start(bf16[32,5120]{1,0:T(8,128)(2,1)S(1)} %copy-done.4), channel_id=1, source_target_pairs={{0,1},{1,0},{2,3},{3,2},{4,5},{5,4},{6,7},{7,6},{8,9},{9,8},{10,11... | collective-permute-start | bytes 983048 | tf_op jit(solution)/shard_map/ppermute | solution.py:614
  13.8 5.7 %collective-permute-start.6 = (bf16[32,5120]{1,0:T(8,128)(2,1)S(1)}, bf16[32,5120]{1,0:T(8,128)(2,1)S(1)}, u32[]{:S(2)}, u32[]{:S(2)}) collective-permute-start(bf16[32,5120]{1,0:T(8,128)(2,1)S(1)} %collective-permute-done.4.g1), channel_id=1, source_target_pairs={{0,1},{1,0},{2,3},{3,2},{4,5},{5,4},{6,7},{7,6},{8,9},{9,8},{10,11... | collective-permute-start | bytes 983048 | tf_op jit(solution)/shard_map/ppermute | solution.py:614
  14.3 16.6 %collective-permute-start.1 = (bf16[8,128,128]{2,1,0:T(8,128)(2,1)S(1)}, bf16[8,128,128]{2,1,0:T(8,128)(2,1)S(1)}, u32[]{:S(2)}, u32[]{:S(2)}) collective-permute-start(bf16[8,128,128]{2,1,0:T(8,128)(2,1)S(1)} %copy-done.5), channel_id=1, source_target_pairs={{128,0},{192,64},{0,128},{64,192},{129,1},{193,65},{1,129},{65,193... | collective-permute-start | bytes 786440 | tf_op jit(solution)/shard_map/ppermute | solution.py:606
  17.5 13.4 %collective-permute-start = (bf16[8,128,128]{2,1,0:T(8,128)(2,1)S(1)}, bf16[8,128,128]{2,1,0:T(8,128)(2,1)S(1)}, u32[]{:S(2)}, u32[]{:S(2)}) collective-permute-start(bf16[8,128,128]{2,1,0:T(8,128)(2,1)S(1)} %copy-done.5), channel_id=1, source_target_pairs={{64,0},{128,64},{192,128},{0,192},{65,1},{129,65},{193,129},{1,193... | collective-permute-start | bytes 786440 | tf_op jit(solution)/shard_map/ppermute | solution.py:606
  18.5 14.5 %collective-permute-start.2 = (bf16[8,128,128]{2,1,0:T(8,128)(2,1)S(1)}, bf16[8,128,128]{2,1,0:T(8,128)(2,1)S(1)}, u32[]{:S(2)}, u32[]{:S(2)}) collective-permute-start(bf16[8,128,128]{2,1,0:T(8,128)(2,1)S(1)} %copy-done.5), channel_id=1, source_target_pairs={{192,0},{0,64},{64,128},{128,192},{193,1},{1,65},{65,129},{129,193... | collective-permute-start | bytes 786440 | tf_op jit(solution)/shard_map/ppermute | solution.py:606
  19.5 4.0 %copy-start.3 = (bf16[1024,5120]{1,0:T(8,128)(2,1)S(1)}, bf16[1024,5120]{1,0:T(8,128)(2,1)}, u32[]{:S(2)}) copy-start(bf16[1024,5120]{1,0:T(8,128)(2,1)} %w_ref.1) | copy-start | bytes 31457284
  27.1 25.7 %collective-permute-start.9 = (bf16[8,128,128]{2,1,0:T(8,128)(2,1)S(1)}, bf16[8,128,128]{2,1,0:T(8,128)(2,1)S(1)}, u32[]{:S(2)}, u32[]{:S(2)}) collective-permute-start(bf16[8,128,128]{2,1,0:T(8,128)(2,1)S(1)} %cotangent.1.c0), channel_id=1, source_target_pairs={{192,0},{0,64},{64,128},{128,192},{193,1},{1,65},{65,129},{129,193... | collective-permute-start | bytes 786440 | tf_op jit(solution)/shard_map/ppermute | solution.py:606
  27.8 25.0 %collective-permute-start.8 = (bf16[8,128,128]{2,1,0:T(8,128)(2,1)S(1)}, bf16[8,128,128]{2,1,0:T(8,128)(2,1)S(1)}, u32[]{:S(2)}, u32[]{:S(2)}) collective-permute-start(bf16[8,128,128]{2,1,0:T(8,128)(2,1)S(1)} %cotangent.1.c0), channel_id=1, source_target_pairs={{128,0},{192,64},{0,128},{64,192},{129,1},{193,65},{1,129},{65,193... | collective-permute-start | bytes 786440 | tf_op jit(solution)/shard_map/ppermute | solution.py:606
  30.9 21.9 %collective-permute-start.7 = (bf16[8,128,128]{2,1,0:T(8,128)(2,1)S(1)}, bf16[8,128,128]{2,1,0:T(8,128)(2,1)S(1)}, u32[]{:S(2)}, u32[]{:S(2)}) collective-permute-start(bf16[8,128,128]{2,1,0:T(8,128)(2,1)S(1)} %cotangent.1.c0), channel_id=1, source_target_pairs={{64,0},{128,64},{192,128},{0,192},{65,1},{129,65},{193,129},{1,193... | collective-permute-start | bytes 786440 | tf_op jit(solution)/shard_map/ppermute | solution.py:606
  31.6 14.1 %collective-permute-start.3 = (bf16[8,272,128]{2,1,0:T(8,128)(2,1)S(1)}, bf16[8,272,128]{2,1,0:T(8,128)(2,1)S(1)}, u32[]{:S(2)}, u32[]{:S(2)}) collective-permute-start(bf16[8,272,128]{2,1,0:T(8,128)(2,1)S(1)} %all-to-all-done.refs_4_.refs_3_), channel_id=1, source_target_pairs={{0,4},{4,0},{1,5},{5,1},{2,6},{6,2},{3,7},{7,3},{8,12},{12,8},{9,1... | collective-permute-start | bytes 1671176 | tf_op jit(solution)/shard_map/ppermute | solution.py:614
  53.6 5.9 %collective-permute-start.12 = (f32[16,512]{1,0:T(8,128)S(1)}, f32[16,512]{1,0:T(8,128)S(1)}, u32[]{:S(2)}, u32[]{:S(2)}) collective-permute-start(f32[16,512]{1,0:T(8,128)S(1)} %get-tuple-element.50.refs_6_), channel_id=1, source_target_pairs={{192,0},{0,64},{64,128},{128,192},{193,1},{1,65},{65,129},{129,193... | collective-permute-start | bytes 98312 | tf_op jit(solution)/shard_map/ppermute | solution.py:606
  54.6 5.8 %collective-permute-start.11 = (f32[16,512]{1,0:T(8,128)S(1)}, f32[16,512]{1,0:T(8,128)S(1)}, u32[]{:S(2)}, u32[]{:S(2)}) collective-permute-start(f32[16,512]{1,0:T(8,128)S(1)} %get-tuple-element.50.refs_6_), channel_id=1, source_target_pairs={{128,0},{192,64},{0,128},{64,192},{129,1},{193,65},{1,129},{65,193... | collective-permute-start | bytes 98312 | tf_op jit(solution)/shard_map/ppermute | solution.py:606
  58.1 3.9 %collective-permute-start.10 = (f32[16,512]{1,0:T(8,128)S(1)}, f32[16,512]{1,0:T(8,128)S(1)}, u32[]{:S(2)}, u32[]{:S(2)}) collective-permute-start(f32[16,512]{1,0:T(8,128)S(1)} %get-tuple-element.50.refs_6_), channel_id=1, source_target_pairs={{64,0},{128,64},{192,128},{0,192},{65,1},{129,65},{193,129},{1,193... | collective-permute-start | bytes 98312 | tf_op jit(solution)/shard_map/ppermute | solution.py:606
  70.8 11.5 %collective-permute-start.16 = (bf16[8,272,128]{2,1,0:T(8,128)(2,1)S(1)}, bf16[8,272,128]{2,1,0:T(8,128)(2,1)S(1)}, u32[]{:S(2)}, u32[]{:S(2)}) collective-permute-start(bf16[8,272,128]{2,1,0:T(8,128)(2,1)S(1)} %get-tuple-element.60), channel_id=1, source_target_pairs={{0,4},{4,0},{1,5},{5,1},{2,6},{6,2},{3,7},{7,3},{8,12},{12,8},{9,1... | collective-permute-start | bytes 1671176 | tf_op jit(solution)/shard_map/ppermute | solution.py:614
  83.2 22.4 %all-to-all-start.1 = ((bf16[8,272,128]{2,1,0:T(8,128)(2,1)}), bf16[8,272,128]{2,1,0:T(8,128)(2,1)S(1)}, u32[]{:S(2)}, u32[]{:S(2)}) async-start(bf16[8,272,128]{2,1,0:T(8,128)(2,1)} %add_convert_fusion), calls=%async_computation.1 | async-start | bytes 1114112 | tf_op jit(solution)/shard_map/all_to_all | solution.py:646
  90.2 11.9 %collective-permute-start.13 = (bf16[8,128,128]{2,1,0:T(8,128)(2,1)S(1)}, bf16[8,128,128]{2,1,0:T(8,128)(2,1)S(1)}, u32[]{:S(2)}, u32[]{:S(2)}) collective-permute-start(bf16[8,128,128]{2,1,0:T(8,128)(2,1)S(1)} %get-tuple-element.56), channel_id=1, source_target_pairs={{192,0},{0,64},{64,128},{128,192},{193,1},{1,65},{65,129},{129,193... | collective-permute-start | bytes 786440 | tf_op jit(solution)/shard_map/ppermute | solution.py:606
  90.2 11.9 %collective-permute-start.14 = (bf16[8,128,128]{2,1,0:T(8,128)(2,1)S(1)}, bf16[8,128,128]{2,1,0:T(8,128)(2,1)S(1)}, u32[]{:S(2)}, u32[]{:S(2)}) collective-permute-start(bf16[8,128,128]{2,1,0:T(8,128)(2,1)S(1)} %get-tuple-element.57), channel_id=1, source_target_pairs={{128,0},{192,64},{0,128},{64,192},{129,1},{193,65},{1,129},{65,193... | collective-permute-start | bytes 786440 | tf_op jit(solution)/shard_map/ppermute | solution.py:606
  92.5 10.2 %collective-permute-start.15 = (bf16[8,128,128]{2,1,0:T(8,128)(2,1)S(1)}, bf16[8,128,128]{2,1,0:T(8,128)(2,1)S(1)}, u32[]{:S(2)}, u32[]{:S(2)}) collective-permute-start(bf16[8,128,128]{2,1,0:T(8,128)(2,1)S(1)} %get-tuple-element.58), channel_id=1, source_target_pairs={{64,0},{128,64},{192,128},{0,192},{65,1},{129,65},{193,129},{1,193... | collective-permute-start | bytes 786440 | tf_op jit(solution)/shard_map/ppermute | solution.py:606
  (2 other events, 1.4 us)

commit v6 on v5

--- a/solution.py
+++ b/solution.py
@@ -76,11 +76,8 @@
     return sum(jnp.where(at == n, value, 0.0) for n, value in columns.items()).astype(i32)
 
 
-def plan_kernel(where, blocks_ref, plan_ref):
+def pack_kernel(where, k_ref, v_ref, logit_ref, blocks_ref, out_ref, plan_ref):
     plan_ref[...] = plan_of(blocks_ref[...], *where())
-
-
-def pack_kernel(k_ref, v_ref, logit_ref, out_ref):
     logit = logit_ref[...]
     penalty = jnp.maximum(logit, 0.0) + jnp.log(1.0 + jnp.exp(-jnp.abs(logit)))
     upper = penalty.astype(bf16).astype(f32)
@@ -343,20 +340,24 @@
         stats[rh, 1:2, :] = mean
 
 
+def ready_kernel(plan_ref, kv0, kv1, vs0, kt0, vs1, kt1, ks):
+    for col, kv_ref, vs, kt in ((0, kv0, vs0, kt0), (1, kv1, vs1, kt1)):
+        sort_keys(plan_ref, col, kv_ref, ks, vs)
+        turn(ks, kt)
+
+
 def backward_kernel(col, plan_ref, steps, *refs):
-    (qs, cs, ct, kv_ref, peaks, exps), pieces, refs = refs[:6], refs[6:10], refs[10:]
+    (qs, cs, ct, vs, kt, peaks, exps), pieces, refs = refs[:7], refs[7:11], refs[11:]
     if col == 1:
         dq, dkv_ref, refs = refs[:2], refs[2], refs[3:]
     else:
         dq_before, dq_out, dkv_ref, dq, refs = refs[:2], refs[2:6], refs[6], refs[7:9], refs[9:]
         (turned, sems), refs = refs[:2], refs[2:]
-    (ks, vs, kt, stats), dk, dv, dl, refs = refs[:4], refs[4:6], refs[6:8], refs[8:10], refs[10:]
+    stats, dk, dv, dl, refs = refs[0], refs[1:3], refs[3:5], refs[5:7], refs[7:]
     p_even, p_odd, d_even, d_odd, refs = refs[:2], refs[2:4], refs[4:6], refs[6:8], refs[8:]
     (pos,) = refs
     list_positions(plan_ref, col, pos)
     kept_at, count = Part(steps, KEPT_AT), steps[COUNT_AT]
-    sort_keys(plan_ref, col, kv_ref, ks, vs)
-    turn(ks, kt)
     for ref in dk + dv + dl + p_odd + d_odd:
         ref[...] = jnp.zeros_like(ref)
     for n in STREAMS:
@@ -461,27 +462,14 @@
     return pl.CostEstimate(flops=int(us * 1e9), bytes_accessed=2**20, transcendentals=0)
 
 
-def run_plan(where, block_order):
+def run_pack(where, keys, values, logits, block_order):
     return pl.pallas_call(
-        functools.partial(plan_kernel, where),
-        out_shape=shaped((8, SHARD), i32),
-        in_specs=[VMEM],
-        out_specs=VMEM,
-        compiler_params=grant(4),
-        cost_estimate=cost(12),
-        name="plan",
-    )(block_order.T)
-
-
-def run_pack(keys, values, logits):
-    return pl.pallas_call(
-        pack_kernel,
-        out_shape=shaped((NZ, KV_ROWS, HD), bf16),
-        in_specs=[VMEM] * 3,
-        out_specs=VMEM,
-        compiler_params=grant(4),
+        functools.partial(pack_kernel, where),
+        out_shape=(shaped((NZ, KV_ROWS, HD), bf16), shaped((8, SHARD), i32)),
+        in_specs=[VMEM] * 4,
+        out_specs=(VMEM, VMEM),
         name="pack",
-    )(keys, values, logits)
+    )(keys, values, logits, block_order.T)
 
 
 def run_cotangent(where, pieces, w_out):
@@ -545,7 +533,7 @@
     )(*sums, *cot)
 
 
-def run_backward(col, plan, lists, rows, kv, exps, stats, dq_sum=()):
+def run_backward(col, plan, lists, rows, ready, exps, stats, dq_sum=()):
     sums = [pltpu.VMEM((QS, HD, ROWS), f32)] * 2
     if col == 1:
         scratch = []
@@ -561,22 +549,17 @@
     return pl.pallas_call(
         functools.partial(backward_kernel, col),
         out_shape=out_shape,
-        in_specs=[SMEM] * 2 + [VMEM] * (10 + len(dq_sum)),
+        in_specs=[SMEM] * 2 + [VMEM] * (11 + len(dq_sum)),
         out_specs=out_specs,
         scratch_shapes=scratch
-        + [
-            pltpu.VMEM((KEYS, HD), bf16),
-            pltpu.VMEM((KEYS, HD), bf16),
-            pltpu.VMEM((KEYS // SHARD, HD, SHARD), bf16),
-            pltpu.VMEM((QB, 2, ROWS), f32),
-        ]
+        + [pltpu.VMEM((QB, 2, ROWS), f32)]
         + [pltpu.VMEM((KEYS, HD), f32)] * 6
         + [pltpu.VMEM((CK, ROWS), bf16)] * 8
         + [pltpu.SMEM((SLOTS,), i32)],
         compiler_params=grant(22),
         cost_estimate=cost(15),
         name=f"backward{col}",
-    )(plan, lists, *rows, kv, *exps, *stats, *dq_sum)
+    )(plan, lists, *rows, *ready, *exps, *stats, *dq_sum)
 
 
 def run_lists(plan):
@@ -591,6 +574,21 @@
     )(plan)
 
 
+def run_ready(plan, kv0, kv1):
+    shapes = (shaped((KEYS, HD), bf16), shaped((KEYS // SHARD, HD, SHARD), bf16))
+    out = pl.pallas_call(
+        ready_kernel,
+        out_shape=shapes * 2,
+        in_specs=[SMEM] + [VMEM] * 2,
+        out_specs=(VMEM,) * 4,
+        scratch_shapes=[pltpu.VMEM((KEYS, HD), bf16)],
+        compiler_params=grant(4),
+        cost_estimate=cost(2),
+        name="ready",
+    )(plan, kv0, kv1)
+    return out[:2], out[2:]
+
+
 def run_total(parts, logits):
     return pl.pallas_call(
         total_kernel,
@@ -623,9 +621,8 @@
 
 
 def per_device(queries, keys, values, evict_logits, block_order, grad_y, w_out):
-    plan = run_plan(place, block_order)
-    keys, plan = lax.optimization_barrier((keys, plan))
-    kv = lax.all_to_all(run_pack(keys, values, evict_logits), "z", 0, 0, tiled=True)
+    packed, plan = run_pack(place, keys, values, evict_logits, block_order)
+    kv = lax.all_to_all(packed, "z", 0, 0, tiled=True)
     over = swap(grad_y, "xh")
     pieces = (grad_y, over, swap(grad_y, "core"), swap(over, "core"))
     q_all = gather_y(queries)
@@ -638,10 +635,12 @@
     sums1, exps1, _ = run_forward(1, plan, (qt,), kv_other, (lists1,))
     stats, cs, ct = run_weigh((*sums0, *sums1), cot_all)
     rows = (qs, cs, ct)
+    stats, kv_other = lax.optimization_barrier((stats, kv_other))
+    ready0, ready1 = run_ready(plan, kv, kv_other)
     stats = gather_y(stats)
-    *dq_sum, dkv_other = run_backward(1, plan, lists1, rows, kv_other, exps1, stats)
+    *dq_sum, dkv_other = run_backward(1, plan, lists1, rows, ready1, exps1, stats)
     dkv_here = swap(dkv_other, "xl")
-    *dq, dkv = run_backward(0, plan, lists0, rows, kv, exps0, stats, dq_sum)
+    *dq, dkv = run_backward(0, plan, lists0, rows, ready0, exps0, stats, dq_sum)
     dkv = (dkv + dkv_here.astype(f32)).astype(bf16)
     dkv = lax.all_to_all(dkv, "z", 0, 0, tiled=True)
     key_grad, value_grad, logit_grad = run_total(dkv, evict_logits)

time: 107 us -> 106 us (level)
  waiting for transfers between devices: 17.3 us -> 14.4 us
  Pallas kernels: 41.4 us -> 44 us
    ppermute x12, waiting for transfers between devices: 11.3 us -> 9.75 us  [from_y(): return lax.ppermute(x, 'y', [((i + r) % NA, i) for i in range(NA)])]
    pallas_call x2, Pallas kernels: 1.09 us -> 2.61 us  [the longest x1 1.74 us: run_pack(): pl.pallas_call(functools.partial(pack_kernel, where), out_shape=(shaped((...]
    unnamed x14 -> x10, local copies, waits for them, and re-layouts: 5.24 us -> 4.96 us
  transfers between devices with their start and end apart: 19 -> 19, of which waited for: 8 -> 6; matrix products, arithmetic and copies ran while one was open for 1% -> 1% of each run, Pallas kernels for 29% -> 32%
where the time goes in v6:
time: 106 us
  Pallas kernels  44 us (42%)
  starting transfers between devices  39.9 us (38%)
  waiting for transfers between devices  14.4 us (14%)
  local copies, waits for them, and re-layouts  4.96 us (5%)
  other arithmetic  1.77 us (2%)
    ppermute x12, starting transfers between devices, from_y(): return lax.ppermute(x, 'y', [((i + r) % NA, i) for i in range(NA)])  19.3 us
    pallas_call x2, Pallas kernels, run_backward(): pl.pallas_call(functools.partial(backward_kernel, col), out_shape=out_sha...  19.2 us
    pallas_call x2, Pallas kernels, run_forward(): pl.pallas_call(functools.partial(forward_kernel, col), out_shape=out_shap...  14.9 us
    ppermute x12, waiting for transfers between devices, from_y(): return lax.ppermute(x, 'y', [((i + r) % NA, i) for i in range(NA)])  9.75 us
    all_to_all x1, starting transfers between devices, per_device(): kv = lax.all_to_all(packed, 'z', 0, 0, tiled=True)  8.6 us
    all_to_all x1, starting transfers between devices, per_device(): dkv = lax.all_to_all(dkv, 'z', 0, 0, tiled=True)  6.26 us
    ppermute x5, starting transfers between devices, swap(): return lax.ppermute(x, axis, [(0, 1), (1, 0)])  5.76 us
    unnamed x10, local copies, waits for them, and re-layouts  4.96 us
  transfers between devices with their start and end apart: 19, of which 6 were waited for; matrix products, arithmetic and copies ran while one was open for 1% of the time, Pallas kernels for 32%

profile of v6, /device:TPU:2, one launch (start us, length us, event | category | flops | bytes accessed | tf_op | source)
XLA Modules:
  0.0 105.8 jit_solution(4211002513628481988)
XLA Ops:
  0.6 2.2 %collective-permute-start.4 = (bf16[32,5120]{1,0:T(8,128)(2,1)}, bf16[32,5120]{1,0:T(8,128)(2,1)S(1)}, u32[]{:S(2)}, u32[]{:S(2)}) collective-permute-start(bf16[32,5120]{1,0:T(8,128)(2,1)} %g0.1), channel_id=1, source_target_pairs={{0,2},{2,0},{1,3},{3,1},{4,6},{6,4},{5,7},{7,5},{8,10},{10,8},{9,1... | collective-permute-start | bytes 983048 | tf_op jit(solution)/shard_map/ppermute | solution.py:612
  2.8 1.7 %pack.1 = (bf16[8,272,128]{2,1,0:T(8,128)(2,1)}, s32[8,128]{1,0:T(8,128)}) custom-call(bf16[1,128,128]{2,1,0:T(8,128)(2,1)} %k_ref.1, bf16[1,128,128]{2,1,0:T(8,128)(2,1)} %v_ref.1, f32[1,128]{1,0:T(1,128)} %logit_ref.3, s32[2,64]{1,0:T(2,128)} %bitcast.1), custom_call_target="tpu_custom_call" | custom-call | tf_op jit(solution)/shard_map/pack/pallas_call | solution.py:466
  4.6 8.6 %all-to-all-start = ((bf16[8,272,128]{2,1,0:T(8,128)(2,1)}), bf16[8,272,128]{2,1,0:T(8,128)(2,1)S(1)}, u32[]{:S(2)}, u32[]{:S(2)}) async-start(bf16[8,272,128]{2,1,0:T(8,128)(2,1)} %get-tuple-element.41), calls=%async_computation | async-start | bytes 1114112 | tf_op jit(solution)/shard_map/all_to_all | solution.py:625
  13.7 3.2 %collective-permute-start.1 = (bf16[8,128,128]{2,1,0:T(8,128)(2,1)}, bf16[8,128,128]{2,1,0:T(8,128)(2,1)S(1)}, u32[]{:S(2)}, u32[]{:S(2)}) collective-permute-start(bf16[8,128,128]{2,1,0:T(8,128)(2,1)} %refs_0_.1), channel_id=1, source_target_pairs={{128,0},{192,64},{0,128},{64,192},{129,1},{193,65},{1,129},{65,193... | collective-permute-start | bytes 786440 | tf_op jit(solution)/shard_map/ppermute | solution.py:604
  16.9 1.1 collective-permute-start
  18.9 4.0 %copy-done.1 = bf16[1024,5120]{1,0:T(8,128)(2,1)S(1)} copy-done((bf16[1024,5120]{1,0:T(8,128)(2,1)S(1)}, bf16[1024,5120]{1,0:T(8,128)(2,1)}, u32[]{:S(2)}) %copy-start.1) | copy-done | bytes 10485784
  23.9 3.6 %cotangent.1.c0 = bf16[8,128,128]{2,1,0:T(8,128)(2,1)S(1)} custom-call(bf16[32,5120]{1,0:T(8,128)(2,1)S(1)} %copy-done.2, bf16[32,5120]{1,0:T(8,128)(2,1)S(1)} %collective-permute-done.4.g1, bf16[32,5120]{1,0:T(8,128)(2,1)S(1)} %collective-permute-done.5.g2, bf16[32,5120]{1,0:T(8,128)(2,1)S(1)} %collective-permute-done.6.g3, bf16[1024,5120]{1,0:T(8,128)(2,1)S(1)} %copy-done.1), custom_call_target="tpu_custom_call" | custom-call | flops 5000000000 | bytes 1048576 | tf_op jit(solution)/shard_map/cotangent/pallas_call | solution.py:476
  28.3 3.0 %collective-permute-start.8 = (bf16[8,128,128]{2,1,0:T(8,128)(2,1)S(1)}, bf16[8,128,128]{2,1,0:T(8,128)(2,1)S(1)}, u32[]{:S(2)}, u32[]{:S(2)}) collective-permute-start(bf16[8,128,128]{2,1,0:T(8,128)(2,1)S(1)} %cotangent.1.c0), channel_id=1, source_target_pairs={{128,0},{192,64},{0,128},{64,192},{129,1},{193,65},{1,129},{65,193... | collective-permute-start | bytes 786440 | tf_op jit(solution)/shard_map/ppermute | solution.py:604
  31.3 1.5 %collective-permute-start.3 = (bf16[8,272,128]{2,1,0:T(8,128)(2,1)S(1)}, bf16[8,272,128]{2,1,0:T(8,128)(2,1)S(1)}, u32[]{:S(2)}, u32[]{:S(2)}) collective-permute-start(bf16[8,272,128]{2,1,0:T(8,128)(2,1)S(1)} %all-to-all-done.refs_4_.kv0), channel_id=1, source_target_pairs={{0,4},{4,0},{1,5},{5,1},{2,6},{6,2},{3,7},{7,3},{8,12},{12,8},{9,1... | collective-permute-start | bytes 1671176 | tf_op jit(solution)/shard_map/ppermute | solution.py:612
  32.9 7.5 %forward0.1 = (f32[8,128,512]{2,1,0:T(8,128)S(1)}, f32[8,2,512]{2,1,0:T(2,128)S(1)}, f32[20,1,512]{2,1,0:T(1,128)S(1)}, bf16[20,256,512]{2,1,0:T(8,128)(2,1)S(1)...) custom-call(s32[8,128]{1,0:T(8,128)S(1)} %copy-done.4, bf16[8,128,128]{2,1,0:T(8,128)(2,1)S(1)} %copy-done.3, ...), custom_call_target="tpu_custom_call" | custom-call | flops 10000000000 | bytes 1048576 | tf_op jit(solution)/shard_map/forward0/pallas_call | solution.py:497
  40.4 2.3 %lists.1 = (s32[256]{0:T(256)S(1)}, s32[256]{0:T(256)S(1)}) custom-call(s32[8,128]{1,0:T(8,128)S(1)} %copy-done.4), custom_call_target="tpu_custom_call" | custom-call | flops 2000000000 | bytes 1048576 | tf_op jit(solution)/shard_map/lists/pallas_call | solution.py:566
  42.7 2.5 %collective-permute-done.3.refs_1_.kv1 = bf16[8,272,128]{2,1,0:T(8,128)(2,1)S(1)} collective-permute-done((bf16[8,272,128]{2,1,0:T(8,128)(2,1)S(1)}, bf16[8,272,128]{2,1,0:T(8,128)(2,1)S(1)}, u32[]{:S(2)}, u32[]{:S(2)}) %collective-permute-start.3) | collective-permute-done | bytes 557088 | tf_op jit(solution)/shard_map/ppermute | solution.py:612
  45.2 7.4 %forward1.1 = (f32[8,128,512]{2,1,0:T(8,128)S(1)}, f32[8,2,512]{2,1,0:T(2,128)S(1)}, f32[20,1,512]{2,1,0:T(1,128)S(1)}, bf16[20,256,512]{2,1,0:T(8,128)(2,1)S(1)}) custom-call(s32[8,128]{1,0:T(8,128)S(1)} %copy-done.4, bf16[8,128,512]{2,1,0:T(8,128)(2,1)S(1)} %get-tuple-element.48.refs_0_, bf16[8,272,128]{2,1,0:T(8,128)(2,1)S(1)} %collective-permute-done.3.refs_1_.kv1, ...), custom_call_target="tpu_custom_call" | custom-call | flops 10000000000 | bytes 1048576 | tf_op jit(solution)/shard_map/forward1/pallas_call | solution.py:497
  53.3 1.7 %collective-permute-start.12 = (f32[16,512]{1,0:T(8,128)S(1)}, f32[16,512]{1,0:T(8,128)S(1)}, u32[]{:S(2)}, u32[]{:S(2)}) collective-permute-start(f32[16,512]{1,0:T(8,128)S(1)} %get-tuple-element.60.refs_7_), channel_id=1, source_target_pairs={{192,0},{0,64},{64,128},{128,192},{193,1},{1,65},{65,129},{129,193... | collective-permute-start | bytes 98312 | tf_op jit(solution)/shard_map/ppermute | solution.py:604
  55.0 2.9 %collective-permute-start.11 = (f32[16,512]{1,0:T(8,128)S(1)}, f32[16,512]{1,0:T(8,128)S(1)}, u32[]{:S(2)}, u32[]{:S(2)}) collective-permute-start(f32[16,512]{1,0:T(8,128)S(1)} %get-tuple-element.60.refs_7_), channel_id=1, source_target_pairs={{128,0},{192,64},{0,128},{64,192},{129,1},{193,65},{1,129},{65,193... | collective-permute-start | bytes 98312 | tf_op jit(solution)/shard_map/ppermute | solution.py:604
  57.8 1.4 %collective-permute-start.10 = (f32[16,512]{1,0:T(8,128)S(1)}, f32[16,512]{1,0:T(8,128)S(1)}, u32[]{:S(2)}, u32[]{:S(2)}) collective-permute-start(f32[16,512]{1,0:T(8,128)S(1)} %get-tuple-element.60.refs_7_), channel_id=1, source_target_pairs={{64,0},{128,64},{192,128},{0,192},{65,1},{129,65},{193,129},{1,193... | collective-permute-start | bytes 98312 | tf_op jit(solution)/shard_map/ppermute | solution.py:604
  60.4 1.4 %collective-permute-done.10.refs_8_ = f32[16,512]{1,0:T(8,128)S(1)} collective-permute-done((f32[16,512]{1,0:T(8,128)S(1)}, f32[16,512]{1,0:T(8,128)S(1)}, u32[]{:S(2)}, u32[]{:S(2)}) %collective-permute-start.10) | collective-permute-done | bytes 32800 | tf_op jit(solution)/shard_map/ppermute | solution.py:604
  61.8 9.2 %backward1.1 = (f32[4,128,512]{2,1,0:T(8,128)S(1)}, f32[4,128,512]{2,1,0:T(8,128)S(1)}, bf16[8,272,128]{2,1,0:T(8,128)(2,1)S(1)}) custom-call(s32[8,128]{1,0:T(8,128)S(1)} %copy-done.4, s32[256]{0:T(256)S(1)} %get-tuple-element.49.refs_2_.steps, bf16[8,512,128]{2,1,0:T(8,128)(2,1)S(1)} %get-tuple-element.45.refs_0_, ...), custom_call_target="tpu_custom_call" | custom-call | flops 15000000512 | bytes 1048576 | tf_op jit(solution)/shard_map/backward1/pallas_call | solution.py:549
  70.9 1.5 %collective-permute-start.16 = (bf16[8,272,128]{2,1,0:T(8,128)(2,1)S(1)}, bf16[8,272,128]{2,1,0:T(8,128)(2,1)S(1)}, u32[]{:S(2)}, u32[]{:S(2)}) collective-permute-start(bf16[8,272,128]{2,1,0:T(8,128)(2,1)S(1)} %get-tuple-element.72), channel_id=1, source_target_pairs={{0,4},{4,0},{1,5},{5,1},{2,6},{6,2},{3,7},{7,3},{8,12},{12,8},{9,1... | collective-permute-start | bytes 1671176 | tf_op jit(solution)/shard_map/ppermute | solution.py:612
  72.5 10.0 %backward0.1 = (bf16[8,128,128]{2,1,0:T(8,128)(2,1)S(1)}, bf16[8,128,128]{2,1,0:T(8,128)(2,1)S(1)}, bf16[8,128,128]{2,1,0:T(8,128)(2,1)S(1)}, bf16[8,128,128]{2,1,0:T(8,128)(2,1)S(1)}, f32[8,272,128]{2,1,0:T(8,128)S(1)}) custom-call(s32[8,128]{1,0:T(8,128)S(1)} %copy-done.4, s32[256]{0:T(256)S(1)} %get-tuple-element.44.steps, ...), custom_call_target="tpu_custom_call" | custom-call | flops 15000000512 | bytes 1048576 | tf_op jit(solution)/shard_map/backward0/pallas_call | solution.py:549
  83.4 6.3 %all-to-all-start.1 = ((bf16[8,272,128]{2,1,0:T(8,128)(2,1)}), bf16[8,272,128]{2,1,0:T(8,128)(2,1)S(1)}, u32[]{:S(2)}, u32[]{:S(2)}) async-start(bf16[8,272,128]{2,1,0:T(8,128)(2,1)} %add_convert_fusion), calls=%async_computation.1 | async-start | bytes 1114112 | tf_op jit(solution)/shard_map/all_to_all | solution.py:645
  89.7 3.3 %collective-permute-start.14 = (bf16[8,128,128]{2,1,0:T(8,128)(2,1)S(1)}, bf16[8,128,128]{2,1,0:T(8,128)(2,1)S(1)}, u32[]{:S(2)}, u32[]{:S(2)}) collective-permute-start(bf16[8,128,128]{2,1,0:T(8,128)(2,1)S(1)} %get-tuple-element.69), channel_id=1, source_target_pairs={{128,0},{192,64},{0,128},{64,192},{129,1},{193,65},{1,129},{65,193... | collective-permute-start | bytes 786440 | tf_op jit(solution)/shard_map/ppermute | solution.py:604
  94.0 7.5 %collective-permute-done.13 = bf16[8,128,128]{2,1,0:T(8,128)(2,1)S(1)} collective-permute-done((bf16[8,128,128]{2,1,0:T(8,128)(2,1)S(1)}, bf16[8,128,128]{2,1,0:T(8,128)(2,1)S(1)}, u32[]{:S(2)}, u32[]{:S(2)}) %collective-permute-start.13) | collective-permute-done | bytes 262176 | tf_op jit(solution)/shard_map/ppermute | solution.py:604
  103.0 2.1 %all-to-all-done.1.parts_ref = bf16[8,272,128]{2,1,0:T(8,128)(2,1)S(1)} async-done(((bf16[8,272,128]{2,1,0:T(8,128)(2,1)}), bf16[8,272,128]{2,1,0:T(8,128)(2,1)S(1)}, u32[]{:S(2)}, u32[]{:S(2)}) %all-to-all-start.1) | async-done | bytes 557088 | tf_op jit(solution)/shard_map/all_to_all | solution.py:645
  (36 shorter events, 9.2 us)
Async XLA Ops:
  0.6 12.6 %collective-permute-start.4 = (bf16[32,5120]{1,0:T(8,128)(2,1)}, bf16[32,5120]{1,0:T(8,128)(2,1)S(1)}, u32[]{:S(2)}, u32[]{:S(2)}) collective-permute-start(bf16[32,5120]{1,0:T(8,128)(2,1)} %g0.1), channel_id=1, source_target_pairs={{0,2},{2,0},{1,3},{3,1},{4,6},{6,4},{5,7},{7,5},{8,10},{10,8},{9,1... | collective-permute-start | bytes 983048 | tf_op jit(solution)/shard_map/ppermute | solution.py:612
  4.6 28.3 %copy-start.3 = (bf16[8,128,128]{2,1,0:T(8,128)(2,1)S(1)}, bf16[8,128,128]{2,1,0:T(8,128)(2,1)}, u32[]{:S(2)}) copy-start(bf16[8,128,128]{2,1,0:T(8,128)(2,1)} %refs_0_.1) | copy-start | bytes 786436
  4.6 28.3 %copy-start.4 = (s32[8,128]{1,0:T(8,128)S(1)}, s32[8,128]{1,0:T(8,128)}, u32[]{:S(2)}) copy-start(s32[8,128]{1,0:T(8,128)} %get-tuple-element.43.plan_ref) | copy-start | bytes 12292
  4.6 26.7 %all-to-all-start = ((bf16[8,272,128]{2,1,0:T(8,128)(2,1)}), bf16[8,272,128]{2,1,0:T(8,128)(2,1)S(1)}, u32[]{:S(2)}, u32[]{:S(2)}) async-start(bf16[8,272,128]{2,1,0:T(8,128)(2,1)} %get-tuple-element.41), calls=%async_computation | async-start | bytes 1114112 | tf_op jit(solution)/shard_map/all_to_all | solution.py:625
  13.2 5.7 %collective-permute-start.5 = (bf16[32,5120]{1,0:T(8,128)(2,1)}, bf16[32,5120]{1,0:T(8,128)(2,1)S(1)}, u32[]{:S(2)}, u32[]{:S(2)}) collective-permute-start(bf16[32,5120]{1,0:T(8,128)(2,1)} %g0.1), channel_id=1, source_target_pairs={{0,1},{1,0},{2,3},{3,2},{4,5},{5,4},{6,7},{7,6},{8,9},{9,8},{10,11... | collective-permute-start | bytes 983048 | tf_op jit(solution)/shard_map/ppermute | solution.py:612
  13.2 5.7 %collective-permute-start.6 = (bf16[32,5120]{1,0:T(8,128)(2,1)S(1)}, bf16[32,5120]{1,0:T(8,128)(2,1)S(1)}, u32[]{:S(2)}, u32[]{:S(2)}) collective-permute-start(bf16[32,5120]{1,0:T(8,128)(2,1)S(1)} %collective-permute-done.4.g1), channel_id=1, source_target_pairs={{0,1},{1,0},{2,3},{3,2},{4,5},{5,4},{6,7},{7,6},{8,9},{9,8},{10,11... | collective-permute-start | bytes 983048 | tf_op jit(solution)/shard_map/ppermute | solution.py:612
  13.7 17.6 %collective-permute-start.1 = (bf16[8,128,128]{2,1,0:T(8,128)(2,1)}, bf16[8,128,128]{2,1,0:T(8,128)(2,1)S(1)}, u32[]{:S(2)}, u32[]{:S(2)}) collective-permute-start(bf16[8,128,128]{2,1,0:T(8,128)(2,1)} %refs_0_.1), channel_id=1, source_target_pairs={{128,0},{192,64},{0,128},{64,192},{129,1},{193,65},{1,129},{65,193... | collective-permute-start | bytes 786440 | tf_op jit(solution)/shard_map/ppermute | solution.py:604
  16.9 14.4 %collective-permute-start = (bf16[8,128,128]{2,1,0:T(8,128)(2,1)}, bf16[8,128,128]{2,1,0:T(8,128)(2,1)S(1)}, u32[]{:S(2)}, u32[]{:S(2)}) collective-permute-start(bf16[8,128,128]{2,1,0:T(8,128)(2,1)} %refs_0_.1), channel_id=1, source_target_pairs={{64,0},{128,64},{192,128},{0,192},{65,1},{129,65},{193,129},{1,193... | collective-permute-start | bytes 786440 | tf_op jit(solution)/shard_map/ppermute | solution.py:604
  18.0 14.9 %collective-permute-start.2 = (bf16[8,128,128]{2,1,0:T(8,128)(2,1)}, bf16[8,128,128]{2,1,0:T(8,128)(2,1)S(1)}, u32[]{:S(2)}, u32[]{:S(2)}) collective-permute-start(bf16[8,128,128]{2,1,0:T(8,128)(2,1)} %refs_0_.1), channel_id=1, source_target_pairs={{192,0},{0,64},{64,128},{128,192},{193,1},{1,65},{65,129},{129,193... | collective-permute-start | bytes 786440 | tf_op jit(solution)/shard_map/ppermute | solution.py:604
  18.9 4.0 %copy-start.1 = (bf16[1024,5120]{1,0:T(8,128)(2,1)S(1)}, bf16[1024,5120]{1,0:T(8,128)(2,1)}, u32[]{:S(2)}) copy-start(bf16[1024,5120]{1,0:T(8,128)(2,1)} %w_ref.1) | copy-start | bytes 31457284
  22.9 1.0 copy-start.2
  27.5 25.1 %collective-permute-start.9 = (bf16[8,128,128]{2,1,0:T(8,128)(2,1)S(1)}, bf16[8,128,128]{2,1,0:T(8,128)(2,1)S(1)}, u32[]{:S(2)}, u32[]{:S(2)}) collective-permute-start(bf16[8,128,128]{2,1,0:T(8,128)(2,1)S(1)} %cotangent.1.c0), channel_id=1, source_target_pairs={{192,0},{0,64},{64,128},{128,192},{193,1},{1,65},{65,129},{129,193... | collective-permute-start | bytes 786440 | tf_op jit(solution)/shard_map/ppermute | solution.py:604
  28.3 24.3 %collective-permute-start.8 = (bf16[8,128,128]{2,1,0:T(8,128)(2,1)S(1)}, bf16[8,128,128]{2,1,0:T(8,128)(2,1)S(1)}, u32[]{:S(2)}, u32[]{:S(2)}) collective-permute-start(bf16[8,128,128]{2,1,0:T(8,128)(2,1)S(1)} %cotangent.1.c0), channel_id=1, source_target_pairs={{128,0},{192,64},{0,128},{64,192},{129,1},{193,65},{1,129},{65,193... | collective-permute-start | bytes 786440 | tf_op jit(solution)/shard_map/ppermute | solution.py:604
  31.3 21.3 %collective-permute-start.7 = (bf16[8,128,128]{2,1,0:T(8,128)(2,1)S(1)}, bf16[8,128,128]{2,1,0:T(8,128)(2,1)S(1)}, u32[]{:S(2)}, u32[]{:S(2)}) collective-permute-start(bf16[8,128,128]{2,1,0:T(8,128)(2,1)S(1)} %cotangent.1.c0), channel_id=1, source_target_pairs={{64,0},{128,64},{192,128},{0,192},{65,1},{129,65},{193,129},{1,193... | collective-permute-start | bytes 786440 | tf_op jit(solution)/shard_map/ppermute | solution.py:604
  31.3 13.9 %collective-permute-start.3 = (bf16[8,272,128]{2,1,0:T(8,128)(2,1)S(1)}, bf16[8,272,128]{2,1,0:T(8,128)(2,1)S(1)}, u32[]{:S(2)}, u32[]{:S(2)}) collective-permute-start(bf16[8,272,128]{2,1,0:T(8,128)(2,1)S(1)} %all-to-all-done.refs_4_.kv0), channel_id=1, source_target_pairs={{0,4},{4,0},{1,5},{5,1},{2,6},{6,2},{3,7},{7,3},{8,12},{12,8},{9,1... | collective-permute-start | bytes 1671176 | tf_op jit(solution)/shard_map/ppermute | solution.py:612
  53.3 6.8 %collective-permute-start.12 = (f32[16,512]{1,0:T(8,128)S(1)}, f32[16,512]{1,0:T(8,128)S(1)}, u32[]{:S(2)}, u32[]{:S(2)}) collective-permute-start(f32[16,512]{1,0:T(8,128)S(1)} %get-tuple-element.60.refs_7_), channel_id=1, source_target_pairs={{192,0},{0,64},{64,128},{128,192},{193,1},{1,65},{65,129},{129,193... | collective-permute-start | bytes 98312 | tf_op jit(solution)/shard_map/ppermute | solution.py:604
  55.0 5.4 %collective-permute-start.11 = (f32[16,512]{1,0:T(8,128)S(1)}, f32[16,512]{1,0:T(8,128)S(1)}, u32[]{:S(2)}, u32[]{:S(2)}) collective-permute-start(f32[16,512]{1,0:T(8,128)S(1)} %get-tuple-element.60.refs_7_), channel_id=1, source_target_pairs={{128,0},{192,64},{0,128},{64,192},{129,1},{193,65},{1,129},{65,193... | collective-permute-start | bytes 98312 | tf_op jit(solution)/shard_map/ppermute | solution.py:604
  57.8 3.9 %collective-permute-start.10 = (f32[16,512]{1,0:T(8,128)S(1)}, f32[16,512]{1,0:T(8,128)S(1)}, u32[]{:S(2)}, u32[]{:S(2)}) collective-permute-start(f32[16,512]{1,0:T(8,128)S(1)} %get-tuple-element.60.refs_7_), channel_id=1, source_target_pairs={{64,0},{128,64},{192,128},{0,192},{65,1},{129,65},{193,129},{1,193... | collective-permute-start | bytes 98312 | tf_op jit(solution)/shard_map/ppermute | solution.py:604
  70.9 11.6 %collective-permute-start.16 = (bf16[8,272,128]{2,1,0:T(8,128)(2,1)S(1)}, bf16[8,272,128]{2,1,0:T(8,128)(2,1)S(1)}, u32[]{:S(2)}, u32[]{:S(2)}) collective-permute-start(bf16[8,272,128]{2,1,0:T(8,128)(2,1)S(1)} %get-tuple-element.72), channel_id=1, source_target_pairs={{0,4},{4,0},{1,5},{5,1},{2,6},{6,2},{3,7},{7,3},{8,12},{12,8},{9,1... | collective-permute-start | bytes 1671176 | tf_op jit(solution)/shard_map/ppermute | solution.py:612
  82.5 22.5 %copy-start = (f32[1,128]{1,0:T(1,128)S(1)}, f32[1,128]{1,0:T(1,128)}, u32[]{:S(2)}) copy-start(f32[1,128]{1,0:T(1,128)} %logit_ref.3) | copy-start | bytes 1540
  83.4 21.6 %all-to-all-start.1 = ((bf16[8,272,128]{2,1,0:T(8,128)(2,1)}), bf16[8,272,128]{2,1,0:T(8,128)(2,1)S(1)}, u32[]{:S(2)}, u32[]{:S(2)}) async-start(bf16[8,272,128]{2,1,0:T(8,128)(2,1)} %add_convert_fusion), calls=%async_computation.1 | async-start | bytes 1114112 | tf_op jit(solution)/shard_map/all_to_all | solution.py:645
  89.7 11.7 %collective-permute-start.13 = (bf16[8,128,128]{2,1,0:T(8,128)(2,1)S(1)}, bf16[8,128,128]{2,1,0:T(8,128)(2,1)S(1)}, u32[]{:S(2)}, u32[]{:S(2)}) collective-permute-start(bf16[8,128,128]{2,1,0:T(8,128)(2,1)S(1)} %get-tuple-element.68), channel_id=1, source_target_pairs={{192,0},{0,64},{64,128},{128,192},{193,1},{1,65},{65,129},{129,193... | collective-permute-start | bytes 786440 | tf_op jit(solution)/shard_map/ppermute | solution.py:604
  89.7 11.7 %collective-permute-start.14 = (bf16[8,128,128]{2,1,0:T(8,128)(2,1)S(1)}, bf16[8,128,128]{2,1,0:T(8,128)(2,1)S(1)}, u32[]{:S(2)}, u32[]{:S(2)}) collective-permute-start(bf16[8,128,128]{2,1,0:T(8,128)(2,1)S(1)} %get-tuple-element.69), channel_id=1, source_target_pairs={{128,0},{192,64},{0,128},{64,192},{129,1},{193,65},{1,129},{65,193... | collective-permute-start | bytes 786440 | tf_op jit(solution)/shard_map/ppermute | solution.py:604
  93.0 9.1 %collective-permute-start.15 = (bf16[8,128,128]{2,1,0:T(8,128)(2,1)S(1)}, bf16[8,128,128]{2,1,0:T(8,128)(2,1)S(1)}, u32[]{:S(2)}, u32[]{:S(2)}) collective-permute-start(bf16[8,128,128]{2,1,0:T(8,128)(2,1)S(1)} %get-tuple-element.70), channel_id=1, source_target_pairs={{64,0},{128,64},{192,128},{0,192},{65,1},{129,65},{193,129},{1,193... | collective-permute-start | bytes 786440 | tf_op jit(solution)/shard_map/ppermute | solution.py:604

commit v7 on v5

--- a/solution.py
+++ b/solution.py
@@ -646,7 +646,7 @@
     dkv = lax.all_to_all(dkv, "z", 0, 0, tiled=True)
     key_grad, value_grad, logit_grad = run_total(dkv, evict_logits)
     query_grad = dq[0].astype(f32)
-    for r in range(1, NA):
+    for r in (2, 1, 3):
         query_grad = query_grad + from_y(dq[r], NA - r).astype(f32)
     return query_grad.astype(bf16), key_grad, value_grad, logit_grad
 

time: 107 us -> 107 us (level)
  no operation moved by 1% of the time
where the time goes in v7:
time: 107 us; the launch traced here: 106 us
  Pallas kernels  41.3 us (39%)
  starting transfers between devices  40.5 us (38%)
  waiting for transfers between devices  16.8 us (16%)
  local copies, waits for them, and re-layouts  5.24 us (5%)
  other arithmetic  1.77 us (2%)
    ppermute x12, starting transfers between devices, from_y(): return lax.ppermute(x, 'y', [((i + r) % NA, i) for i in range(NA)])  19.3 us
    pallas_call x2, Pallas kernels, run_backward(): pl.pallas_call(functools.partial(backward_kernel, col), out_shape=out_sha...  18.3 us
    pallas_call x2, Pallas kernels, run_forward(): pl.pallas_call(functools.partial(forward_kernel, col), out_shape=out_shap...  14.6 us
    ppermute x12, waiting for transfers between devices, from_y(): return lax.ppermute(x, 'y', [((i + r) % NA, i) for i in range(NA)])  10.4 us
    all_to_all x1, starting transfers between devices, per_device(): lax.all_to_all(run_pack(keys, values, evict_logits), 'z', 0, 0, tiled=True)  8.47 us
    all_to_all x1, starting transfers between devices, per_device(): dkv = lax.all_to_all(dkv, 'z', 0, 0, tiled=True)  6.93 us
    ppermute x5, starting transfers between devices, swap(): return lax.ppermute(x, axis, [(0, 1), (1, 0)])  5.82 us
    unnamed x14, local copies, waits for them, and re-layouts  5.24 us
  transfers between devices with their start and end apart: 19, of which 8 were waited for; matrix products, arithmetic and copies ran while one was open for 1% of the time, Pallas kernels for 29%

profile of v7, /device:TPU:2, one launch (start us, length us, event | category | flops | bytes accessed | tf_op | source)
XLA Modules:
  0.0 106.4 jit_solution(9282763981433886681)
XLA Ops:
  0.6 2.2 %collective-permute-start.4 = (bf16[32,5120]{1,0:T(8,128)(2,1)}, bf16[32,5120]{1,0:T(8,128)(2,1)S(1)}, u32[]{:S(2)}, u32[]{:S(2)}) collective-permute-start(bf16[32,5120]{1,0:T(8,128)(2,1)} %g0.1), channel_id=1, source_target_pairs={{0,2},{2,0},{1,3},{3,1},{4,6},{6,4},{5,7},{7,5},{8,10},{10,8},{9,1... | collective-permute-start | bytes 983048 | tf_op jit(solution)/shard_map/ppermute | solution.py:614
  5.2 8.5 %all-to-all-start = ((bf16[8,272,128]{2,1,0:T(8,128)(2,1)}), bf16[8,272,128]{2,1,0:T(8,128)(2,1)S(1)}, u32[]{:S(2)}, u32[]{:S(2)}) async-start(bf16[8,272,128]{2,1,0:T(8,128)(2,1)} %pack.1), calls=%async_computation | async-start | bytes 1114112 | tf_op jit(solution)/shard_map/all_to_all | solution.py:628
  14.3 3.2 %collective-permute-start.1 = (bf16[8,128,128]{2,1,0:T(8,128)(2,1)S(1)}, bf16[8,128,128]{2,1,0:T(8,128)(2,1)S(1)}, u32[]{:S(2)}, u32[]{:S(2)}) collective-permute-start(bf16[8,128,128]{2,1,0:T(8,128)(2,1)S(1)} %copy-done.5), channel_id=1, source_target_pairs={{128,0},{192,64},{0,128},{64,192},{129,1},{193,65},{1,129},{65,193... | collective-permute-start | bytes 786440 | tf_op jit(solution)/shard_map/ppermute | solution.py:606
  17.5 1.1 collective-permute-start
  19.5 4.0 %copy-done.3 = bf16[1024,5120]{1,0:T(8,128)(2,1)S(1)} copy-done((bf16[1024,5120]{1,0:T(8,128)(2,1)S(1)}, bf16[1024,5120]{1,0:T(8,128)(2,1)}, u32[]{:S(2)}) %copy-start.3) | copy-done | bytes 10485784
  23.5 3.6 %cotangent.1.c0 = bf16[8,128,128]{2,1,0:T(8,128)(2,1)S(1)} custom-call(bf16[32,5120]{1,0:T(8,128)(2,1)S(1)} %copy-done.4, bf16[32,5120]{1,0:T(8,128)(2,1)S(1)} %collective-permute-done.4.g1, bf16[32,5120]{1,0:T(8,128)(2,1)S(1)} %collective-permute-done.5.g2, bf16[32,5120]{1,0:T(8,128)(2,1)S(1)} %collective-permute-done.6.g3, bf16[1024,5120]{1,0:T(8,128)(2,1)S(1)} %copy-done.3), custom_call_target="tpu_custom_call" | custom-call | flops 5000000000 | bytes 1048576 | tf_op jit(solution)/shard_map/cotangent/pallas_call | solution.py:488
  27.8 3.0 %collective-permute-start.8 = (bf16[8,128,128]{2,1,0:T(8,128)(2,1)S(1)}, bf16[8,128,128]{2,1,0:T(8,128)(2,1)S(1)}, u32[]{:S(2)}, u32[]{:S(2)}) collective-permute-start(bf16[8,128,128]{2,1,0:T(8,128)(2,1)S(1)} %cotangent.1.c0), channel_id=1, source_target_pairs={{128,0},{192,64},{0,128},{64,192},{129,1},{193,65},{1,129},{65,193... | collective-permute-start | bytes 786440 | tf_op jit(solution)/shard_map/ppermute | solution.py:606
  31.6 1.4 %collective-permute-start.3 = (bf16[8,272,128]{2,1,0:T(8,128)(2,1)S(1)}, bf16[8,272,128]{2,1,0:T(8,128)(2,1)S(1)}, u32[]{:S(2)}, u32[]{:S(2)}) collective-permute-start(bf16[8,272,128]{2,1,0:T(8,128)(2,1)S(1)} %all-to-all-done.refs_4_.refs_3_), channel_id=1, source_target_pairs={{0,4},{4,0},{1,5},{5,1},{2,6},{6,2},{3,7},{7,3},{8,12},{12,8},{9,1... | collective-permute-start | bytes 1671176 | tf_op jit(solution)/shard_map/ppermute | solution.py:614
  33.0 7.4 %forward0.1 = (f32[8,128,512]{2,1,0:T(8,128)S(1)}, f32[8,2,512]{2,1,0:T(2,128)S(1)}, f32[20,1,512]{2,1,0:T(1,128)S(1)}, bf16[20,256,512]{2,1,0:T(8,128)(2,1)S(1)...) custom-call(s32[8,128]{1,0:T(8,128)S(1)} %plan.1.plan_ref, bf16[8,128,128]{2,1,0:T(8,128)(2,1)S(1)} %copy-done.5, ...), custom_call_target="tpu_custom_call" | custom-call | flops 10000000000 | bytes 1048576 | tf_op jit(solution)/shard_map/forward0/pallas_call | solution.py:509
  40.5 2.3 %lists.1 = (s32[256]{0:T(256)S(1)}, s32[256]{0:T(256)S(1)}) custom-call(s32[8,128]{1,0:T(8,128)S(1)} %plan.1.plan_ref), custom_call_target="tpu_custom_call" | custom-call | flops 2000000000 | bytes 1048576 | tf_op jit(solution)/shard_map/lists/pallas_call | solution.py:583
  42.8 2.9 %collective-permute-done.3.refs_1_.refs_3_ = bf16[8,272,128]{2,1,0:T(8,128)(2,1)S(1)} collective-permute-done((bf16[8,272,128]{2,1,0:T(8,128)(2,1)S(1)}, bf16[8,272,128]{2,1,0:T(8,128)(2,1)S(1)}, u32[]{:S(2)}, u32[]{:S(2)}) %collective-permute-start.3) | collective-permute-done | bytes 557088 | tf_op jit(solution)/shard_map/ppermute | solution.py:614
  45.7 7.1 %forward1.1 = (f32[8,128,512]{2,1,0:T(8,128)S(1)}, f32[8,2,512]{2,1,0:T(2,128)S(1)}, f32[20,1,512]{2,1,0:T(1,128)S(1)}, bf16[20,256,512]{2,1,0:T(8,128)(2,1)S(1)}) custom-call(s32[8,128]{1,0:T(8,128)S(1)} %plan.1.plan_ref, bf16[8,128,512]{2,1,0:T(8,128)(2,1)S(1)} %get-tuple-element.42.refs_0_, ...), custom_call_target="tpu_custom_call" | custom-call | flops 10000000000 | bytes 1048576 | tf_op jit(solution)/shard_map/forward1/pallas_call | solution.py:509
  54.6 3.5 %collective-permute-start.11 = (f32[16,512]{1,0:T(8,128)S(1)}, f32[16,512]{1,0:T(8,128)S(1)}, u32[]{:S(2)}, u32[]{:S(2)}) collective-permute-start(f32[16,512]{1,0:T(8,128)S(1)} %get-tuple-element.50.refs_6_), channel_id=1, source_target_pairs={{128,0},{192,64},{0,128},{64,192},{129,1},{193,65},{1,129},{65,193... | collective-permute-start | bytes 98312 | tf_op jit(solution)/shard_map/ppermute | solution.py:606
  58.1 1.3 %collective-permute-start.10 = (f32[16,512]{1,0:T(8,128)S(1)}, f32[16,512]{1,0:T(8,128)S(1)}, u32[]{:S(2)}, u32[]{:S(2)}) collective-permute-start(f32[16,512]{1,0:T(8,128)S(1)} %get-tuple-element.50.refs_6_), channel_id=1, source_target_pairs={{64,0},{128,64},{192,128},{0,192},{65,1},{129,65},{193,129},{1,193... | collective-permute-start | bytes 98312 | tf_op jit(solution)/shard_map/ppermute | solution.py:606
  60.4 1.7 %collective-permute-done.10.refs_7_ = f32[16,512]{1,0:T(8,128)S(1)} collective-permute-done((f32[16,512]{1,0:T(8,128)S(1)}, f32[16,512]{1,0:T(8,128)S(1)}, u32[]{:S(2)}, u32[]{:S(2)}) %collective-permute-start.10) | collective-permute-done | bytes 32800 | tf_op jit(solution)/shard_map/ppermute | solution.py:606
  62.1 8.7 %backward1.1 = (f32[4,128,512]{2,1,0:T(8,128)S(1)}, f32[4,128,512]{2,1,0:T(8,128)S(1)}, bf16[8,272,128]{2,1,0:T(8,128)(2,1)S(1)}) custom-call(s32[8,128]{1,0:T(8,128)S(1)} %plan.1.plan_ref, s32[256]{0:T(256)S(1)} %get-tuple-element.43.refs_2_.steps, bf16[8,512,128]{2,1,0:T(8,128)(2,1)S(1)} %get-tuple-element.39.refs_0_, ...), custom_call_target="tpu_custom_call" | custom-call | flops 15000000512 | bytes 1048576 | tf_op jit(solution)/shard_map/backward1/pallas_call | solution.py:561
  70.8 1.6 %collective-permute-start.16 = (bf16[8,272,128]{2,1,0:T(8,128)(2,1)S(1)}, bf16[8,272,128]{2,1,0:T(8,128)(2,1)S(1)}, u32[]{:S(2)}, u32[]{:S(2)}) collective-permute-start(bf16[8,272,128]{2,1,0:T(8,128)(2,1)S(1)} %get-tuple-element.60), channel_id=1, source_target_pairs={{0,4},{4,0},{1,5},{5,1},{2,6},{6,2},{3,7},{7,3},{8,12},{12,8},{9,1... | collective-permute-start | bytes 1671176 | tf_op jit(solution)/shard_map/ppermute | solution.py:614
  72.4 9.6 %backward0.1 = (bf16[8,128,128]{2,1,0:T(8,128)(2,1)S(1)}, bf16[8,128,128]{2,1,0:T(8,128)(2,1)S(1)}, bf16[8,128,128]{2,1,0:T(8,128)(2,1)S(1)}, bf16[8,128,128]{2,1,0:T(8,128)(2,1)S(1)}, f32[8,272,128]{2,1,0:T(8,128)S(1)}) custom-call(s32[8,128]{1,0:T(8,128)S(1)} %plan.1.plan_ref, s32[256]{0:T(256)S(1)} %get-tuple-element.38.steps, ...), custom_call_target="tpu_custom_call" | custom-call | flops 15000000512 | bytes 1048576 | tf_op jit(solution)/shard_map/backward0/pallas_call | solution.py:561
  83.2 6.9 %all-to-all-start.1 = ((bf16[8,272,128]{2,1,0:T(8,128)(2,1)}), bf16[8,272,128]{2,1,0:T(8,128)(2,1)S(1)}, u32[]{:S(2)}, u32[]{:S(2)}) async-start(bf16[8,272,128]{2,1,0:T(8,128)(2,1)} %add_convert_fusion), calls=%async_computation.1 | async-start | bytes 1114112 | tf_op jit(solution)/shard_map/all_to_all | solution.py:646
  90.1 1.1 %collective-permute-start.13 = (bf16[8,128,128]{2,1,0:T(8,128)(2,1)S(1)}, bf16[8,128,128]{2,1,0:T(8,128)(2,1)S(1)}, u32[]{:S(2)}, u32[]{:S(2)}) collective-permute-start(bf16[8,128,128]{2,1,0:T(8,128)(2,1)S(1)} %get-tuple-element.56), channel_id=1, source_target_pairs={{128,0},{192,64},{0,128},{64,192},{129,1},{193,65},{1,129},{65,193... | collective-permute-start | bytes 786440 | tf_op jit(solution)/shard_map/ppermute | solution.py:606
  91.9 2.7 %collective-permute-start.15 = (bf16[8,128,128]{2,1,0:T(8,128)(2,1)S(1)}, bf16[8,128,128]{2,1,0:T(8,128)(2,1)S(1)}, u32[]{:S(2)}, u32[]{:S(2)}) collective-permute-start(bf16[8,128,128]{2,1,0:T(8,128)(2,1)S(1)} %get-tuple-element.58), channel_id=1, source_target_pairs={{64,0},{128,64},{192,128},{0,192},{65,1},{129,65},{193,129},{1,193... | collective-permute-start | bytes 786440 | tf_op jit(solution)/shard_map/ppermute | solution.py:606
  94.5 5.2 %collective-permute-done.13 = bf16[8,128,128]{2,1,0:T(8,128)(2,1)S(1)} collective-permute-done((bf16[8,128,128]{2,1,0:T(8,128)(2,1)S(1)}, bf16[8,128,128]{2,1,0:T(8,128)(2,1)S(1)}, u32[]{:S(2)}, u32[]{:S(2)}) %collective-permute-start.13) | collective-permute-done | bytes 262176 | tf_op jit(solution)/shard_map/ppermute | solution.py:606
  99.7 2.7 %collective-permute-done.14 = bf16[8,128,128]{2,1,0:T(8,128)(2,1)S(1)} collective-permute-done((bf16[8,128,128]{2,1,0:T(8,128)(2,1)S(1)}, bf16[8,128,128]{2,1,0:T(8,128)(2,1)S(1)}, u32[]{:S(2)}, u32[]{:S(2)}) %collective-permute-start.14) | collective-permute-done | bytes 262176 | tf_op jit(solution)/shard_map/ppermute | solution.py:606
  103.2 2.5 %all-to-all-done.1.parts_ref = bf16[8,272,128]{2,1,0:T(8,128)(2,1)S(1)} async-done(((bf16[8,272,128]{2,1,0:T(8,128)(2,1)}), bf16[8,272,128]{2,1,0:T(8,128)(2,1)S(1)}, u32[]{:S(2)}, u32[]{:S(2)}) %all-to-all-start.1) | async-done | bytes 557088 | tf_op jit(solution)/shard_map/all_to_all | solution.py:646
  (40 shorter events, 11.4 us)
Async XLA Ops:
  0.6 13.2 %collective-permute-start.4 = (bf16[32,5120]{1,0:T(8,128)(2,1)}, bf16[32,5120]{1,0:T(8,128)(2,1)S(1)}, u32[]{:S(2)}, u32[]{:S(2)}) collective-permute-start(bf16[32,5120]{1,0:T(8,128)(2,1)} %g0.1), channel_id=1, source_target_pairs={{0,2},{2,0},{1,3},{3,1},{4,6},{6,4},{5,7},{7,5},{8,10},{10,8},{9,1... | collective-permute-start | bytes 983048 | tf_op jit(solution)/shard_map/ppermute | solution.py:614
  3.5 0.8 copy-start.1
  3.5 0.8 copy-start.2
  3.5 10.1 %copy-start.4 = (bf16[32,5120]{1,0:T(8,128)(2,1)S(1)}, bf16[32,5120]{1,0:T(8,128)(2,1)}, u32[]{:S(2)}) copy-start(bf16[32,5120]{1,0:T(8,128)(2,1)} %g0.1) | copy-start | bytes 983044
  3.5 10.7 %copy-start.5 = (bf16[8,128,128]{2,1,0:T(8,128)(2,1)S(1)}, bf16[8,128,128]{2,1,0:T(8,128)(2,1)}, u32[]{:S(2)}) copy-start(bf16[8,128,128]{2,1,0:T(8,128)(2,1)} %refs_0_.1) | copy-start | bytes 786436
  5.2 26.4 %all-to-all-start = ((bf16[8,272,128]{2,1,0:T(8,128)(2,1)}), bf16[8,272,128]{2,1,0:T(8,128)(2,1)S(1)}, u32[]{:S(2)}, u32[]{:S(2)}) async-start(bf16[8,272,128]{2,1,0:T(8,128)(2,1)} %pack.1), calls=%async_computation | async-start | bytes 1114112 | tf_op jit(solution)/shard_map/all_to_all | solution.py:628
  13.7 5.8 %collective-permute-start.5 = (bf16[32,5120]{1,0:T(8,128)(2,1)S(1)}, bf16[32,5120]{1,0:T(8,128)(2,1)S(1)}, u32[]{:S(2)}, u32[]{:S(2)}) collective-permute-start(bf16[32,5120]{1,0:T(8,128)(2,1)S(1)} %copy-done.4), channel_id=1, source_target_pairs={{0,1},{1,0},{2,3},{3,2},{4,5},{5,4},{6,7},{7,6},{8,9},{9,8},{10,11... | collective-permute-start | bytes 983048 | tf_op jit(solution)/shard_map/ppermute | solution.py:614
  13.8 5.7 %collective-permute-start.6 = (bf16[32,5120]{1,0:T(8,128)(2,1)S(1)}, bf16[32,5120]{1,0:T(8,128)(2,1)S(1)}, u32[]{:S(2)}, u32[]{:S(2)}) collective-permute-start(bf16[32,5120]{1,0:T(8,128)(2,1)S(1)} %collective-permute-done.4.g1), channel_id=1, source_target_pairs={{0,1},{1,0},{2,3},{3,2},{4,5},{5,4},{6,7},{7,6},{8,9},{9,8},{10,11... | collective-permute-start | bytes 983048 | tf_op jit(solution)/shard_map/ppermute | solution.py:614
  14.3 16.6 %collective-permute-start.1 = (bf16[8,128,128]{2,1,0:T(8,128)(2,1)S(1)}, bf16[8,128,128]{2,1,0:T(8,128)(2,1)S(1)}, u32[]{:S(2)}, u32[]{:S(2)}) collective-permute-start(bf16[8,128,128]{2,1,0:T(8,128)(2,1)S(1)} %copy-done.5), channel_id=1, source_target_pairs={{128,0},{192,64},{0,128},{64,192},{129,1},{193,65},{1,129},{65,193... | collective-permute-start | bytes 786440 | tf_op jit(solution)/shard_map/ppermute | solution.py:606
  17.5 13.4 %collective-permute-start = (bf16[8,128,128]{2,1,0:T(8,128)(2,1)S(1)}, bf16[8,128,128]{2,1,0:T(8,128)(2,1)S(1)}, u32[]{:S(2)}, u32[]{:S(2)}) collective-permute-start(bf16[8,128,128]{2,1,0:T(8,128)(2,1)S(1)} %copy-done.5), channel_id=1, source_target_pairs={{64,0},{128,64},{192,128},{0,192},{65,1},{129,65},{193,129},{1,193... | collective-permute-start | bytes 786440 | tf_op jit(solution)/shard_map/ppermute | solution.py:606
  18.5 14.5 %collective-permute-start.2 = (bf16[8,128,128]{2,1,0:T(8,128)(2,1)S(1)}, bf16[8,128,128]{2,1,0:T(8,128)(2,1)S(1)}, u32[]{:S(2)}, u32[]{:S(2)}) collective-permute-start(bf16[8,128,128]{2,1,0:T(8,128)(2,1)S(1)} %copy-done.5), channel_id=1, source_target_pairs={{192,0},{0,64},{64,128},{128,192},{193,1},{1,65},{65,129},{129,193... | collective-permute-start | bytes 786440 | tf_op jit(solution)/shard_map/ppermute | solution.py:606
  19.5 4.0 %copy-start.3 = (bf16[1024,5120]{1,0:T(8,128)(2,1)S(1)}, bf16[1024,5120]{1,0:T(8,128)(2,1)}, u32[]{:S(2)}) copy-start(bf16[1024,5120]{1,0:T(8,128)(2,1)} %w_ref.1) | copy-start | bytes 31457284
  27.1 25.7 %collective-permute-start.9 = (bf16[8,128,128]{2,1,0:T(8,128)(2,1)S(1)}, bf16[8,128,128]{2,1,0:T(8,128)(2,1)S(1)}, u32[]{:S(2)}, u32[]{:S(2)}) collective-permute-start(bf16[8,128,128]{2,1,0:T(8,128)(2,1)S(1)} %cotangent.1.c0), channel_id=1, source_target_pairs={{192,0},{0,64},{64,128},{128,192},{193,1},{1,65},{65,129},{129,193... | collective-permute-start | bytes 786440 | tf_op jit(solution)/shard_map/ppermute | solution.py:606
  27.8 25.0 %collective-permute-start.8 = (bf16[8,128,128]{2,1,0:T(8,128)(2,1)S(1)}, bf16[8,128,128]{2,1,0:T(8,128)(2,1)S(1)}, u32[]{:S(2)}, u32[]{:S(2)}) collective-permute-start(bf16[8,128,128]{2,1,0:T(8,128)(2,1)S(1)} %cotangent.1.c0), channel_id=1, source_target_pairs={{128,0},{192,64},{0,128},{64,192},{129,1},{193,65},{1,129},{65,193... | collective-permute-start | bytes 786440 | tf_op jit(solution)/shard_map/ppermute | solution.py:606
  30.9 21.9 %collective-permute-start.7 = (bf16[8,128,128]{2,1,0:T(8,128)(2,1)S(1)}, bf16[8,128,128]{2,1,0:T(8,128)(2,1)S(1)}, u32[]{:S(2)}, u32[]{:S(2)}) collective-permute-start(bf16[8,128,128]{2,1,0:T(8,128)(2,1)S(1)} %cotangent.1.c0), channel_id=1, source_target_pairs={{64,0},{128,64},{192,128},{0,192},{65,1},{129,65},{193,129},{1,193... | collective-permute-start | bytes 786440 | tf_op jit(solution)/shard_map/ppermute | solution.py:606
  31.6 14.1 %collective-permute-start.3 = (bf16[8,272,128]{2,1,0:T(8,128)(2,1)S(1)}, bf16[8,272,128]{2,1,0:T(8,128)(2,1)S(1)}, u32[]{:S(2)}, u32[]{:S(2)}) collective-permute-start(bf16[8,272,128]{2,1,0:T(8,128)(2,1)S(1)} %all-to-all-done.refs_4_.refs_3_), channel_id=1, source_target_pairs={{0,4},{4,0},{1,5},{5,1},{2,6},{6,2},{3,7},{7,3},{8,12},{12,8},{9,1... | collective-permute-start | bytes 1671176 | tf_op jit(solution)/shard_map/ppermute | solution.py:614
  53.6 5.9 %collective-permute-start.12 = (f32[16,512]{1,0:T(8,128)S(1)}, f32[16,512]{1,0:T(8,128)S(1)}, u32[]{:S(2)}, u32[]{:S(2)}) collective-permute-start(f32[16,512]{1,0:T(8,128)S(1)} %get-tuple-element.50.refs_6_), channel_id=1, source_target_pairs={{192,0},{0,64},{64,128},{128,192},{193,1},{1,65},{65,129},{129,193... | collective-permute-start | bytes 98312 | tf_op jit(solution)/shard_map/ppermute | solution.py:606
  54.6 5.8 %collective-permute-start.11 = (f32[16,512]{1,0:T(8,128)S(1)}, f32[16,512]{1,0:T(8,128)S(1)}, u32[]{:S(2)}, u32[]{:S(2)}) collective-permute-start(f32[16,512]{1,0:T(8,128)S(1)} %get-tuple-element.50.refs_6_), channel_id=1, source_target_pairs={{128,0},{192,64},{0,128},{64,192},{129,1},{193,65},{1,129},{65,193... | collective-permute-start | bytes 98312 | tf_op jit(solution)/shard_map/ppermute | solution.py:606
  58.1 3.9 %collective-permute-start.10 = (f32[16,512]{1,0:T(8,128)S(1)}, f32[16,512]{1,0:T(8,128)S(1)}, u32[]{:S(2)}, u32[]{:S(2)}) collective-permute-start(f32[16,512]{1,0:T(8,128)S(1)} %get-tuple-element.50.refs_6_), channel_id=1, source_target_pairs={{64,0},{128,64},{192,128},{0,192},{65,1},{129,65},{193,129},{1,193... | collective-permute-start | bytes 98312 | tf_op jit(solution)/shard_map/ppermute | solution.py:606
  70.8 11.5 %collective-permute-start.16 = (bf16[8,272,128]{2,1,0:T(8,128)(2,1)S(1)}, bf16[8,272,128]{2,1,0:T(8,128)(2,1)S(1)}, u32[]{:S(2)}, u32[]{:S(2)}) collective-permute-start(bf16[8,272,128]{2,1,0:T(8,128)(2,1)S(1)} %get-tuple-element.60), channel_id=1, source_target_pairs={{0,4},{4,0},{1,5},{5,1},{2,6},{6,2},{3,7},{7,3},{8,12},{12,8},{9,1... | collective-permute-start | bytes 1671176 | tf_op jit(solution)/shard_map/ppermute | solution.py:614
  83.2 22.5 %all-to-all-start.1 = ((bf16[8,272,128]{2,1,0:T(8,128)(2,1)}), bf16[8,272,128]{2,1,0:T(8,128)(2,1)S(1)}, u32[]{:S(2)}, u32[]{:S(2)}) async-start(bf16[8,272,128]{2,1,0:T(8,128)(2,1)} %add_convert_fusion), calls=%async_computation.1 | async-start | bytes 1114112 | tf_op jit(solution)/shard_map/all_to_all | solution.py:646
  90.1 9.6 %collective-permute-start.13 = (bf16[8,128,128]{2,1,0:T(8,128)(2,1)S(1)}, bf16[8,128,128]{2,1,0:T(8,128)(2,1)S(1)}, u32[]{:S(2)}, u32[]{:S(2)}) collective-permute-start(bf16[8,128,128]{2,1,0:T(8,128)(2,1)S(1)} %get-tuple-element.56), channel_id=1, source_target_pairs={{128,0},{192,64},{0,128},{64,192},{129,1},{193,65},{1,129},{65,193... | collective-permute-start | bytes 786440 | tf_op jit(solution)/shard_map/ppermute | solution.py:606
  91.3 11.1 %collective-permute-start.14 = (bf16[8,128,128]{2,1,0:T(8,128)(2,1)S(1)}, bf16[8,128,128]{2,1,0:T(8,128)(2,1)S(1)}, u32[]{:S(2)}, u32[]{:S(2)}) collective-permute-start(bf16[8,128,128]{2,1,0:T(8,128)(2,1)S(1)} %get-tuple-element.57), channel_id=1, source_target_pairs={{192,0},{0,64},{64,128},{128,192},{193,1},{1,65},{65,129},{129,193... | collective-permute-start | bytes 786440 | tf_op jit(solution)/shard_map/ppermute | solution.py:606
  91.9 10.5 %collective-permute-start.15 = (bf16[8,128,128]{2,1,0:T(8,128)(2,1)S(1)}, bf16[8,128,128]{2,1,0:T(8,128)(2,1)S(1)}, u32[]{:S(2)}, u32[]{:S(2)}) collective-permute-start(bf16[8,128,128]{2,1,0:T(8,128)(2,1)S(1)} %get-tuple-element.58), channel_id=1, source_target_pairs={{64,0},{128,64},{192,128},{0,192},{65,1},{129,65},{193,129},{1,193... | collective-permute-start | bytes 786440 | tf_op jit(solution)/shard_map/ppermute | solution.py:606
  (2 other events, 1.4 us)
